TPU v7x, 128 devices: a whole 4x4x4 slice. The times are simulated.
128 devices in a mesh: dp: 16 (over z_hi, y, core), ctx: 8 (over z_lo, x).
Axes of the slice: x: 4, y: 4, z: 4 (z_hi: 2, z_lo: 2; z = z_hi * 2 + z_lo), core: 2. Of those that a mesh axis runs over, the one named last changes fastest.
Arguments:
- inputs: bfloat16 [16, 2048, 960], P('dp', 'ctx'), may hold values from -6 to 6
- cotangent: bfloat16 [16, 2048, 960], P('dp', 'ctx'), may hold values from -6 to 6
- span_order: int32 [16], replicated, may hold values from 0 to 15, each once
- w_qkv: float32 [960, 1600], P('ctx'), may hold values from -0.1875 to 0.1875
- qkv_first: float32 [960, 1600], P('ctx'), may hold values from -128 to 128
- qkv_second: float32 [960, 1600], P('ctx'), may hold values from 983.04 to 9830.4
- w_proj: float32 [960, 960], P('ctx'), may hold values from -0.5 to 0.5
- proj_first: float32 [960, 960], P('ctx'), may hold values from -48 to 48
- proj_second: float32 [960, 960], P('ctx'), may hold values from 157.2864 to 1572.864
- w_expand: float32 [960, 5120], P('ctx'), may hold values from -0.1875 to 0.1875
- expand_first: float32 [960, 5120], P('ctx'), may hold values from -48 to 48
- expand_second: float32 [960, 5120], P('ctx'), may hold values from 157.2864 to 1572.864
- w_down: float32 [2560, 960], P('ctx'), may hold values from -0.125 to 0.125
- down_first: float32 [2560, 960], P('ctx'), may hold values from -64 to 64
- down_second: float32 [2560, 960], P('ctx'), may hold values from 353.8944 to 3538.944
- gains: float32 [2, 960], P(None, 'ctx'), may hold values from 0.5 to 1.5
- gains_first: float32 [2, 960], P(None, 'ctx'), may hold values from -128 to 128
- gains_second: float32 [2, 960], P(None, 'ctx'), may hold values from 983.04 to 9830.4
Outputs:
- output: bfloat16 [16, 2048, 960], P('dp', 'ctx')
- input_grad: bfloat16 [16, 2048, 960], P('dp', 'ctx')
- new_qkv: float32 [960, 1600], P('ctx')
- qkv_mean: float32 [960, 1600], P('ctx')
- qkv_square: float32 [960, 1600], P('ctx')
- new_proj: float32 [960, 960], P('ctx')
- proj_mean: float32 [960, 960], P('ctx')
- proj_square: float32 [960, 960], P('ctx')
- new_expand: float32 [960, 5120], P('ctx')
- expand_mean: float32 [960, 5120], P('ctx')
- expand_square: float32 [960, 5120], P('ctx')
- new_down: float32 [2560, 960], P('ctx')
- down_mean: float32 [2560, 960], P('ctx')
- down_square: float32 [2560, 960], P('ctx')
- new_gains: float32 [2, 960], P(None, 'ctx')
- gains_mean: float32 [2, 960], P(None, 'ctx')
- gains_square: float32 [2, 960], P(None, 'ctx')
Inputs may be any that keep to these rules, and one draw needn't show every extreme that they name: Layout block r of every sequence is sequence block span_order[r] of 128 tokens; each number appears once.
All inputs are finite; a program needn't handle non-finite values.
Results may differ from a plain program's by a relative error of at most 0.015.
Values may be sent and summed in bfloat16 or wider, within the bound.
No kernel may reach another device: no remote copies, remote signals or barrier semaphores. Data moves between devices by JAX's collectives and lax.ppermute only.
A program may use at most 320 MiB of HBM per device.

v0:
```python
import jax
import jax.numpy as jnp
from jax import lax
from jax.sharding import PartitionSpec as P

D = 960
HEADS = 15
KV_HEADS = 5
HEAD_DIM = 64
FF = 2560
STEP = 10


eps = 1e-05
rope_base = 100000.0
beta_first = 0.9
beta_second = 0.95
adam_eps = 1e-08
masked_score = -1e30


def rope_tables(positions):
    halfway = HEAD_DIM // 2
    freqs = rope_base ** (-(jnp.arange(halfway, dtype=jnp.float32) * 2.0) / HEAD_DIM)
    angles = positions.astype(jnp.float32)[:, None] * freqs[None, :]
    return (jnp.cos(angles), jnp.sin(angles))


def rotate(field, cosine, sine):
    halfway = field.shape[-1] // 2
    first = field[..., :halfway]
    second = field[..., halfway:]
    cosine = cosine[:, None, :]
    sine = sine[:, None, :]
    return jnp.concatenate(
        [first * cosine - second * sine, second * cosine + first * sine], axis=-1
    )


def rotate_back(field, cosine, sine):
    halfway = field.shape[-1] // 2
    first = field[..., :halfway]
    second = field[..., halfway:]
    cosine = cosine[:, None, :]
    sine = sine[:, None, :]
    return jnp.concatenate(
        [first * cosine + second * sine, second * cosine - first * sine], axis=-1
    )


def positions_of(order, count, span):
    rows = jnp.arange(count, dtype=jnp.int32)
    slots = rows // span
    labels = jnp.arange(order.shape[0], dtype=jnp.int32)
    picked = jnp.sum(jnp.where(slots[:, None] == labels[None, :], order[None, :], 0), axis=1)
    return picked * span + rows % span


def rms_scale(rows):
    return lax.rsqrt(jnp.mean(rows * rows, axis=-1, keepdims=True) + eps)


def contract_rows(left, right):
    return lax.dot_general(
        left, right, (((0,), (0,)), ((), ())), preferred_element_type=jnp.float32
    )


def contract_cols(left, right):
    return lax.dot_general(
        left, right, (((1,), (1,)), ((), ())), preferred_element_type=jnp.float32
    )


def norm_back(grad_normed, rows, inverse, gain):
    scaled = grad_normed * gain
    inner = jnp.mean(scaled * rows, axis=-1, keepdims=True)
    rows_grad = inverse * (scaled - rows * inverse * inverse * inner)
    gain_grad = jnp.sum(grad_normed * rows * inverse, axis=0)
    return (rows_grad, gain_grad)


def probabilities(query_low, all_keys, visible):
    raw = jnp.einsum(
        "bqkgd,bskd->bkgqs", query_low, all_keys, preferred_element_type=jnp.float32
    ) * HEAD_DIM ** (-0.5)
    raw = jnp.where(visible, raw, masked_score)
    return jax.nn.softmax(raw, axis=-1)


def arrange(term, groups, owners, along):
    moved = term if along == 0 else jnp.transpose(term)
    return jnp.transpose(moved.reshape(groups, owners, -1), (1, 0, 2)).reshape(-1)


def restore(piece, master, along):
    if along == 0:
        return piece.reshape(master.shape)
    return jnp.transpose(piece.reshape(master.shape[1], master.shape[0]))


def adam_step(master, first, second, grad, rate, decay):
    new_first = beta_first * first + (1.0 - beta_first) * grad
    new_second = beta_second * second + (1.0 - beta_second) * grad * grad
    fix_one = 1.0 - beta_first**STEP
    fix_two = 1.0 - beta_second**STEP
    update = new_first / fix_one / (jnp.sqrt(new_second / fix_two) + adam_eps) + decay * master
    return (master - rate * update, new_first, new_second)


def on_device(
    inputs,
    cotangent,
    span_order,
    w_qkv,
    qkv_first,
    qkv_second,
    w_proj,
    proj_first,
    proj_second,
    w_expand,
    expand_first,
    expand_second,
    w_down,
    down_first,
    down_second,
    gains,
    gains_first,
    gains_second,
):
    groups = lax.axis_size("ctx")
    rank = lax.axis_index("ctx")
    full_qkv, full_proj, full_expand, full_down, full_gains = (
        lax.all_gather(w_qkv.astype(jnp.bfloat16), "ctx", axis=0, tiled=True),
        lax.all_gather(w_proj.astype(jnp.bfloat16), "ctx", axis=0, tiled=True),
        lax.all_gather(w_expand.astype(jnp.bfloat16), "ctx", axis=0, tiled=True),
        lax.all_gather(w_down.astype(jnp.bfloat16), "ctx", axis=0, tiled=True),
        lax.all_gather(gains.astype(jnp.bfloat16), "ctx", axis=1, tiled=True),
    )
    batch, local, width = inputs.shape
    length = local * groups
    every_pos = positions_of(span_order, length, local // 2)
    own_pos = lax.dynamic_slice_in_dim(every_pos, rank * local, local)
    cosine, sine = rope_tables(own_pos)
    kv_width = KV_HEADS * HEAD_DIM
    group = HEADS // KV_HEADS
    scale = HEAD_DIM ** (-0.5)
    count = batch * local
    gain_one = full_gains[0].astype(jnp.float32)
    gain_two = full_gains[1].astype(jnp.float32)
    visible = every_pos[None, :] <= own_pos[:, None]
    rows_in = inputs.reshape(count, width).astype(jnp.float32)
    inv_one = rms_scale(rows_in)
    normed_one = (rows_in * inv_one * gain_one).astype(jnp.bfloat16)
    mixed = jnp.dot(normed_one, full_qkv, preferred_element_type=jnp.float32)
    queries = mixed[:, :width].reshape(batch, local, HEADS, HEAD_DIM)
    keys = mixed[:, width : width + kv_width].reshape(batch, local, KV_HEADS, HEAD_DIM)
    values = mixed[:, width + kv_width :].reshape(batch, local, KV_HEADS, HEAD_DIM)
    query_low = (
        rotate(queries, cosine, sine)
        .astype(jnp.bfloat16)
        .reshape(batch, local, KV_HEADS, group, HEAD_DIM)
    )
    key_low = rotate(keys, cosine, sine).astype(jnp.bfloat16)
    value_low = values.astype(jnp.bfloat16)
    all_keys, all_values = (
        lax.all_gather(key_low, "ctx", axis=1, tiled=True),
        lax.all_gather(value_low, "ctx", axis=1, tiled=True),
    )
    probs = probabilities(query_low, all_keys, visible)
    prob_low = probs.astype(jnp.bfloat16)
    attended = jnp.einsum(
        "bkgqs,bskd->bqkgd", prob_low, all_values, preferred_element_type=jnp.float32
    )
    att_low = attended.reshape(count, width).astype(jnp.bfloat16)
    middle = rows_in + jnp.dot(att_low, full_proj, preferred_element_type=jnp.float32)
    inv_two = rms_scale(middle)
    normed_two = (middle * inv_two * gain_two).astype(jnp.bfloat16)
    expanded = jnp.dot(normed_two, full_expand, preferred_element_type=jnp.float32)
    gate = expanded[:, :FF]
    upward = expanded[:, FF:]
    hidden = (jax.nn.silu(gate) * upward).astype(jnp.bfloat16)
    result = middle + jnp.dot(hidden, full_down, preferred_element_type=jnp.float32)
    output = result.astype(jnp.bfloat16).reshape(batch, local, width)
    back_rows = cotangent.reshape(count, width)
    grad_down = contract_rows(hidden, back_rows)
    grad_hidden = contract_cols(back_rows, full_down)
    sigmoid = jax.nn.sigmoid(gate)
    grad_gate = grad_hidden * upward * sigmoid * (1.0 + gate * (1.0 - sigmoid))
    grad_up = grad_hidden * gate * sigmoid
    grad_expand_low = jnp.concatenate([grad_gate, grad_up], axis=1).astype(jnp.bfloat16)
    grad_expand = contract_rows(normed_two, grad_expand_low)
    grad_normed_two = contract_cols(grad_expand_low, full_expand)
    back_two, gain_grad_two = norm_back(grad_normed_two, middle, inv_two, gain_two)
    grad_middle = back_rows.astype(jnp.float32) + back_two
    middle_low = grad_middle.astype(jnp.bfloat16)
    grad_proj = contract_rows(att_low, middle_low)
    grad_att = (
        contract_cols(middle_low, full_proj)
        .astype(jnp.bfloat16)
        .reshape(batch, local, KV_HEADS, group, HEAD_DIM)
    )
    back_keys, back_values, back_probs, back_prob_low = (all_keys, all_values, probs, prob_low)
    grad_probs = jnp.einsum(
        "bqkgd,bskd->bkgqs", grad_att, back_values, preferred_element_type=jnp.float32
    )
    grad_scores = (
        back_probs * (grad_probs - jnp.sum(back_probs * grad_probs, axis=-1, keepdims=True))
    ).astype(jnp.bfloat16)
    grad_query = (
        jnp.einsum("bkgqs,bskd->bqkgd", grad_scores, back_keys, preferred_element_type=jnp.float32)
        * scale
    )
    key_terms = (
        jnp.einsum("bkgqs,bqkgd->bskd", grad_scores, query_low, preferred_element_type=jnp.float32)
        * scale
    )
    value_terms = jnp.einsum(
        "bkgqs,bqkgd->bskd", back_prob_low, grad_att, preferred_element_type=jnp.float32
    )
    grad_keys, grad_values = (
        lax.psum_scatter(
            key_terms.astype(jnp.bfloat16), "ctx", scatter_dimension=1, tiled=True
        ).astype(jnp.float32),
        lax.psum_scatter(
            value_terms.astype(jnp.bfloat16), "ctx", scatter_dimension=1, tiled=True
        ).astype(jnp.float32),
    )
    grad_mixed = jnp.concatenate(
        [
            rotate_back(grad_query.reshape(batch, local, HEADS, HEAD_DIM), cosine, sine).reshape(
                count, width
            ),
            rotate_back(grad_keys, cosine, sine).reshape(count, kv_width),
            grad_values.reshape(count, kv_width),
        ],
        axis=1,
    ).astype(jnp.bfloat16)
    grad_qkv = contract_rows(normed_one, grad_mixed)
    grad_normed_one = contract_cols(grad_mixed, full_qkv)
    back_one, gain_grad_one = norm_back(grad_normed_one, rows_in, inv_one, gain_one)
    input_grad = (grad_middle + back_one).astype(jnp.bfloat16).reshape(batch, local, width)
    grad_gains = jnp.stack([gain_grad_one, gain_grad_two])
    owners = lax.axis_size("dp")
    pieces = (
        lax.psum_scatter(
            arrange(grad_qkv, groups, owners, 0), ("dp", "ctx"), scatter_dimension=0, tiled=True
        ),
        lax.psum_scatter(
            arrange(grad_proj, groups, owners, 0), ("dp", "ctx"), scatter_dimension=0, tiled=True
        ),
        lax.psum_scatter(
            arrange(grad_expand, groups, owners, 0), ("dp", "ctx"), scatter_dimension=0, tiled=True
        ),
        lax.psum_scatter(
            arrange(grad_down, groups, owners, 0), ("dp", "ctx"), scatter_dimension=0, tiled=True
        ),
        lax.psum_scatter(
            arrange(grad_gains, groups, owners, 1), ("dp", "ctx"), scatter_dimension=0, tiled=True
        ),
    )
    whole_qkv, whole_proj, whole_expand, whole_down, whole_gains = (
        lax.all_gather(pieces[0].astype(jnp.bfloat16), "dp", axis=0, tiled=True).astype(
            jnp.float32
        ),
        lax.all_gather(pieces[1].astype(jnp.bfloat16), "dp", axis=0, tiled=True).astype(
            jnp.float32
        ),
        lax.all_gather(pieces[2].astype(jnp.bfloat16), "dp", axis=0, tiled=True).astype(
            jnp.float32
        ),
        lax.all_gather(pieces[3].astype(jnp.bfloat16), "dp", axis=0, tiled=True).astype(
            jnp.float32
        ),
        lax.all_gather(pieces[4].astype(jnp.bfloat16), "dp", axis=0, tiled=True).astype(
            jnp.float32
        ),
    )
    reduced = (
        restore(whole_qkv, w_qkv, 0),
        restore(whole_proj, w_proj, 0),
        restore(whole_expand, w_expand, 0),
        restore(whole_down, w_down, 0),
        restore(whole_gains, gains, 1),
    )
    new_qkv, qkv_mean, qkv_square = adam_step(
        w_qkv, qkv_first, qkv_second, reduced[0], 2.0 * D ** (-0.5), 0.1
    )
    new_proj, proj_mean, proj_square = adam_step(
        w_proj, proj_first, proj_second, reduced[1], 2.0 * (D // 8) ** (-0.5), 0.1
    )
    new_expand, expand_mean, expand_square = adam_step(
        w_expand, expand_first, expand_second, reduced[2], 2.0 * D ** (-0.5), 0.1
    )
    new_down, down_mean, down_square = adam_step(
        w_down, down_first, down_second, reduced[3], 2.0 * FF ** (-0.5), 0.1
    )
    new_gains, gains_mean, gains_square = adam_step(
        gains, gains_first, gains_second, reduced[4], 1.0, 0.0
    )
    return (
        output,
        input_grad,
        new_qkv,
        qkv_mean,
        qkv_square,
        new_proj,
        proj_mean,
        proj_square,
        new_expand,
        expand_mean,
        expand_square,
        new_down,
        down_mean,
        down_square,
        new_gains,
        gains_mean,
        gains_square,
    )


def solution(mesh):
    in_specs = (
        P("dp", "ctx", None),
        P("dp", "ctx", None),
        P(),
        P("ctx", None),
        P("ctx", None),
        P("ctx", None),
        P("ctx", None),
        P("ctx", None),
        P("ctx", None),
        P("ctx", None),
        P("ctx", None),
        P("ctx", None),
        P("ctx", None),
        P("ctx", None),
        P("ctx", None),
        P(None, "ctx"),
        P(None, "ctx"),
        P(None, "ctx"),
    )
    out_specs = (
        P("dp", "ctx", None),
        P("dp", "ctx", None),
        P("ctx", None),
        P("ctx", None),
        P("ctx", None),
        P("ctx", None),
        P("ctx", None),
        P("ctx", None),
        P("ctx", None),
        P("ctx", None),
        P("ctx", None),
        P("ctx", None),
        P("ctx", None),
        P("ctx", None),
        P(None, "ctx"),
        P(None, "ctx"),
        P(None, "ctx"),
    )
    return jax.shard_map(
        on_device, mesh=mesh, in_specs=in_specs, out_specs=out_specs, check_vma=False
    )
```

profile of v0, /device:TPU:1, one launch (start us, length us, event | category | flops | bytes accessed | tf_op | source)
XLA Modules:
  0.0 1060.4 jit_solution(11292182160342503384)
XLA Ops:
  9.9 16.1 %all-gather = bf16[8,120,2]{1,2,0:T(2,128)(2,1)S(1)} all-gather(bf16[1,120,2]{1,2,0:T(2,128)(2,1)S(1)} %convert_bitcast_fusion), channel_id=1, replica_groups=mesh['dp'=16,'ctx'=8] {'ctx'}, dimensions={0}, use_global_device_ids=true | all-gather | bytes 4320 | tf_op jit(solution)/shard_map/all_gather | solution.py:138
  28.5 27.2 %all-gather.11.cloned.1.call-done = bf16[960,1600]{1,0:T(8,128)(2,1)} async-done(((bf16[120,1600]{1,0:T(8,128)(2,1)}), bf16[960,1600]{1,0:T(8,128)(2,1)}) %all-gather.11.cloned.1.call-update) | async-done | bytes 3072016 | tf_op jit(solution)/shard_map/all_gather | solution.py:134
  71.1 27.7 %all-gather.15.cloned.1.call-done = bf16[1,2048,5,64]{1,3,2,0:T(8,128)(2,1)} async-done(((bf16[1,256,5,64]{1,3,2,0:T(8,128)(2,1)}), bf16[1,2048,5,64]{1,3,2,0:T(8,128)(2,1)}) %all-gather.15.cloned.1.call-update) | async-done | bytes 1310736 | tf_op jit(solution)/shard_map/all_gather | solution.py:167
  98.8 14.0 %fusion.5 = (f32[5,3,256]{2,1,0:T(4,128)S(1)}, f32[5,2048,256,3]{2,1,3,0:T(8,128)}) fusion(pred[256,2048]{0,1:T(8,128)(4,1)S(1)} %broadcast_compare_fusion, bf16[256,5,3,32]{0,3,2,1:T(8,128)(2,1)S(1)} %bitcast.197, bf16[256,5,3,32]{0,3,2,1:T(8,128)(2,1)S(1)} %bitcast.195, bf16[1,2048,5,64]{1,3,2,0:T(8,128)(2,1)} %all-gather.15.cloned.1.call-done), kind=kOutput, calls=%fused_computation.9 | convolution fusion | flops 1031205120 | bytes 33799168 | tf_op jit(solution)/shard_map/bqkgd,bskd->bkgqs/dot_general | solution.py:84
  112.8 13.8 %fusion.4 = f32[5,3,256]{2,1,0:T(4,128)S(1)} fusion(f32[5,2048,256,3]{2,1,3,0:T(8,128)} %get-tuple-element.129, f32[5,3,256]{2,1,0:T(4,128)S(1)} %get-tuple-element.128, pred[256,2048]{0,1:T(8,128)(4,1)S(1)} %broadcast_compare_fusion), kind=kLoop, calls=%fused_computation.8 | loop fusion | flops 31453440 | bytes 32012288 | tf_op jit(solution)/shard_map/reduce_sum | solution.py:88
  126.6 14.9 %all-gather.13.cloned.1.call-done = bf16[1,2048,5,64]{1,3,2,0:T(8,128)(2,1)} async-done(((bf16[1,256,5,64]{1,3,2,0:T(8,128)(2,1)}), bf16[1,2048,5,64]{1,3,2,0:T(8,128)(2,1)}) %all-gather.13.cloned.1.call-update) | async-done | bytes 1310736 | tf_op jit(solution)/shard_map/all_gather | solution.py:168
  141.6 14.5 %fusion.35 = bf16[5,64,3,256]{3,1,2,0:T(8,128)(2,1)S(1)} fusion(bf16[1,2048,5,64]{1,3,2,0:T(8,128)(2,1)} %all-gather.13.cloned.1.call-done, f32[5,3,256]{2,1,0:T(4,128)S(1)} %fusion.4, f32[5,3,256]{2,1,0:T(4,128)S(1)} %get-tuple-element.128, f32[5,2048,256,3]{2,1,3,0:T(8,128)} %get-tuple-element.129, pred[256,2048]{0,1:T(8,128)(4,1)S(1)} %broadcast_compare_fusion), kind=kOutput, calls=%fused_computation.57 | convolution fusion | flops 1046200320 | bytes 33814528 | tf_op jit(solution)/shard_map/bkgqs,bskd->bqkgd/dot_general | solution.py:172
  156.1 28.9 %all-gather.17.cloned.1.call-done = bf16[960,960]{1,0:T(8,128)(2,1)} async-done(((bf16[120,960]{1,0:T(8,128)(2,1)}), bf16[960,960]{1,0:T(8,128)(2,1)}) %all-gather.17.cloned.1.call-update) | async-done | bytes 1843216 | tf_op jit(solution)/shard_map/all_gather | solution.py:135
  187.5 109.5 %all-gather.19.cloned.1.call-done = bf16[960,5120]{1,0:T(8,128)(2,1)} async-done(((bf16[120,5120]{1,0:T(8,128)(2,1)}), bf16[960,5120]{1,0:T(8,128)(2,1)}) %all-gather.19.cloned.1.call-update) | async-done | bytes 9830416 | tf_op jit(solution)/shard_map/all_gather | solution.py:136
  296.9 8.7 fusion.84
  305.7 54.5 %all-gather.21.cloned.1.call-done = bf16[2560,960]{1,0:T(8,128)(2,1)} async-done(((bf16[320,960]{1,0:T(8,128)(2,1)}), bf16[2560,960]{1,0:T(8,128)(2,1)}) %all-gather.21.cloned.1.call-update) | async-done | bytes 4915216 | tf_op jit(solution)/shard_map/all_gather | solution.py:137
  360.2 9.0 multiply_convert_fusion.1
  369.3 8.2 fusion.25
  385.2 22.4 %fusion = (f32[5,3,256]{2,1,0:T(4,128)S(1)}, f32[5,2048,256,3]{2,1,3,0:T(8,128)}) fusion(f32[5,3,256]{2,1,0:T(4,128)S(1)} %fusion.4, f32[5,3,256]{2,1,0:T(4,128)S(1)} %get-tuple-element.128, f32[5,2048,256,3]{2,1,3,0:T(8,128)} %get-tuple-element.129, pred[256,2048]{0,1:T(8,128)(4,1)S(1)} %broadcast_compare_fusion, bf16[256,5,3,64]{0,3,2,1:T(8,128)(2,1)S(1)} %bitcast.209, ...), kind=kOutput, calls=%fused_computation.3 | convolution fusion | flops 1053815040 | bytes 65287168 | tf_op jit(solution)/shard_map/bqkgd,bskd->bkgqs/dot_general | solution.py:204
  407.6 27.1 %fusion.6 = bf16[5,3,256,2048]{2,3,1,0:T(8,128)(2,1)} fusion(f32[5,2048,256,3]{2,1,3,0:T(8,128)} %get-tuple-element.134, f32[5,3,256]{2,1,0:T(4,128)S(1)} %get-tuple-element.133, f32[5,3,256]{2,1,0:T(4,128)S(1)} %fusion.4, f32[5,3,256]{2,1,0:T(4,128)S(1)} %get-tuple-element.128, f32[5,2048,256,3]{2,1,3,0:T(8,128)} %get-tuple-element.129, ...), kind=kLoop, calls=%fused_computation.11 | loop fusion | flops 55050240 | bytes 79213568 | tf_op jit(solution)/shard_map/reshape.21
  434.7 11.3 %fusion.20 = bf16[1,2048,5,64]{1,3,2,0:T(8,128)(2,1)} fusion(bf16[5,3,256,2048]{2,3,1,0:T(8,128)(2,1)} %fusion.6, bf16[256,5,3,32]{0,3,2,1:T(8,128)(2,1)S(1)} %bitcast.198, bf16[256,5,3,32]{0,3,2,1:T(8,128)(2,1)S(1)} %bitcast.196), kind=kOutput, calls=%fused_computation.30 | convolution fusion | flops 1008926720 | bytes 17530880 | tf_op jit(solution)/shard_map/bkgqs,bqkgd->bskd/dot_general | solution.py:215
  462.6 19.1 %reshape.386 = f32[8,16,38400]{2,1,0:T(8,128)} reshape(f32[960,5120]{1,0:T(8,128)} %fusion.25) | data formatting | bytes 39321600 | tf_op jit(solution)/shard_map/reshape | solution.py:93
  481.8 20.3 %copy.159 = f32[8,16,38400]{2,0,1:T(8,128)} copy(f32[8,16,38400]{2,1,0:T(8,128)} %reshape.386) | data formatting | bytes 39321600 | tf_op jit(solution)/shard_map/reshape | solution.py:93
  502.1 19.0 %reshape.387 = f32[4915200]{0:T(1024)} reshape(f32[16,8,38400]{2,1,0:T(8,128)} %bitcast.187) | data formatting | bytes 39321600 | tf_op jit(solution)/shard_map/reshape | solution.py:93
  521.1 15.6 %fusion.21 = bf16[1,2048,5,64]{1,3,2,0:T(8,128)(2,1)} fusion(bf16[256,5,3,64]{0,3,2,1:T(8,128)(2,1)S(1)} %bitcast.210, f32[5,3,256]{2,1,0:T(4,128)S(1)} %fusion.4, f32[5,3,256]{2,1,0:T(4,128)S(1)} %get-tuple-element.128, f32[5,2048,256,3]{2,1,3,0:T(8,128)} %get-tuple-element.129, pred[256,2048]{0,1:T(8,128)(4,1)S(1)} %broadcast_compare_fusion), kind=kOutput, calls=%fused_computation.31 | convolution fusion | flops 1046609920 | bytes 33814528 | tf_op jit(solution)/shard_map/bkgqs,bqkgd->bskd/dot_general | solution.py:218
  542.3 12.3 %reshape.390 = f32[8,16,19200]{2,1,0:T(8,128)} reshape(f32[2560,960]{1,0:T(8,128)} %fusion.56) | data formatting | bytes 19660800 | tf_op jit(solution)/shard_map/reshape | solution.py:93
  554.6 13.3 %copy.143 = f32[16,8,19200]{2,1,0:T(8,128)} copy(f32[16,8,19200]{2,0,1:T(8,128)} %bitcast.188) | data formatting | bytes 19660800 | tf_op jit(solution)/shard_map/transpose | solution.py:93
  567.9 9.9 reshape.391
  592.0 8.8 reshape.378
  600.8 8.9 copy.160
  622.1 216.5 %all-reduce.14 = (bf16[1536000]{0:T(1024)(128)(2,1)}, bf16[921600]{0:T(1024)(128)(2,1)}, bf16[1920]{0:T(1024)(128)(2,1)S(1)}, bf16[4915200]{0:T(1024)(128)(2,1)}, bf16[2457600]{0:T(1024)(128)(2,1)}) all-reduce(f32[1536000]{0:T(1024)} %reshape.379, f32[921600]{0:T(1024)} %reshape.383, ...), channel_id=4, replica_groups=mesh['dp'=16,'ctx'=8] {'dp','ctx'}, use_global_device_ids=true, to_apply=%region_10.11.clone | all-reduce | flops 9832320 | bytes 58993920
  850.1 28.4 %all-gather.2 = bf16[16,1,19200]{2,1,0:T(2,128)(2,1)S(1)} all-gather(bf16[1,1,19200]{2,1,0:T(2,128)(2,1)S(1)} %reshape.422), channel_id=1, replica_groups=mesh['dp'=16,'ctx'=8] {'dp'}, dimensions={0}, use_global_device_ids=true | all-gather | bytes 652800 | tf_op jit(solution)/shard_map/all_gather | solution.py:272
  885.3 32.7 %all-reduce.2 = bf16[240]{0:T(256)(128)(2,1)S(1)} all-reduce(bf16[240]{0:T(256)(128)(2,1)S(1)} %dynamic-update-slice.2), channel_id=1, replica_groups=mesh['dp'=16,'ctx'=8] {'dp'}, use_global_device_ids=true, to_apply=%add.2 | all-reduce | flops 240 | bytes 960
  925.3 54.3 %all-reduce.13.cloned.1.call-done = (bf16[192000]{0:T(1024)(128)(2,1)}, bf16[115200]{0:T(1024)(128)(2,1)}) async-done(((bf16[192000]{0:T(1024)(128)(2,1)}, bf16[115200]{0:T(1024)(128)(2,1)}), (bf16[192000]{0:T(1024)(128)(2,1)}, bf16[115200]{0:T(1024)(128)(2,1)})) %all-reduce.13.cloned.1.call-update) | async-done | bytes 614416
  987.9 46.4 %all-gather.23.cloned.1.call-done = bf16[16,1,38400]{2,1,0:T(2,128)(2,1)} async-done(((bf16[1,1,38400]{2,1,0:T(2,128)(2,1)}), bf16[16,1,38400]{2,1,0:T(2,128)(2,1)}) %all-gather.23.cloned.1.call-update) | async-done | bytes 1228816 | tf_op jit(solution)/shard_map/all_gather | solution.py:269
  1034.3 8.6 convert_reduce_fusion
  1045.1 8.3 multiply_subtract_fusion
  (185 shorter events, 113.0 us)
Async XLA Ops:
  7.2 48.6 %all-gather.11.cloned.1.call-start = ((), (), s32[]{:S(2)}) async-start(), calls=%async_computation.2 | async-start | bytes 3594240 | tf_op jit(solution)/shard_map/all_gather | solution.py:134
  9.2 89.6 %all-gather.15.cloned.1.call-start = ((), (), s32[]{:S(2)}) async-start(), calls=%async_computation.4 | async-start | bytes 1474560 | tf_op jit(solution)/shard_map/all_gather | solution.py:167
  28.2 27.5 %copy-start.31 = (f32[256]{0:T(256)}, f32[256]{0:T(256)S(1)}, u32[]{:S(2)}) copy-start(f32[256]{0:T(256)S(1)} %add_rsqrt_fusion.1) | copy-start | bytes 3076
  28.3 27.5 %copy-start.29 = (f32[1,960]{1,0:T(1,128)}, f32[1,960]{1,0:T(1,128)S(1)}, u32[]{:S(2)}) copy-start(f32[1,960]{1,0:T(1,128)S(1)} %get-tuple-element.125) | copy-start | bytes 11524
  28.5 42.4 %copy-start.24 = (f32[256,32]{0,1:T(8,128)}, f32[256,32]{0,1:T(8,128)S(1)}, u32[]{:S(2)}) copy-start(f32[256,32]{0,1:T(8,128)S(1)} %get-tuple-element.126) | copy-start | bytes 98308
  28.5 42.4 %copy-start.26 = (f32[256,32]{0,1:T(8,128)}, f32[256,32]{0,1:T(8,128)S(1)}, u32[]{:S(2)}) copy-start(f32[256,32]{0,1:T(8,128)S(1)} %get-tuple-element.127) | copy-start | bytes 98308
  61.4 80.1 %all-gather.13.cloned.1.call-start = ((), (), s32[]{:S(2)}) async-start(), calls=%async_computation.3 | async-start | bytes 1474560 | tf_op jit(solution)/shard_map/all_gather | solution.py:168
  63.2 121.8 %all-gather.17.cloned.1.call-start = ((), (), s32[]{:S(2)}) async-start(), calls=%async_computation.5 | async-start | bytes 2211840 | tf_op jit(solution)/shard_map/all_gather | solution.py:135
  64.0 233.0 %all-gather.19.cloned.1.call-start = ((), (), s32[]{:S(2)}) async-start(), calls=%async_computation.6 | async-start | bytes 11059200 | tf_op jit(solution)/shard_map/all_gather | solution.py:136
  65.3 295.0 %all-gather.21.cloned.1.call-start = ((), (), s32[]{:S(2)}) async-start(), calls=%async_computation.7 | async-start | bytes 5898240 | tf_op jit(solution)/shard_map/all_gather | solution.py:137
  67.7 518.6 %reduce-scatter.3.cloned.1.call-start = ((), (), s32[]{:S(2)}) async-start(), calls=%async_computation.8 | async-start | bytes 1474560 | tf_op jit(solution)/shard_map/reduce_scatter | solution.py:222
  71.1 41.7 %copy-start.11 = (bf16[1,256,15,32]{1,3,2,0:T(8,128)(2,1)}, bf16[1,256,15,32]{1,3,2,0:T(8,128)(2,1)S(1)}, u32[]{:S(2)}) copy-start(bf16[1,256,15,32]{1,3,2,0:T(8,128)(2,1)S(1)} %get-tuple-element.118) | copy-start | bytes 737284
  71.1 41.7 %copy-start.13 = (bf16[1,256,15,32]{1,3,2,0:T(8,128)(2,1)}, bf16[1,256,15,32]{1,3,2,0:T(8,128)(2,1)S(1)}, u32[]{:S(2)}) copy-start(bf16[1,256,15,32]{1,3,2,0:T(8,128)(2,1)S(1)} %get-tuple-element.119) | copy-start | bytes 737284
  126.6 58.3 %copy-start.6 = (bf16[1,256,960]{1,2,0:T(8,128)(2,1)S(1)}, bf16[1,256,960]{1,2,0:T(8,128)(2,1)}, u32[]{:S(2)}) copy-start(bf16[1,256,960]{1,2,0:T(8,128)(2,1)} %param.18) | copy-start | bytes 1474564
  187.4 193.5 %copy-start.3 = (f32[256,960]{0,1:T(8,128)}, f32[256,960]{0,1:T(8,128)S(1)}, u32[]{:S(2)}) copy-start(f32[256,960]{0,1:T(8,128)S(1)} %get-tuple-element.131) | copy-start | bytes 2949124
  296.9 63.3 %copy-start.16 = (bf16[1,256,960]{1,2,0:T(8,128)(2,1)S(1)}, bf16[1,256,960]{1,2,0:T(8,128)(2,1)}, u32[]{:S(2)}) copy-start(bf16[1,256,960]{1,2,0:T(8,128)(2,1)} %param.19) | copy-start | bytes 1474564
  360.2 17.3 %slice-start = ((s8[9830400]{0:T(1024)(128)(4,1)}), s8[4194304]{0:T(1024)(128)(4,1)S(1)}, s32[]{:S(2)}) async-start(s8[9830400]{0:T(1024)(128)(4,1)} %bitcast.191), calls=%async_computation.12 | async-start | bytes 8388608
  360.2 17.3 %slice-start.1 = ((s8[9830400]{0:T(1024)(128)(4,1)}), s8[4194304]{0:T(1024)(128)(4,1)S(1)}, s32[]{:S(2)}) async-start(s8[9830400]{0:T(1024)(128)(4,1)} %bitcast.191), calls=%async_computation.13 | async-start | bytes 8388608
  407.6 27.1 %copy-start.12 = (bf16[1,256,15,32]{1,3,2,0:T(8,128)(2,1)S(1)}, bf16[1,256,15,32]{1,3,2,0:T(8,128)(2,1)}, u32[]{:S(2)}) copy-start(bf16[1,256,15,32]{1,3,2,0:T(8,128)(2,1)} %copy-done.11) | copy-start | bytes 737284
  407.6 27.1 %copy-start.14 = (bf16[1,256,15,32]{1,3,2,0:T(8,128)(2,1)S(1)}, bf16[1,256,15,32]{1,3,2,0:T(8,128)(2,1)}, u32[]{:S(2)}) copy-start(bf16[1,256,15,32]{1,3,2,0:T(8,128)(2,1)} %copy-done.13) | copy-start | bytes 737284
  446.1 141.2 %reduce-scatter.5.cloned.1.call-start = ((), (), s32[]{:S(2)}) async-start(), calls=%async_computation.9 | async-start | bytes 1474560 | tf_op jit(solution)/shard_map/reduce_scatter | solution.py:225
  521.1 15.6 %copy-start.17 = (bf16[1,256,960]{1,2,0:T(8,128)(2,1)S(1)}, bf16[1,256,960]{1,2,0:T(8,128)(2,1)}, u32[]{:S(2)}) copy-start(bf16[1,256,960]{1,2,0:T(8,128)(2,1)} %param.19) | copy-start | bytes 1474564
  521.1 15.6 %copy-start.20 = (bf16[256,2560]{1,0:T(8,128)(2,1)S(1)}, bf16[256,2560]{1,0:T(8,128)(2,1)}, u32[]{:S(2)}) copy-start(bf16[256,2560]{1,0:T(8,128)(2,1)} %get-tuple-element.115) | copy-start | bytes 3932164
  536.7 443.0 %all-reduce.13.cloned.1.call-start = ((), (), s32[]{:S(2)}) async-start(), calls=%async_computation.11 | async-start | bytes 1232896
  567.9 9.9 copy-start.5
  622.1 219.9 %copy-start.4 = (f32[256,960]{0,1:T(8,128)S(1)}, f32[256,960]{0,1:T(8,128)}, u32[]{:S(2)}) copy-start(f32[256,960]{0,1:T(8,128)} %copy-done.3) | copy-start | bytes 2949124
  842.0 192.3 %all-gather.23.cloned.1.call-start = ((), (), s32[]{:S(2)}) async-start(), calls=%async_computation.10 | async-start | bytes 2611200 | tf_op jit(solution)/shard_map/all_gather | solution.py:269
  878.4 39.8 %copy-start.34 = (f32[2,120]{1,0:T(2,128)S(1)}, f32[2,120]{1,0:T(2,128)}, u32[]{:S(2)}) copy-start(f32[2,120]{1,0:T(2,128)} %param.33) | copy-start | bytes 2884
  878.4 39.8 %copy-start.35 = (f32[2,120]{1,0:T(2,128)S(1)}, f32[2,120]{1,0:T(2,128)}, u32[]{:S(2)}) copy-start(f32[2,120]{1,0:T(2,128)} %param.34) | copy-start | bytes 2884
  878.5 39.8 %copy-start.36 = (f32[2,120]{1,0:T(2,128)S(1)}, f32[2,120]{1,0:T(2,128)}, u32[]{:S(2)}) copy-start(f32[2,120]{1,0:T(2,128)} %param.35) | copy-start | bytes 2884
  878.5 40.4 %copy-start.1 = (f32[256,960]{0,1:T(8,128)S(1)}, f32[256,960]{0,1:T(8,128)}, u32[]{:S(2)}) copy-start(f32[256,960]{0,1:T(8,128)} %copy-done) | copy-start | bytes 2949124
  921.3 60.8 %copy-start.19 = (f32[120,960]{1,0:T(8,128)S(1)}, f32[120,960]{1,0:T(8,128)}, u32[]{:S(2)}) copy-start(f32[120,960]{1,0:T(8,128)} %param.24) | copy-start | bytes 1382404
  (21 other events, 80.3 us)
Sparse Core Ops, SparseCore 0:
  10.2 45.4 all-gather.10
  61.6 37.2 all-gather.14
  101.0 40.5 all-gather.12
  143.6 41.2 all-gather.16
  187.0 109.8 all-gather.18
  299.0 61.1 all-gather.20
  446.2 33.6 reduce-scatter.2
  536.8 33.6 reduce-scatter.4
  842.1 137.5 all-reduce.12
  982.9 51.3 all-gather.22
where the time goes:
time: 1070 us; the launch traced here: 1060 us
  waiting for transfers between devices  364 us (34%)
  blocking collectives  294 us (27%)
  local copies, waits for them, and re-layouts  154 us (14%)
  matrix products  144 us (13%)
  other arithmetic  87.1 us (8%)
  between operations  17 us (2%)
    unnamed x2, blocking collectives  249 us
    all_gather x1, waiting for transfers between devices, on_device(): lax.all_gather(w_expand.astype(jnp.bfloat16), 'ctx', axis=0, tiled=True)  109 us
    reshape x8, local copies, waits for them, and re-layouts, arrange(): moved.reshape(groups, owners, -1)  80.5 us
    all_gather x1, waiting for transfers between devices, on_device(): lax.all_gather(w_down.astype(jnp.bfloat16), 'ctx', axis=0, tiled=True)  54.5 us
    unnamed x11, waiting for transfers between devices  54.5 us
    all_gather x1, waiting for transfers between devices, on_device(): lax.all_gather(pieces[2].astype(jnp.bfloat16), 'dp', axis=0, tiled=True)  46.4 us
    reshape x5, local copies, waits for them, and re-layouts, arrange(): jnp.transpose(moved.reshape(groups, owners, -1), (1, 0, 2)).reshape(-1)  42.5 us
    all_gather x1, waiting for transfers between devices, on_device(): lax.all_gather(w_proj.astype(jnp.bfloat16), 'ctx', axis=0, tiled=True)  28.9 us
  transfers between devices with their start and end apart: 10, of which 8 were waited for; matrix products, arithmetic and copies ran while one was open for 22% of the time, Pallas kernels for 0%

commit v1 on v0

v1 whole, which is shorter than its diff:
```python
import itertools

import jax
import jax.numpy as jnp
from jax import lax
from jax.experimental import pallas as pl
from jax.experimental.pallas import tpu as pltpu
from jax.sharding import PartitionSpec as P

D = 960
HEADS = 15
KV_HEADS = 5
GROUP = HEADS // KV_HEADS
HEAD_DIM = 64
FF = 2560
STEP = 10
HALF = FF // 2
QKVW = D + 2 * KV_HEADS * HEAD_DIM
PART = 896


eps = 1e-05
rope_base = 100000.0
beta_first = 0.9
beta_second = 0.95
adam_eps = 1e-08
masked_score = -1e30
low = jnp.bfloat16


def linear(zh, y, core, zl, x):
    return (zh * 8 + y * 2 + core) * 8 + zl * 4 + x


def send(value, target):
    pairs = []
    for place in itertools.product(range(2), range(4), range(2), range(2), range(4)):
        to = target(*place)
        if to is not None:
            pairs.append((linear(*place), linear(*to)))
    return lax.ppermute(value, ("dp", "ctx"), pairs)


def to_x(k):
    return lambda zh, y, core, zl, x: (zh, y, core, zl, x ^ k)


def to_x_owner(k):
    return lambda zh, y, core, zl, x: (zh, y, core, zl, x ^ k) if core == zl else None


def to_core(zh, y, core, zl, x):
    return (zh, y, 1 - core, zl, x)


def to_z(step):
    def target(zh, y, core, zl, x):
        z = (zh * 2 + zl + step) % 4
        return (z // 2, y, core, z % 2, x)

    return target


def to_z_from(step, owner):
    def target(zh, y, core, zl, x):
        if (core == zl) != owner:
            return None
        z = (zh * 2 + zl + step) % 4
        return (z // 2, y, core, z % 2, x)

    return target


def to_chip(k):
    return lambda zh, y, core, zl, x: (zh ^ (k >> 2), y ^ (k & 3), core, zl, x)


def to_chip_owner(k):
    return lambda zh, y, core, zl, x: (
        (zh ^ (k >> 2), y ^ (k & 3), core, zl, x) if core == zl else None
    )


def pick(stack, index):
    return lax.dynamic_index_in_dim(stack, index, 0, keepdims=False)


def reduce_direct(stack, me, targets):
    total = pick(stack, me).astype(jnp.float32)
    for k, target in targets:
        total = total + send(pick(stack, me ^ k), target).astype(jnp.float32)
    return total.astype(low)


def gather_direct(piece, me, targets):
    count = len(targets) + 1
    whole = jnp.zeros((count,) + piece.shape, piece.dtype)
    whole = lax.dynamic_update_index_in_dim(whole, piece, me, 0)
    for k, target in targets:
        whole = lax.dynamic_update_index_in_dim(whole, send(piece, target), me ^ k, 0)
    return whole


def rope_tables(positions):
    halfway = HEAD_DIM // 2
    freqs = rope_base ** (-(jnp.arange(halfway, dtype=jnp.float32) * 2.0) / HEAD_DIM)
    angles = freqs[:, None] * positions.astype(jnp.float32)[None, :]
    return (jnp.cos(angles), jnp.sin(angles))


def rotate(field, cosine, sine):
    halfway = HEAD_DIM // 2
    first = field[:, :halfway]
    second = field[:, halfway:]
    return jnp.concatenate(
        [first * cosine - second * sine, second * cosine + first * sine], axis=1
    )


def rotate_back(field, cosine, sine):
    halfway = HEAD_DIM // 2
    first = field[:, :halfway]
    second = field[:, halfway:]
    return jnp.concatenate(
        [first * cosine + second * sine, second * cosine - first * sine], axis=1
    )


def positions_of(order, count, span):
    rows = jnp.arange(count, dtype=jnp.int32)
    slots = rows // span
    labels = jnp.arange(order.shape[0], dtype=jnp.int32)
    picked = jnp.sum(jnp.where(slots[:, None] == labels[None, :], order[None, :], 0), axis=1)
    return picked * span + rows % span


def rms_scale(rows):
    return lax.rsqrt(jnp.mean(rows * rows, axis=-1, keepdims=True) + eps)


def contract(left, right, left_axis, right_axis):
    return lax.dot_general(
        left,
        right,
        (((left_axis,), (right_axis,)), ((), ())),
        preferred_element_type=jnp.float32,
    )


def norm_back(grad_normed, rows, inverse, gain):
    scaled = grad_normed * gain
    inner = jnp.mean(scaled * rows, axis=-1, keepdims=True)
    rows_grad = inverse * (scaled - rows * inverse * inverse * inner)
    gain_grad = jnp.sum(grad_normed * rows * inverse, axis=0)
    return (rows_grad, gain_grad)


def load_keys(kv_ref):
    columns = jnp.concatenate([kv_ref[j, 0] for j in range(kv_ref.shape[0])], axis=1)
    return columns, columns.T


def attend_kernel(q_ref, kv_ref, bias_ref, o_ref, lse_ref):
    columns, rows = load_keys(kv_ref)
    bias = bias_ref[...]
    blank = jnp.zeros((HEAD_DIM, q_ref.shape[1]), low)
    for h in range(GROUP):
        part = pl.ds(h * HEAD_DIM, HEAD_DIM)
        query = jnp.concatenate([q_ref[part, :], blank], axis=0)
        scores = contract(rows, query, 1, 0) + bias
        top = jnp.max(scores, axis=0, keepdims=True)
        weights = jnp.exp(scores - top)
        total = jnp.sum(weights, axis=0, keepdims=True)
        mixed = contract(columns[HEAD_DIM:], weights.astype(low), 1, 0)
        o_ref[part, :] = (mixed / total).astype(low)
        lse_ref[h] = top + jnp.log(total)


def attend_back_kernel(q_ref, kv_ref, bias_ref, do_ref, o_ref, lse_ref, dq_ref, dkv_ref):
    columns, rows = load_keys(kv_ref)
    bias = bias_ref[...]
    local = q_ref.shape[1]
    blank = jnp.zeros((HEAD_DIM, local), low)
    terms = None
    for h in range(GROUP):
        part = pl.ds(h * HEAD_DIM, HEAD_DIM)
        query = jnp.concatenate([q_ref[part, :], blank], axis=0)
        back = jnp.concatenate([blank, do_ref[part, :]], axis=0)
        delta = jnp.sum(
            do_ref[part, :].astype(jnp.float32) * o_ref[part, :].astype(jnp.float32),
            axis=0,
            keepdims=True,
        )
        weights = jnp.exp(contract(rows, query, 1, 0) + bias - lse_ref[h])
        grad = contract(rows, back, 1, 0)
        scores = (weights * (grad - delta)).astype(low)
        dq_ref[part, :] = contract(columns[:HEAD_DIM], scores, 1, 0) * HEAD_DIM ** (-0.5)
        term = contract(scores, query, 1, 1) + contract(weights.astype(low), back, 1, 1)
        terms = term if terms is None else terms + term
    for j in range(dkv_ref.shape[0]):
        dkv_ref[j, 0] = terms[j * local : (j + 1) * local].astype(low)


def attention_specs(chunks, local):
    wide = GROUP * HEAD_DIM
    heads = pl.BlockSpec((wide, local), lambda g: (g, 0))
    keys = pl.BlockSpec((chunks, 1, 2 * HEAD_DIM, local), lambda g: (0, g, 0, 0))
    bias = pl.BlockSpec((chunks * local, local), lambda g: (0, 0))
    sums = pl.BlockSpec((GROUP, 1, local), lambda g: (g, 0, 0))
    return heads, keys, bias, sums


def attend(query, keys, bias):
    chunks, _, _, local = keys.shape
    heads, kv, mask, sums = attention_specs(chunks, local)
    flops = 4 * HEADS * local * chunks * local * HEAD_DIM
    return pl.pallas_call(
        attend_kernel,
        grid=(KV_HEADS,),
        out_shape=(
            jax.ShapeDtypeStruct((D, local), low),
            jax.ShapeDtypeStruct((HEADS, 1, local), jnp.float32),
        ),
        in_specs=[heads, kv, mask],
        out_specs=(heads, sums),
        compiler_params=pltpu.CompilerParams(vmem_limit_bytes=48 * 1024 * 1024),
        cost_estimate=pl.CostEstimate(
            flops=4 * flops, bytes_accessed=8 * 1024 * 1024, transcendentals=0
        ),
        name="attend",
    )(query, keys, bias)


def attend_back(query, keys, bias, back, out, lse):
    chunks, _, _, local = keys.shape
    heads, kv, mask, sums = attention_specs(chunks, local)
    grads = pl.BlockSpec((chunks, 1, local, 2 * HEAD_DIM), lambda g: (0, g, 0, 0))
    flops = 10 * HEADS * local * chunks * local * HEAD_DIM
    return pl.pallas_call(
        attend_back_kernel,
        grid=(KV_HEADS,),
        out_shape=(
            jax.ShapeDtypeStruct((D, local), jnp.float32),
            jax.ShapeDtypeStruct((chunks, KV_HEADS, local, 2 * HEAD_DIM), low),
        ),
        in_specs=[heads, kv, mask, heads, heads, sums],
        out_specs=(heads, grads),
        compiler_params=pltpu.CompilerParams(vmem_limit_bytes=48 * 1024 * 1024),
        cost_estimate=pl.CostEstimate(
            flops=4 * flops, bytes_accessed=8 * 1024 * 1024, transcendentals=0
        ),
        name="attend_back",
    )(query, keys, bias, back, out, lse)


def adam_step(master, first, second, grad, rate, decay):
    new_first = beta_first * first + (1.0 - beta_first) * grad
    new_second = beta_second * second + (1.0 - beta_second) * grad * grad
    fix_one = 1.0 - beta_first**STEP
    fix_two = 1.0 - beta_second**STEP
    update = new_first / fix_one / (jnp.sqrt(new_second / fix_two) + adam_eps) + decay * master
    return (master - rate * update, new_first, new_second)


def on_device(
    inputs,
    cotangent,
    span_order,
    w_qkv,
    qkv_first,
    qkv_second,
    w_proj,
    proj_first,
    proj_second,
    w_expand,
    expand_first,
    expand_second,
    w_down,
    down_first,
    down_second,
    gains,
    gains_first,
    gains_second,
):
    dp = lax.axis_index("dp")
    rank = lax.axis_index("ctx")
    core = dp % 2
    chip = dp // 2
    zl = rank // 4
    x = rank % 4
    owner = core == zl
    first_core = core == 0
    groups = lax.axis_size("ctx")
    batch, local, width = inputs.shape
    shard = w_qkv.shape[0]
    length = local * groups

    qkv_low = jnp.pad(w_qkv.astype(low), ((0, 0), (0, 2 * PART - QKVW)))
    qkv_half = lax.dynamic_slice_in_dim(qkv_low, PART * core, PART, 1)
    qkv_mine = lax.all_to_all(
        jnp.broadcast_to(qkv_half[None], (groups, shard, PART)), "ctx", 0, 0, tiled=True
    ).reshape(width, PART)
    qkv_theirs = send(qkv_mine, to_core)
    full_proj = lax.all_gather(w_proj.astype(low), "ctx", axis=0, tiled=True)
    full_gains = lax.all_gather(gains.astype(low), "ctx", axis=1, tiled=True)
    gain_one = full_gains[0].astype(jnp.float32)
    gain_two = full_gains[1].astype(jnp.float32)

    gate_low = lax.dynamic_slice_in_dim(w_expand, HALF * core, HALF, 1).astype(low)
    up_low = lax.dynamic_slice_in_dim(w_expand, FF + HALF * core, HALF, 1).astype(low)
    expand_low = jnp.concatenate([gate_low, up_low], axis=1)
    down_low = w_down.astype(low)
    expand_low, down_low, qkv_mine = lax.optimization_barrier((expand_low, down_low, qkv_mine))
    near = [expand_low] + [send(expand_low, to_x(k)) for k in (1, 2, 3)]
    far = [send(near[k], to_z(1 if k % 2 else -1)) for k in range(4)]
    half_expand = jnp.zeros((width, FF), low)
    for k in range(4):
        half_expand = lax.dynamic_update_slice(
            half_expand, near[k], (shard * (zl * 4 + (x ^ k)), 0)
        )
        half_expand = lax.dynamic_update_slice(
            half_expand, far[k], (shard * ((1 - zl) * 4 + (x ^ k)), 0)
        )
    near = [down_low] + [send(down_low, to_x_owner(k)) for k in (1, 2, 3)]
    far = [send(near[k], to_z_from(1 if k % 2 else -1, True)) for k in range(4)]
    half_down = jnp.zeros((HALF, width), low)
    for k in range(4):
        half_down = lax.dynamic_update_slice(
            half_down, jnp.where(owner, near[k], far[k]), (down_low.shape[0] * (x ^ k), 0)
        )

    every_pos = positions_of(span_order, length, local // 2)
    own_pos = lax.dynamic_slice_in_dim(every_pos, rank * local, local)
    cosine, sine = rope_tables(own_pos)
    bias = jnp.where(every_pos[:, None] <= own_pos[None, :], 0.0, masked_score)
    rows_in = inputs.reshape(local, width).astype(jnp.float32)
    inv_one = rms_scale(rows_in)
    normed_one = (rows_in * inv_one * gain_one).astype(low)
    mixed_mine = contract(normed_one, qkv_mine, 1, 0)
    mixed_theirs = contract(normed_one, qkv_theirs, 1, 0)
    mixed = jnp.concatenate(
        [
            jnp.where(first_core, mixed_mine, mixed_theirs),
            jnp.where(first_core, mixed_theirs, mixed_mine),
        ],
        axis=1,
    ).T
    kv_width = KV_HEADS * HEAD_DIM
    queries = mixed[:width].reshape(HEADS, HEAD_DIM, local)
    keys = mixed[width : width + kv_width].reshape(KV_HEADS, HEAD_DIM, local)
    values = mixed[width + kv_width : QKVW].reshape(KV_HEADS, HEAD_DIM, local)
    key_values = jnp.concatenate(
        [rotate(keys, cosine, sine).astype(low), values.astype(low)], axis=1
    )
    all_keys = lax.all_to_all(
        jnp.broadcast_to(key_values[None], (groups,) + key_values.shape), "ctx", 0, 0, tiled=True
    )
    query = (rotate(queries, cosine, sine).astype(low) * HEAD_DIM ** (-0.5)).reshape(width, local)
    attended, lse = attend(query, all_keys, bias)
    middle = rows_in + contract(attended, full_proj, 0, 0)
    inv_two = rms_scale(middle)
    normed_two = (middle * inv_two * gain_two).astype(low)

    back_rows = cotangent.reshape(local, width)
    both_back = jnp.concatenate([back_rows, send(back_rows, to_core)], axis=0)
    both_normed = jnp.concatenate([normed_two, send(normed_two, to_core)], axis=0)
    expanded = contract(both_normed, half_expand, 1, 0)
    gate = expanded[:, :HALF]
    upward = expanded[:, HALF:]
    hidden = (jax.nn.silu(gate) * upward).astype(low)
    fed = contract(hidden, half_down, 1, 0)
    fed_other = send(fed[local:].astype(low), to_core)
    output = (middle + fed[:local] + fed_other.astype(jnp.float32)).astype(low)
    grad_down = contract(hidden, both_back, 0, 0).astype(low)
    grad_hidden = contract(both_back, half_down, 1, 1)
    sigmoid = jax.nn.sigmoid(gate)
    grad_gate = grad_hidden * upward * sigmoid * (1.0 + gate * (1.0 - sigmoid))
    grad_up = grad_hidden * gate * sigmoid
    grad_expanded = jnp.concatenate([grad_gate, grad_up], axis=1).astype(low)
    grad_normed = contract(grad_expanded, half_expand, 1, 1)
    grad_expand = contract(both_normed, grad_expanded, 0, 0).astype(low)
    grad_other = send(grad_normed[local:].astype(low), to_core)
    grad_normed_two = grad_normed[:local] + grad_other.astype(jnp.float32)
    back_two, gain_grad_two = norm_back(grad_normed_two, middle, inv_two, gain_two)
    grad_middle = back_rows.astype(jnp.float32) + back_two
    middle_low = grad_middle.astype(low)
    grad_proj = contract(attended, middle_low, 1, 0).astype(low)
    grad_att = contract(full_proj, middle_low, 1, 1).astype(low)

    other = lax.dynamic_slice_in_dim(grad_expand, 480 * (1 - zl), 480, 0)
    kept = lax.dynamic_slice_in_dim(grad_expand, 480 * zl, 480, 0)
    came = jnp.concatenate([send(other[:, :HALF], to_z(1)), send(other[:, HALF:], to_z(-1))], axis=1)
    expand_sum = (kept.astype(jnp.float32) + came.astype(jnp.float32)).astype(low)
    expand_sum = reduce_direct(
        expand_sum.reshape(4, shard, FF), x, [(k, to_x(k)) for k in (1, 2, 3)]
    )
    chips = [(k, to_chip(k)) for k in range(1, 8)]
    expand_sum = reduce_direct(expand_sum.reshape(8, shard // 8, FF), chip, chips)
    expand_sum = gather_direct(expand_sum, chip, chips).reshape(shard, FF)
    expand_other = send(expand_sum, to_core)
    expand_one = jnp.where(first_core, expand_sum, expand_other)
    expand_two = jnp.where(first_core, expand_other, expand_sum)
    whole_expand = jnp.concatenate(
        [expand_one[:, :HALF], expand_two[:, :HALF], expand_one[:, HALF:], expand_two[:, HALF:]],
        axis=1,
    ).astype(jnp.float32)

    proj_kept = lax.dynamic_slice_in_dim(grad_proj, 480 * core, 480, 0)
    proj_sent = lax.dynamic_slice_in_dim(grad_proj, 480 * (1 - core), 480, 0)
    proj_sum = proj_kept.astype(jnp.float32) + send(proj_sent, to_core).astype(jnp.float32)
    tall = jnp.concatenate(
        [
            grad_down.reshape(4, 320, width),
            proj_sum.astype(low).reshape(4, shard, width),
            jnp.zeros((4, 8, width), low),
        ],
        axis=1,
    )
    came = jnp.concatenate(
        [send(tall[:2], to_z_from(1, False)), send(tall[2:], to_z_from(-1, False))], axis=0
    )
    tall = (tall.astype(jnp.float32) + came.astype(jnp.float32)).astype(low)
    tall = reduce_direct(tall, x, [(k, to_x_owner(k)) for k in (1, 2, 3)])
    chips_owner = [(k, to_chip_owner(k)) for k in range(1, 8)]
    tall = reduce_direct(tall.reshape(8, 56, width), chip, chips_owner)
    tall = gather_direct(tall, chip, chips_owner).reshape(448, width)
    tall = jnp.where(owner, tall, send(tall, to_core)).astype(jnp.float32)
    whole_down = tall[:320]
    whole_proj = tall[320:440]

    grad_query, key_terms = attend_back(query, all_keys, bias, grad_att, attended, lse)
    grad_keys = jnp.sum(
        lax.all_to_all(key_terms, "ctx", 0, 0, tiled=True).astype(jnp.float32), axis=0
    )
    grad_keys = jnp.transpose(grad_keys, (0, 2, 1))
    grad_mixed = jnp.concatenate(
        [
            rotate_back(grad_query.reshape(HEADS, HEAD_DIM, local), cosine, sine).reshape(
                width, local
            ),
            rotate_back(grad_keys[:, :HEAD_DIM], cosine, sine).reshape(kv_width, local),
            grad_keys[:, HEAD_DIM:].reshape(kv_width, local),
        ],
        axis=0,
    ).astype(low)
    mixed_one = grad_mixed[:PART]
    mixed_two = jnp.pad(grad_mixed[PART:], ((0, 2 * PART - QKVW), (0, 0)))
    grad_normed_one = contract(
        jnp.where(first_core, mixed_one, mixed_two), qkv_mine, 0, 1
    ) + contract(jnp.where(first_core, mixed_two, mixed_one), qkv_theirs, 0, 1)
    back_one, gain_grad_one = norm_back(grad_normed_one, rows_in, inv_one, gain_one)
    input_grad = (grad_middle + back_one).astype(low).reshape(batch, local, width)
    grad_qkv = contract(normed_one, grad_mixed, 0, 1)
    wide = jnp.concatenate(
        [
            grad_qkv,
            gain_grad_one[:, None],
            gain_grad_two[:, None],
            jnp.zeros((width, 2 * PART - QKVW - 2), jnp.float32),
        ],
        axis=1,
    ).astype(low)
    kept = lax.dynamic_slice_in_dim(wide, PART * core, PART, 1)
    sent = lax.dynamic_slice_in_dim(wide, PART * (1 - core), PART, 1)
    wide = (kept.astype(jnp.float32) + send(sent, to_core).astype(jnp.float32)).astype(low)
    wide = jnp.sum(
        lax.all_to_all(wide.reshape(groups, shard, PART), "ctx", 0, 0, tiled=True).astype(
            jnp.float32
        ),
        axis=0,
    ).astype(low)
    same_core = [[2 * c + k for c in range(8)] for k in range(2)]
    wide = jnp.sum(
        lax.all_to_all(
            jnp.broadcast_to(wide[None], (8, shard, PART)),
            "dp",
            0,
            0,
            axis_index_groups=same_core,
            tiled=True,
        ).astype(jnp.float32),
        axis=0,
    ).astype(low)
    wide_other = send(wide, to_core)
    wide = jnp.concatenate(
        [jnp.where(first_core, wide, wide_other), jnp.where(first_core, wide_other, wide)], axis=1
    ).astype(jnp.float32)
    whole_qkv = wide[:, :QKVW]
    whole_gains = wide[:, QKVW : QKVW + 2].T

    new_qkv, qkv_mean, qkv_square = adam_step(
        w_qkv, qkv_first, qkv_second, whole_qkv, 2.0 * D ** (-0.5), 0.1
    )
    new_proj, proj_mean, proj_square = adam_step(
        w_proj, proj_first, proj_second, whole_proj, 2.0 * (D // 8) ** (-0.5), 0.1
    )
    new_expand, expand_mean, expand_square = adam_step(
        w_expand, expand_first, expand_second, whole_expand, 2.0 * D ** (-0.5), 0.1
    )
    new_down, down_mean, down_square = adam_step(
        w_down, down_first, down_second, whole_down, 2.0 * FF ** (-0.5), 0.1
    )
    new_gains, gains_mean, gains_square = adam_step(
        gains, gains_first, gains_second, whole_gains, 1.0, 0.0
    )
    return (
        output.reshape(batch, local, width),
        input_grad,
        new_qkv,
        qkv_mean,
        qkv_square,
        new_proj,
        proj_mean,
        proj_square,
        new_expand,
        expand_mean,
        expand_square,
        new_down,
        down_mean,
        down_square,
        new_gains,
        gains_mean,
        gains_square,
    )


def solution(mesh):
    rows = P("dp", "ctx", None)
    owned = P("ctx", None)
    split = P(None, "ctx")
    return jax.shard_map(
        on_device,
        mesh=mesh,
        in_specs=(rows, rows, P()) + (owned,) * 12 + (split,) * 3,
        out_specs=(rows, rows) + (owned,) * 12 + (split,) * 3,
        check_vma=False,
    )
```

time: 1070 us -> 619 us (0.58)
  blocking collectives: 294 us -> 33.4 us
  waiting for transfers between devices: 364 us -> 132 us
  starting transfers between devices: 0.59 us -> 192 us
  matrix products: 144 us -> 34.6 us
  local copies, waits for them, and re-layouts: 154 us -> 86.3 us
  Pallas kernels: 0 us -> 45.4 us
  other arithmetic: 87.1 us -> 68.2 us
    all_gather x7 -> x1, waiting for transfers between devices: 309 us -> 0.02 us  [on_device(): full_proj = lax.all_gather(w_proj.astype(low), 'ctx', axis=0, tiled=True)]
    unnamed x2 -> x0, blocking collectives: 249 us -> none
    reshape x17 -> x2, local copies, waits for them, and re-layouts: 130 us -> 3.52 us  [the longest x1 2.11 us: on_device(): expand_sum = gather_direct(expand_sum, chip, chips).reshape(shard, FF)]
    ppermute x0 -> x62, starting transfers between devices: none -> 117 us  [send(): return lax.ppermute(value, ('dp', 'ctx'), pairs)]
    ppermute x0 -> x62, waiting for transfers between devices: none -> 117 us  [send(): return lax.ppermute(value, ('dp', 'ctx'), pairs)]
    dot_general x18 -> x14, matrix products: 144 us -> 34.6 us  [contract(): lax.dot_general(left, right, (((left_axis,), (right_axis,)), ((), ())), p...]
    all_to_all x0 -> x5, starting transfers between devices: none -> 74.5 us  [the longest x1 51.6 us: on_device(): lax.all_to_all(wide.reshape(groups, shard, PART), 'ctx', 0, 0, tiled=True)]
    unnamed x11 -> x1, waiting for transfers between devices: 54.5 us -> 0.02 us
  transfers between devices with their start and end apart: 10 -> 68, of which waited for: 8 -> 12; matrix products, arithmetic and copies ran while one was open for 22% -> 27% of each run, Pallas kernels for 0% -> 7%
where the time goes in v1:
time: 619 us; the launch traced here: 608 us
  starting transfers between devices  192 us (31%)
  waiting for transfers between devices  132 us (21%)
  local copies, waits for them, and re-layouts  86.3 us (14%)
  other arithmetic  68.2 us (11%)
  Pallas kernels  45.4 us (7%)
  matrix products  34.6 us (6%)
  blocking collectives  33.4 us (5%)
  between operations  15.9 us (3%)
    ppermute x62, starting transfers between devices, send(): return lax.ppermute(value, ('dp', 'ctx'), pairs)  117 us
    ppermute x62, waiting for transfers between devices, send(): return lax.ppermute(value, ('dp', 'ctx'), pairs)  117 us
    all_to_all x1, starting transfers between devices, on_device(): lax.all_to_all(wide.reshape(groups, shard, PART), 'ctx', 0, 0, tiled=True)  51.6 us
    dot_general x14, matrix products, contract(): lax.dot_general(left, right, (((left_axis,), (right_axis,)), ((), ())), p...  34.6 us
    all_gather x1, blocking collectives, on_device(): full_gains = lax.all_gather(gains.astype(low), 'ctx', axis=1, tiled=True)  33.4 us
    pallas_call x1, Pallas kernels, attend_back(): pl.pallas_call(attend_back_kernel, grid=(KV_HEADS,), out_shape=(jax.Shape...  26.7 us
    pallas_call x1, Pallas kernels, attend(): pl.pallas_call(attend_kernel, grid=(KV_HEADS,), out_shape=(jax.ShapeDtype...  18.7 us
    unnamed x131, local copies, waits for them, and re-layouts  18.2 us
  transfers between devices with their start and end apart: 68, of which 12 were waited for; matrix products, arithmetic and copies ran while one was open for 27% of the time, Pallas kernels for 7%

profile of v1, /device:TPU:1, one launch (start us, length us, event | category | flops | bytes accessed | tf_op | source)
XLA Modules:
  0.0 607.7 jit_solution(17947175054388504715)
XLA Ops:
  9.8 6.3 %all-to-all-start = ((bf16[8,120,896]{2,1,0:T(8,128)(2,1)}), bf16[8,120,896]{2,1,0:T(8,128)(2,1)S(1)}, u32[]{:S(2)}, u32[]{:S(2)}) async-start(bf16[8,120,896]{2,1,0:T(8,128)(2,1)} %broadcast_in_dim.145), calls=%async_computation | async-start | bytes 3440640 | tf_op jit(solution)/shard_map/all_to_all | solution.py:300
  17.0 33.4 %all-gather = bf16[8,120,2]{1,2,0:T(2,128)(2,1)S(1)} all-gather(bf16[1,120,2]{1,2,0:T(2,128)(2,1)S(1)} %convert_bitcast_fusion.1), channel_id=1, replica_groups=mesh['dp'=16,'ctx'=8] {'ctx'}, dimensions={0}, use_global_device_ids=true | all-gather | bytes 4320 | tf_op jit(solution)/shard_map/all_gather | solution.py:305
  58.0 6.0 collective-permute-start
  81.9 8.9 %collective-permute-done.2 = bf16[120,2560]{1,0:T(8,128)(2,1)S(1)} collective-permute-done((bf16[120,2560]{1,0:T(8,128)(2,1)}, bf16[120,2560]{1,0:T(8,128)(2,1)S(1)}, u32[]{:S(2)}, u32[]{:S(2)}) %collective-permute-start.2) | collective-permute-done | bytes 614432 | tf_op jit(solution)/shard_map/ppermute | solution.py:41
  90.8 6.8 %collective-permute-done.9 = bf16[320,960]{1,0:T(8,128)(2,1)S(1)} collective-permute-done((bf16[320,960]{1,0:T(8,128)(2,1)}, bf16[320,960]{1,0:T(8,128)(2,1)S(1)}, u32[]{:S(2)}, u32[]{:S(2)}) %collective-permute-start.9) | collective-permute-done | bytes 614432 | tf_op jit(solution)/shard_map/ppermute | solution.py:41
  108.3 11.4 %collective-permute-start.4 = (bf16[120,2560]{1,0:T(8,128)(2,1)}, bf16[120,2560]{1,0:T(8,128)(2,1)}, u32[]{:S(2)}, u32[]{:S(2)}) collective-permute-start(bf16[120,2560]{1,0:T(8,128)(2,1)} %copy-done.44), channel_id=1, source_target_pairs={{0,4},{1,5},{2,6},{3,7},{4,64},{5,65},{6,66},{7,67},{8,12},{9,13},... | collective-permute-start | bytes 1843208 | tf_op jit(solution)/shard_map/ppermute | solution.py:41
  125.0 3.9 all-to-all-start.1
  132.5 7.6 %collective-permute-start.17 = (bf16[256,960]{0,1:T(8,128)(2,1)}, bf16[256,960]{0,1:T(8,128)(2,1)}, u32[]{:S(2)}, u32[]{:S(2)}) collective-permute-start(bf16[256,960]{0,1:T(8,128)(2,1)} %bitcast.14), channel_id=1, source_target_pairs={{0,8},{1,9},{2,10},{3,11},{4,12},{5,13},{6,14},{7,15},{8,0},{9,1},... | collective-permute-start | bytes 1474568 | tf_op jit(solution)/shard_map/ppermute | solution.py:41
  145.0 25.2 %collective-permute-done.13 = bf16[320,960]{1,0:T(8,128)(2,1)S(1)} collective-permute-done((bf16[320,960]{1,0:T(8,128)(2,1)}, bf16[320,960]{1,0:T(8,128)(2,1)S(1)}, u32[]{:S(2)}, u32[]{:S(2)}) %collective-permute-start.13) | collective-permute-done | bytes 614432 | tf_op jit(solution)/shard_map/ppermute | solution.py:41
  173.2 6.6 %collective-permute-done.6 = bf16[120,2560]{1,0:T(8,128)(2,1)S(1)} collective-permute-done((bf16[120,2560]{1,0:T(8,128)(2,1)}, bf16[120,2560]{1,0:T(8,128)(2,1)S(1)}, u32[]{:S(2)}, u32[]{:S(2)}) %collective-permute-start.6) | collective-permute-done | bytes 614432 | tf_op jit(solution)/shard_map/ppermute | solution.py:41
  192.1 18.7 %attend.1 = (bf16[960,256]{1,0:T(8,128)(2,1)S(1)}, f32[15,1,256]{2,1,0:T(1,128)S(1)}) custom-call(bf16[960,256]{1,0:T(8,128)(2,1)S(1)} %bitcast.165, bf16[8,5,128,256]{3,2,1,0:T(8,128)(2,1)S(1)} %all-to-all-done.1.kv_ref, f32[2048,256]{1,0:T(8,128)S(1)} %copy-done.1), custom_call_target="tpu_custom_call" | custom-call | flops 8053063680 | bytes 8388608 | tf_op jit(solution)/shard_map/attend/pallas_call | solution.py:217
  217.2 5.0 fusion.35
  222.2 3.9 multiply_convert_fusion.1
  241.9 4.1 convolution_convert_fusion.1
  246.0 4.4 copy.160
  257.1 26.7 %attend_back.1 = (f32[960,256]{1,0:T(8,128)S(1)}, bf16[8,5,256,128]{3,2,1,0:T(8,128)(2,1)}) custom-call(bf16[960,256]{1,0:T(8,128)(2,1)S(1)} %bitcast.166, bf16[8,5,128,256]{3,2,1,0:T(8,128)(2,1)} %copy-done, f32[2048,256]{1,0:T(8,128)S(1)} %copy-done.2, bf16[960,256]{1,0:T(8,128)(2,1)S(1)} %fusion.10.do_ref, bf16[960,256]{1,0:T(8,128)(2,1)S(1)} %get-tuple-element.25.o_ref, ...), custom_call_target="tpu_custom_call" | custom-call | flops 20132659200 | bytes 8388608 | tf_op jit(solution)/shard_map/attend_back/pallas_call | solution.py:239
  283.8 4.9 all-to-all-start.2
  290.4 3.7 add_convert_fusion.1
  302.9 34.1 %collective-permute-done.44 = bf16[120,2560]{1,0:T(8,128)(2,1)S(1)} collective-permute-done((bf16[120,2560]{1,0:T(8,128)(2,1)S(1)}, bf16[120,2560]{1,0:T(8,128)(2,1)S(1)}, u32[]{:S(2)}, u32[]{:S(2)}) %collective-permute-start.44) | collective-permute-done | bytes 614432 | tf_op jit(solution)/shard_map/ppermute | solution.py:41
  337.0 12.8 %collective-permute-done.45 = bf16[120,2560]{1,0:T(8,128)(2,1)S(1)} collective-permute-done((bf16[120,2560]{1,0:T(8,128)(2,1)S(1)}, bf16[120,2560]{1,0:T(8,128)(2,1)S(1)}, u32[]{:S(2)}, u32[]{:S(2)}) %collective-permute-start.45) | collective-permute-done | bytes 614432 | tf_op jit(solution)/shard_map/ppermute | solution.py:41
  361.3 6.1 collective-permute-start.52
  378.3 3.7 collective-permute-start.22
  395.7 13.9 %collective-permute-done.57 = bf16[15,2560]{1,0:T(8,128)(2,1)S(1)} collective-permute-done((bf16[15,2560]{1,0:T(8,128)(2,1)S(1)}, bf16[15,2560]{1,0:T(8,128)(2,1)S(1)}, u32[]{:S(2)}, u32[]{:S(2)}) %collective-permute-start.57) | collective-permute-done | bytes 76832 | tf_op jit(solution)/shard_map/ppermute | solution.py:41
  428.1 4.5 add_convert_fusion
  441.0 3.7 fusion.22
  449.3 4.9 concatenate.67
  454.3 6.2 %collective-permute-start.19 = (bf16[960,896]{1,0:T(8,128)(2,1)S(1)}, bf16[960,896]{1,0:T(8,128)(2,1)S(1)}, u32[]{:S(2)}, u32[]{:S(2)}) collective-permute-start(bf16[960,896]{1,0:T(8,128)(2,1)S(1)} %constant_dynamic-slice_fusion.1), channel_id=1, source_target_pairs={{0,8},{1,9},{2,10},{3,11},{4,12},{5,13},{6,14},{7,15},{8,0},{9,1},... | collective-permute-start | bytes 5160968 | tf_op jit(solution)/shard_map/ppermute | solution.py:41
  480.0 51.6 %all-to-all-start.3 = ((bf16[8,120,896]{2,1,0:T(8,128)(2,1)}), bf16[8,120,896]{2,1,0:T(8,128)(2,1)S(1)}, u32[]{:S(2)}, u32[]{:S(2)}) async-start(bf16[8,120,896]{2,1,0:T(8,128)(2,1)} %bitcast.180), calls=%async_computation.3 | async-start | bytes 3440640 | tf_op jit(solution)/shard_map/all_to_all | solution.py:467
  541.2 12.2 %collective-permute-start.41 = (bf16[448,960]{1,0:T(8,128)(2,1)}, bf16[448,960]{1,0:T(8,128)(2,1)}, u32[]{:S(2)}, u32[]{:S(2)}) collective-permute-start(bf16[448,960]{1,0:T(8,128)(2,1)} %bitcast.47), channel_id=1, source_target_pairs={{0,8},{1,9},{2,10},{3,11},{4,12},{5,13},{6,14},{7,15},{8,0},{9,1},... | collective-permute-start | bytes 2580488 | tf_op jit(solution)/shard_map/ppermute | solution.py:41
  557.6 7.6 %all-to-all-start.4 = ((bf16[8,120,896]{2,1,0:T(8,128)(2,1)}), bf16[8,120,896]{2,1,0:T(8,128)(2,1)S(1)}, u32[]{:S(2)}, u32[]{:S(2)}) async-start(bf16[8,120,896]{2,1,0:T(8,128)(2,1)} %broadcast_in_dim.156), calls=%async_computation.4 | async-start | bytes 3440640 | tf_op jit(solution)/shard_map/all_to_all | solution.py:474
  565.3 6.2 %multiply_subtract_fusion = (f32[120,5120]{1,0:T(8,128)}, f32[120,5120]{1,0:T(8,128)}, f32[120,5120]{1,0:T(8,128)}) fusion(f32[120,5120]{1,0:T(8,128)} %param.27, bf16[120,1280]{1,0:T(8,128)(2,1)S(1)} %copy-done.36, bf16[120,1280]{1,0:T(8,128)(2,1)S(1)} %copy-done.35, bf16[120,1280]{1,0:T(8,128)(2,1)S(1)} %copy-done.37, bf16[120,1280]{1,0:T(8,128)(2,1)S(1)} %copy-done.34, ...), kind=kLoop, calls=%fused_computation.17 | loop fusion | flops 14131200 | bytes 15974400 | tf_op jit(solution)/shard_map/sub | solution.py:262
  577.7 12.1 %all-to-all-done.4 = bf16[8,120,896]{2,1,0:T(8,128)(2,1)S(1)} async-done(((bf16[8,120,896]{2,1,0:T(8,128)(2,1)}), bf16[8,120,896]{2,1,0:T(8,128)(2,1)S(1)}, u32[]{:S(2)}, u32[]{:S(2)}) %all-to-all-start.4) | async-done | bytes 1720352 | tf_op jit(solution)/shard_map/all_to_all | solution.py:474
  (379 shorter events, 224.5 us)
Async XLA Ops:
  9.8 48.2 %all-to-all-start = ((bf16[8,120,896]{2,1,0:T(8,128)(2,1)}), bf16[8,120,896]{2,1,0:T(8,128)(2,1)S(1)}, u32[]{:S(2)}, u32[]{:S(2)}) async-start(bf16[8,120,896]{2,1,0:T(8,128)(2,1)} %broadcast_in_dim.145), calls=%async_computation | async-start | bytes 3440640 | tf_op jit(solution)/shard_map/all_to_all | solution.py:300
  16.1 194.6 %all-gather.3.cloned.1.call-start = ((), (), s32[]{:S(2)}) async-start(), calls=%async_computation.5 | async-start | bytes 2211840 | tf_op jit(solution)/shard_map/all_gather | solution.py:304
  58.0 45.8 %collective-permute-start = (bf16[960,896]{1,0:T(8,128)(2,1)S(1)}, bf16[960,896]{1,0:T(8,128)(2,1)}, u32[]{:S(2)}, u32[]{:S(2)}) collective-permute-start(bf16[960,896]{1,0:T(8,128)(2,1)S(1)} %bitcast.171), channel_id=1, source_target_pairs={{0,8},{1,9},{2,10},{3,11},{4,12},{5,13},{6,14},{7,15},{8,0},{9,1},... | collective-permute-start | bytes 5160968 | tf_op jit(solution)/shard_map/ppermute | solution.py:41
  77.2 55.3 %collective-permute-start.5 = (bf16[120,2560]{1,0:T(8,128)(2,1)}, bf16[120,2560]{1,0:T(8,128)(2,1)}, u32[]{:S(2)}, u32[]{:S(2)}) collective-permute-start(bf16[120,2560]{1,0:T(8,128)(2,1)} %pad_maximum_fusion.10), channel_id=1, source_target_pairs={{0,2},{1,3},{2,0},{3,1},{4,6},{5,7},{6,4},{7,5},{8,10},{9,11},{10,... | collective-permute-start | bytes 1843208 | tf_op jit(solution)/shard_map/ppermute | solution.py:41
  90.8 49.3 %collective-permute-start.7 = (bf16[120,2560]{1,0:T(8,128)(2,1)}, bf16[120,2560]{1,0:T(8,128)(2,1)}, u32[]{:S(2)}, u32[]{:S(2)}) collective-permute-start(bf16[120,2560]{1,0:T(8,128)(2,1)} %pad_maximum_fusion.10), channel_id=1, source_target_pairs={{0,3},{1,2},{2,1},{3,0},{4,7},{5,6},{6,5},{7,4},{8,11},{9,10},{10,... | collective-permute-start | bytes 1843208 | tf_op jit(solution)/shard_map/ppermute | solution.py:41
  101.8 38.3 %collective-permute-start.14 = (bf16[320,960]{1,0:T(8,128)(2,1)}, bf16[320,960]{1,0:T(8,128)(2,1)}, u32[]{:S(2)}, u32[]{:S(2)}) collective-permute-start(bf16[320,960]{1,0:T(8,128)(2,1)} %convert_element_type.243), channel_id=1, source_target_pairs={{0,3},{1,2},{2,1},{3,0},{12,15},{13,14},{14,13},{15,12},{16,19},{1... | collective-permute-start | bytes 1843208 | tf_op jit(solution)/shard_map/ppermute | solution.py:41
  103.7 25.2 %collective-permute-start.11 = (bf16[320,960]{1,0:T(8,128)(2,1)}, bf16[320,960]{1,0:T(8,128)(2,1)}, u32[]{:S(2)}, u32[]{:S(2)}) collective-permute-start(bf16[320,960]{1,0:T(8,128)(2,1)} %collective-permute-done.10), channel_id=1, source_target_pairs={{0,4},{1,5},{2,6},{3,7},{12,72},{13,73},{14,74},{15,75},{16,20},{1... | collective-permute-start | bytes 1843208 | tf_op jit(solution)/shard_map/ppermute | solution.py:41
  108.3 33.2 %collective-permute-start.4 = (bf16[120,2560]{1,0:T(8,128)(2,1)}, bf16[120,2560]{1,0:T(8,128)(2,1)}, u32[]{:S(2)}, u32[]{:S(2)}) collective-permute-start(bf16[120,2560]{1,0:T(8,128)(2,1)} %copy-done.44), channel_id=1, source_target_pairs={{0,4},{1,5},{2,6},{3,7},{4,64},{5,65},{6,66},{7,67},{8,12},{9,13},... | collective-permute-start | bytes 1843208 | tf_op jit(solution)/shard_map/ppermute | solution.py:41
  125.0 63.5 %all-to-all-start.1 = ((bf16[8,5,128,256]{3,2,1,0:T(8,128)(2,1)}), bf16[8,5,128,256]{3,2,1,0:T(8,128)(2,1)S(1)}, u32[]{:S(2)}, u32[]{:S(2)}) async-start(bf16[8,5,128,256]{3,2,1,0:T(8,128)(2,1)} %broadcast_in_dim.148), calls=%async_computation.1 | async-start | bytes 5242880 | tf_op jit(solution)/shard_map/all_to_all | solution.py:355
  128.9 41.2 %collective-permute-start.13 = (bf16[320,960]{1,0:T(8,128)(2,1)}, bf16[320,960]{1,0:T(8,128)(2,1)S(1)}, u32[]{:S(2)}, u32[]{:S(2)}) collective-permute-start(bf16[320,960]{1,0:T(8,128)(2,1)} %collective-permute-done.12), channel_id=1, source_target_pairs={{0,68},{1,69},{2,70},{3,71},{12,8},{13,9},{14,10},{15,11},{16,84},... | collective-permute-start | bytes 1843208 | tf_op jit(solution)/shard_map/ppermute | solution.py:41
  132.5 89.8 %collective-permute-start.17 = (bf16[256,960]{0,1:T(8,128)(2,1)}, bf16[256,960]{0,1:T(8,128)(2,1)}, u32[]{:S(2)}, u32[]{:S(2)}) collective-permute-start(bf16[256,960]{0,1:T(8,128)(2,1)} %bitcast.14), channel_id=1, source_target_pairs={{0,8},{1,9},{2,10},{3,11},{4,12},{5,13},{6,14},{7,15},{8,0},{9,1},... | collective-permute-start | bytes 1474568 | tf_op jit(solution)/shard_map/ppermute | solution.py:41
  140.0 39.8 %collective-permute-start.6 = (bf16[120,2560]{1,0:T(8,128)(2,1)}, bf16[120,2560]{1,0:T(8,128)(2,1)S(1)}, u32[]{:S(2)}, u32[]{:S(2)}) collective-permute-start(bf16[120,2560]{1,0:T(8,128)(2,1)} %collective-permute-done.5), channel_id=1, source_target_pairs={{0,68},{1,69},{2,70},{3,71},{4,0},{5,1},{6,2},{7,3},{8,76},{9,77},... | collective-permute-start | bytes 1843208 | tf_op jit(solution)/shard_map/ppermute | solution.py:41
  140.0 75.2 %collective-permute-start.8 = (bf16[120,2560]{1,0:T(8,128)(2,1)}, bf16[120,2560]{1,0:T(8,128)(2,1)}, u32[]{:S(2)}, u32[]{:S(2)}) collective-permute-start(bf16[120,2560]{1,0:T(8,128)(2,1)} %collective-permute-done.7), channel_id=1, source_target_pairs={{0,4},{1,5},{2,6},{3,7},{4,64},{5,65},{6,66},{7,67},{8,12},{9,13},... | collective-permute-start | bytes 1843208 | tf_op jit(solution)/shard_map/ppermute | solution.py:41
  141.5 72.3 %collective-permute-start.15 = (bf16[320,960]{1,0:T(8,128)(2,1)}, bf16[320,960]{1,0:T(8,128)(2,1)}, u32[]{:S(2)}, u32[]{:S(2)}) collective-permute-start(bf16[320,960]{1,0:T(8,128)(2,1)} %collective-permute-done.14), channel_id=1, source_target_pairs={{0,4},{1,5},{2,6},{3,7},{12,72},{13,73},{14,74},{15,75},{16,20},{1... | collective-permute-start | bytes 1843208 | tf_op jit(solution)/shard_map/ppermute | solution.py:41
  239.2 51.1 %collective-permute-start.42 = (bf16[480,1280]{1,0:T(8,128)(2,1)}, bf16[480,1280]{1,0:T(8,128)(2,1)}, u32[]{:S(2)}, u32[]{:S(2)}) collective-permute-start(bf16[480,1280]{1,0:T(8,128)(2,1)} %get-tuple-element.161), channel_id=1, source_target_pairs={{0,4},{1,5},{2,6},{3,7},{4,64},{5,65},{6,66},{7,67},{8,12},{9,13},... | collective-permute-start | bytes 3686408 | tf_op jit(solution)/shard_map/ppermute | solution.py:41
  239.2 51.1 %collective-permute-start.43 = (bf16[480,1280]{1,0:T(8,128)(2,1)}, bf16[480,1280]{1,0:T(8,128)(2,1)}, u32[]{:S(2)}, u32[]{:S(2)}) collective-permute-start(bf16[480,1280]{1,0:T(8,128)(2,1)} %get-tuple-element.162), channel_id=1, source_target_pairs={{0,68},{1,69},{2,70},{3,71},{4,0},{5,1},{6,2},{7,3},{8,76},{9,77},... | collective-permute-start | bytes 3686408 | tf_op jit(solution)/shard_map/ppermute | solution.py:41
  283.8 135.7 %all-to-all-start.2 = ((bf16[8,5,256,128]{3,2,1,0:T(8,128)(2,1)}), bf16[8,5,256,128]{3,2,1,0:T(8,128)(2,1)}, u32[]{:S(2)}, u32[]{:S(2)}) async-start(bf16[8,5,256,128]{3,2,1,0:T(8,128)(2,1)} %get-tuple-element.30), calls=%async_computation.2 | async-start | bytes 5242880 | tf_op jit(solution)/shard_map/all_to_all | solution.py:433
  294.3 42.8 %collective-permute-start.44 = (bf16[120,2560]{1,0:T(8,128)(2,1)S(1)}, bf16[120,2560]{1,0:T(8,128)(2,1)S(1)}, u32[]{:S(2)}, u32[]{:S(2)}) collective-permute-start(bf16[120,2560]{1,0:T(8,128)(2,1)S(1)} %get-tuple-element.168), channel_id=1, source_target_pairs={{0,1},{1,0},{2,3},{3,2},{4,5},{5,4},{6,7},{7,6},{8,9},{9,8},{10,11... | collective-permute-start | bytes 1843208 | tf_op jit(solution)/shard_map/ppermute | solution.py:41
  295.8 54.0 %collective-permute-start.45 = (bf16[120,2560]{1,0:T(8,128)(2,1)S(1)}, bf16[120,2560]{1,0:T(8,128)(2,1)S(1)}, u32[]{:S(2)}, u32[]{:S(2)}) collective-permute-start(bf16[120,2560]{1,0:T(8,128)(2,1)S(1)} %get-tuple-element.170), channel_id=1, source_target_pairs={{0,2},{1,3},{2,0},{3,1},{4,6},{5,7},{6,4},{7,5},{8,10},{9,11},{10,... | collective-permute-start | bytes 1843208 | tf_op jit(solution)/shard_map/ppermute | solution.py:41
  298.2 51.6 %collective-permute-start.46 = (bf16[120,2560]{1,0:T(8,128)(2,1)S(1)}, bf16[120,2560]{1,0:T(8,128)(2,1)S(1)}, u32[]{:S(2)}, u32[]{:S(2)}) collective-permute-start(bf16[120,2560]{1,0:T(8,128)(2,1)S(1)} %get-tuple-element.169), channel_id=1, source_target_pairs={{0,3},{1,2},{2,1},{3,0},{4,7},{5,6},{6,5},{7,4},{8,11},{9,10},{10,... | collective-permute-start | bytes 1843208 | tf_op jit(solution)/shard_map/ppermute | solution.py:41
  299.3 57.3 %collective-permute-start.21 = (bf16[480,960]{1,0:T(8,128)(2,1)}, bf16[480,960]{1,0:T(8,128)(2,1)}, u32[]{:S(2)}, u32[]{:S(2)}) collective-permute-start(bf16[480,960]{1,0:T(8,128)(2,1)} %constant_dynamic-slice_fusion), channel_id=1, source_target_pairs={{0,8},{1,9},{2,10},{3,11},{4,12},{5,13},{6,14},{7,15},{8,0},{9,1},... | collective-permute-start | bytes 2764808 | tf_op jit(solution)/shard_map/ppermute | solution.py:41
  378.3 49.7 %collective-permute-start.22 = (bf16[2,448,960]{2,1,0:T(8,128)(2,1)}, bf16[2,448,960]{2,1,0:T(8,128)(2,1)}, u32[]{:S(2)}, u32[]{:S(2)}) collective-permute-start(bf16[2,448,960]{2,1,0:T(8,128)(2,1)} %get-tuple-element.166), channel_id=1, source_target_pairs={{4,64},{5,65},{6,66},{7,67},{8,12},{9,13},{10,14},{11,15},{20,80},... | collective-permute-start | bytes 5160968 | tf_op jit(solution)/shard_map/ppermute | solution.py:41
  382.0 46.0 %collective-permute-start.23 = (bf16[2,448,960]{2,1,0:T(8,128)(2,1)}, bf16[2,448,960]{2,1,0:T(8,128)(2,1)}, u32[]{:S(2)}, u32[]{:S(2)}) collective-permute-start(bf16[2,448,960]{2,1,0:T(8,128)(2,1)} %get-tuple-element.167), channel_id=1, source_target_pairs={{4,0},{5,1},{6,2},{7,3},{8,76},{9,77},{10,78},{11,79},{20,16},{21,... | collective-permute-start | bytes 5160968 | tf_op jit(solution)/shard_map/ppermute | solution.py:41
  419.3 46.2 %collective-permute-start.61 = (bf16[120,2560]{1,0:T(8,128)(2,1)}, bf16[120,2560]{1,0:T(8,128)(2,1)}, u32[]{:S(2)}, u32[]{:S(2)}) collective-permute-start(bf16[120,2560]{1,0:T(8,128)(2,1)} %reshape.244), channel_id=1, source_target_pairs={{0,8},{1,9},{2,10},{3,11},{4,12},{5,13},{6,14},{7,15},{8,0},{9,1},... | collective-permute-start | bytes 1843208 | tf_op jit(solution)/shard_map/ppermute | solution.py:41
  472.5 59.2 %collective-permute-start.34 = (bf16[56,960]{1,0:T(8,128)(2,1)}, bf16[56,960]{1,0:T(8,128)(2,1)}, u32[]{:S(2)}, u32[]{:S(2)}) collective-permute-start(bf16[56,960]{1,0:T(8,128)(2,1)} %get-tuple-element.152), channel_id=1, source_target_pairs={{0,16},{1,17},{2,18},{3,19},{12,28},{13,29},{14,30},{15,31},{16,0}... | collective-permute-start | bytes 322568 | tf_op jit(solution)/shard_map/ppermute | solution.py:41
  473.8 60.1 %collective-permute-start.35 = (bf16[56,960]{1,0:T(8,128)(2,1)}, bf16[56,960]{1,0:T(8,128)(2,1)}, u32[]{:S(2)}, u32[]{:S(2)}) collective-permute-start(bf16[56,960]{1,0:T(8,128)(2,1)} %get-tuple-element.152), channel_id=1, source_target_pairs={{0,32},{1,33},{2,34},{3,35},{12,44},{13,45},{14,46},{15,47},{16,48... | collective-permute-start | bytes 322568 | tf_op jit(solution)/shard_map/ppermute | solution.py:41
  475.1 61.0 %collective-permute-start.36 = (bf16[56,960]{1,0:T(8,128)(2,1)}, bf16[56,960]{1,0:T(8,128)(2,1)}, u32[]{:S(2)}, u32[]{:S(2)}) collective-permute-start(bf16[56,960]{1,0:T(8,128)(2,1)} %get-tuple-element.152), channel_id=1, source_target_pairs={{0,48},{1,49},{2,50},{3,51},{12,60},{13,61},{14,62},{15,63},{16,32... | collective-permute-start | bytes 322568 | tf_op jit(solution)/shard_map/ppermute | solution.py:41
  476.3 61.3 %collective-permute-start.37 = (bf16[56,960]{1,0:T(8,128)(2,1)}, bf16[56,960]{1,0:T(8,128)(2,1)S(1)}, u32[]{:S(2)}, u32[]{:S(2)}) collective-permute-start(bf16[56,960]{1,0:T(8,128)(2,1)} %get-tuple-element.152), channel_id=1, source_target_pairs={{0,64},{1,65},{2,66},{3,67},{12,76},{13,77},{14,78},{15,79},{16,80... | collective-permute-start | bytes 322568 | tf_op jit(solution)/shard_map/ppermute | solution.py:41
  477.0 61.3 %collective-permute-start.38 = (bf16[56,960]{1,0:T(8,128)(2,1)}, bf16[56,960]{1,0:T(8,128)(2,1)}, u32[]{:S(2)}, u32[]{:S(2)}) collective-permute-start(bf16[56,960]{1,0:T(8,128)(2,1)} %get-tuple-element.152), channel_id=1, source_target_pairs={{0,80},{1,81},{2,82},{3,83},{12,92},{13,93},{14,94},{15,95},{16,64... | collective-permute-start | bytes 322568 | tf_op jit(solution)/shard_map/ppermute | solution.py:41
  480.0 76.0 %all-to-all-start.3 = ((bf16[8,120,896]{2,1,0:T(8,128)(2,1)}), bf16[8,120,896]{2,1,0:T(8,128)(2,1)S(1)}, u32[]{:S(2)}, u32[]{:S(2)}) async-start(bf16[8,120,896]{2,1,0:T(8,128)(2,1)} %bitcast.180), calls=%async_computation.3 | async-start | bytes 3440640 | tf_op jit(solution)/shard_map/all_to_all | solution.py:467
  541.2 31.5 %collective-permute-start.41 = (bf16[448,960]{1,0:T(8,128)(2,1)}, bf16[448,960]{1,0:T(8,128)(2,1)}, u32[]{:S(2)}, u32[]{:S(2)}) collective-permute-start(bf16[448,960]{1,0:T(8,128)(2,1)} %bitcast.47), channel_id=1, source_target_pairs={{0,8},{1,9},{2,10},{3,11},{4,12},{5,13},{6,14},{7,15},{8,0},{9,1},... | collective-permute-start | bytes 2580488 | tf_op jit(solution)/shard_map/ppermute | solution.py:41
  557.6 32.2 %all-to-all-start.4 = ((bf16[8,120,896]{2,1,0:T(8,128)(2,1)}), bf16[8,120,896]{2,1,0:T(8,128)(2,1)S(1)}, u32[]{:S(2)}, u32[]{:S(2)}) async-start(bf16[8,120,896]{2,1,0:T(8,128)(2,1)} %broadcast_in_dim.156), calls=%async_computation.4 | async-start | bytes 3440640 | tf_op jit(solution)/shard_map/all_to_all | solution.py:474
  (97 other events, 936.4 us)
Sparse Core Ops, SparseCore 0:
  19.2 43.1 all-gather.2

commit v2 on v1

v2 whole, which is shorter than its diff:
```python
import jax
import jax.numpy as jnp
from jax import lax
from jax.experimental import pallas as pl
from jax.experimental.pallas import tpu as pltpu
from jax.sharding import PartitionSpec as P

D = 960
HEADS = 15
KV_HEADS = 5
GROUP = HEADS // KV_HEADS
HEAD_DIM = 64
FF = 2560
STEP = 10
HALF = FF // 2
QKVW = D + 2 * KV_HEADS * HEAD_DIM


eps = 1e-05
rope_base = 100000.0
beta_first = 0.9
beta_second = 0.95
adam_eps = 1e-08
masked_score = -1e30
low = jnp.bfloat16


AXES = ("zh", "y", "core", "zl", "x")
CHIPS = ("zh", "y")
CTX = ("zl", "x")


def swap_cores(value):
    return lax.ppermute(value, "core", [(0, 1), (1, 0)])


def exchange(stack, axes):
    return lax.all_to_all(stack, axes, 0, 0, tiled=True)


def spread(piece, axes, count):
    return exchange(jnp.broadcast_to(piece[None], (count,) + piece.shape), axes)


def total(stack):
    return jnp.sum(stack.astype(jnp.float32), axis=0).astype(low)


def ordered(core, mine, theirs):
    first = core == 0
    return jnp.where(first, mine, theirs), jnp.where(first, theirs, mine)


def rope_tables(positions):
    halfway = HEAD_DIM // 2
    freqs = rope_base ** (-(jnp.arange(halfway, dtype=jnp.float32) * 2.0) / HEAD_DIM)
    angles = freqs[:, None] * positions.astype(jnp.float32)[None, :]
    return (jnp.cos(angles), jnp.sin(angles))


def rotate(field, cosine, sine):
    halfway = HEAD_DIM // 2
    first = field[:, :halfway]
    second = field[:, halfway:]
    return jnp.concatenate(
        [first * cosine - second * sine, second * cosine + first * sine], axis=1
    )


def rotate_back(field, cosine, sine):
    halfway = HEAD_DIM // 2
    first = field[:, :halfway]
    second = field[:, halfway:]
    return jnp.concatenate(
        [first * cosine + second * sine, second * cosine - first * sine], axis=1
    )


def positions_of(order, count, span):
    rows = jnp.arange(count, dtype=jnp.int32)
    slots = rows // span
    labels = jnp.arange(order.shape[0], dtype=jnp.int32)
    picked = jnp.sum(jnp.where(slots[:, None] == labels[None, :], order[None, :], 0), axis=1)
    return picked * span + rows % span


def rms_scale(rows):
    return lax.rsqrt(jnp.mean(rows * rows, axis=-1, keepdims=True) + eps)


def contract(left, right, left_axis, right_axis):
    return lax.dot_general(
        left,
        right,
        (((left_axis,), (right_axis,)), ((), ())),
        preferred_element_type=jnp.float32,
    )


def norm_back(grad_normed, rows, inverse, gain):
    scaled = grad_normed * gain
    inner = jnp.mean(scaled * rows, axis=-1, keepdims=True)
    rows_grad = inverse * (scaled - rows * inverse * inverse * inner)
    gain_grad = jnp.sum(grad_normed * rows * inverse, axis=0)
    return (rows_grad, gain_grad)


def load_keys(kv_ref):
    columns = jnp.concatenate([kv_ref[j, 0] for j in range(kv_ref.shape[0])], axis=1)
    return columns, columns.T


def attend_kernel(q_ref, kv_ref, bias_ref, o_ref, lse_ref):
    columns, rows = load_keys(kv_ref)
    bias = bias_ref[...]
    blank = jnp.zeros((HEAD_DIM, q_ref.shape[1]), low)
    for h in range(GROUP):
        part = pl.ds(h * HEAD_DIM, HEAD_DIM)
        query = jnp.concatenate([q_ref[part, :], blank], axis=0)
        scores = contract(rows, query, 1, 0) + bias
        top = jnp.max(scores, axis=0, keepdims=True)
        weights = jnp.exp(scores - top)
        total = jnp.sum(weights, axis=0, keepdims=True)
        mixed = contract(columns[HEAD_DIM:], weights.astype(low), 1, 0)
        o_ref[part, :] = (mixed / total).astype(low)
        lse_ref[h] = top + jnp.log(total)


def attend_back_kernel(q_ref, kv_ref, bias_ref, do_ref, o_ref, lse_ref, dq_ref, dkv_ref):
    columns, rows = load_keys(kv_ref)
    bias = bias_ref[...]
    local = q_ref.shape[1]
    blank = jnp.zeros((HEAD_DIM, local), low)
    terms = None
    for h in range(GROUP):
        part = pl.ds(h * HEAD_DIM, HEAD_DIM)
        query = jnp.concatenate([q_ref[part, :], blank], axis=0)
        back = jnp.concatenate([blank, do_ref[part, :]], axis=0)
        delta = jnp.sum(
            do_ref[part, :].astype(jnp.float32) * o_ref[part, :].astype(jnp.float32),
            axis=0,
            keepdims=True,
        )
        weights = jnp.exp(contract(rows, query, 1, 0) + bias - lse_ref[h])
        grad = contract(rows, back, 1, 0)
        scores = (weights * (grad - delta)).astype(low)
        dq_ref[part, :] = contract(columns[:HEAD_DIM], scores, 1, 0) * HEAD_DIM ** (-0.5)
        term = contract(scores, query, 1, 1) + contract(weights.astype(low), back, 1, 1)
        terms = term if terms is None else terms + term
    for j in range(dkv_ref.shape[0]):
        dkv_ref[j, 0] = terms[j * local : (j + 1) * local].astype(low)


def attention_specs(chunks, local):
    wide = GROUP * HEAD_DIM
    heads = pl.BlockSpec((wide, local), lambda g: (g, 0))
    keys = pl.BlockSpec((chunks, 1, 2 * HEAD_DIM, local), lambda g: (0, g, 0, 0))
    bias = pl.BlockSpec((chunks * local, local), lambda g: (0, 0))
    sums = pl.BlockSpec((GROUP, 1, local), lambda g: (g, 0, 0))
    return heads, keys, bias, sums


def attend(query, keys, bias):
    chunks, _, _, local = keys.shape
    heads, kv, mask, sums = attention_specs(chunks, local)
    flops = 4 * HEADS * local * chunks * local * HEAD_DIM
    return pl.pallas_call(
        attend_kernel,
        grid=(KV_HEADS,),
        out_shape=(
            jax.ShapeDtypeStruct((D, local), low),
            jax.ShapeDtypeStruct((HEADS, 1, local), jnp.float32),
        ),
        in_specs=[heads, kv, mask],
        out_specs=(heads, sums),
        compiler_params=pltpu.CompilerParams(vmem_limit_bytes=48 * 1024 * 1024),
        cost_estimate=pl.CostEstimate(
            flops=4 * flops, bytes_accessed=8 * 1024 * 1024, transcendentals=0
        ),
        name="attend",
    )(query, keys, bias)


def attend_back(query, keys, bias, back, out, lse):
    chunks, _, _, local = keys.shape
    heads, kv, mask, sums = attention_specs(chunks, local)
    grads = pl.BlockSpec((chunks, 1, local, 2 * HEAD_DIM), lambda g: (0, g, 0, 0))
    flops = 10 * HEADS * local * chunks * local * HEAD_DIM
    return pl.pallas_call(
        attend_back_kernel,
        grid=(KV_HEADS,),
        out_shape=(
            jax.ShapeDtypeStruct((D, local), jnp.float32),
            jax.ShapeDtypeStruct((chunks, KV_HEADS, local, 2 * HEAD_DIM), low),
        ),
        in_specs=[heads, kv, mask, heads, heads, sums],
        out_specs=(heads, grads),
        compiler_params=pltpu.CompilerParams(vmem_limit_bytes=48 * 1024 * 1024),
        cost_estimate=pl.CostEstimate(
            flops=4 * flops, bytes_accessed=8 * 1024 * 1024, transcendentals=0
        ),
        name="attend_back",
    )(query, keys, bias, back, out, lse)


def adam_step(master, first, second, grad, rate, decay):
    new_first = beta_first * first + (1.0 - beta_first) * grad
    new_second = beta_second * second + (1.0 - beta_second) * grad * grad
    fix_one = 1.0 - beta_first**STEP
    fix_two = 1.0 - beta_second**STEP
    update = new_first / fix_one / (jnp.sqrt(new_second / fix_two) + adam_eps) + decay * master
    return (master - rate * update, new_first, new_second)


def on_device(
    inputs,
    cotangent,
    span_order,
    w_qkv,
    qkv_first,
    qkv_second,
    w_proj,
    proj_first,
    proj_second,
    w_expand,
    expand_first,
    expand_second,
    w_down,
    down_first,
    down_second,
    gains,
    gains_first,
    gains_second,
):
    core = lax.axis_index("core")
    rank = lax.axis_index(CTX)
    first_core = core == 0
    groups = 8
    batch, local, width = inputs.shape
    shard = w_qkv.shape[0]
    hidden_shard = w_down.shape[0] // 2
    length = local * groups
    kv_width = KV_HEADS * HEAD_DIM

    full_gains = spread(gains.astype(low), CTX, groups)
    full_gains = jnp.transpose(full_gains, (1, 0, 2)).reshape(2, width).astype(jnp.float32)
    gain_one = full_gains[0]
    gain_two = full_gains[1]

    qkv_low = w_qkv.astype(low)
    proj_low = w_proj.astype(low)
    half_low = jnp.concatenate(
        [
            jnp.where(first_core, qkv_low[:, : QKVW // 2], qkv_low[:, QKVW // 2 :]),
            jnp.where(first_core, proj_low[:, : D // 2], proj_low[:, D // 2 :]),
        ],
        axis=1,
    )
    mine = spread(half_low, CTX, groups).reshape(width, HALF)
    theirs = swap_cores(mine)

    down_low = lax.dynamic_slice_in_dim(w_down, hidden_shard * core, hidden_shard, 0).astype(low)
    half_down = lax.all_gather(down_low, CTX, axis=0, tiled=True)
    expand_low = w_expand.astype(low)
    expand_low = jnp.concatenate(
        [
            jnp.where(
                first_core,
                expand_low[:, k * hidden_shard : (k + 1) * hidden_shard],
                expand_low[:, (k + 1) * hidden_shard : (k + 2) * hidden_shard],
            )
            for k in range(0, 32, 2)
        ],
        axis=1,
    )
    half_expand = lax.all_gather(expand_low, CTX, axis=0, tiled=True)

    every_pos = positions_of(span_order, length, local // 2)
    own_pos = lax.dynamic_slice_in_dim(every_pos, rank * local, local)
    cosine, sine = rope_tables(own_pos)
    bias = jnp.where(every_pos[:, None] <= own_pos[None, :], 0.0, masked_score)
    rows_in = inputs.reshape(local, width).astype(jnp.float32)
    inv_one = rms_scale(rows_in)
    normed_one = (rows_in * inv_one * gain_one).astype(low)
    mixed = jnp.concatenate(
        ordered(
            core,
            contract(normed_one, mine[:, : QKVW // 2], 1, 0),
            contract(normed_one, theirs[:, : QKVW // 2], 1, 0),
        ),
        axis=1,
    ).T
    queries = mixed[:width].reshape(HEADS, HEAD_DIM, local)
    keys = mixed[width : width + kv_width].reshape(KV_HEADS, HEAD_DIM, local)
    values = mixed[width + kv_width :].reshape(KV_HEADS, HEAD_DIM, local)
    key_values = jnp.concatenate(
        [rotate(keys, cosine, sine).astype(low), values.astype(low)], axis=1
    )
    all_keys = spread(key_values, CTX, groups)
    query = (rotate(queries, cosine, sine).astype(low) * HEAD_DIM ** (-0.5)).reshape(width, local)
    attended, lse = attend(query, all_keys, bias)
    proj_one, proj_two = mine[:, QKVW // 2 :], theirs[:, QKVW // 2 :]
    mixed_out = jnp.concatenate(
        ordered(core, contract(attended, proj_one, 0, 0), contract(attended, proj_two, 0, 0)),
        axis=1,
    )
    middle = rows_in + mixed_out
    inv_two = rms_scale(middle)
    normed_two = (middle * inv_two * gain_two).astype(low)

    back_rows = cotangent.reshape(local, width)
    both_back = jnp.concatenate([back_rows, swap_cores(back_rows)], axis=0)
    both_normed = jnp.concatenate([normed_two, swap_cores(normed_two)], axis=0)
    expanded = contract(both_normed, half_expand, 1, 0)
    gate = expanded[:, :HALF]
    upward = expanded[:, HALF:]
    hidden = (jax.nn.silu(gate) * upward).astype(low)
    fed = contract(hidden, half_down, 1, 0)
    fed_other = swap_cores(fed[local:].astype(low))
    output = (middle + fed[:local] + fed_other.astype(jnp.float32)).astype(low)
    grad_down = contract(hidden, both_back, 0, 0).astype(low)
    grad_hidden = contract(both_back, half_down, 1, 1)
    sigmoid = jax.nn.sigmoid(gate)
    grad_gate = grad_hidden * upward * sigmoid * (1.0 + gate * (1.0 - sigmoid))
    grad_up = grad_hidden * gate * sigmoid
    grad_expanded = jnp.concatenate([grad_gate, grad_up], axis=1).astype(low)
    grad_normed = contract(grad_expanded, half_expand, 1, 1)
    grad_expand = contract(both_normed, grad_expanded, 0, 0).astype(low)
    grad_other = swap_cores(grad_normed[local:].astype(low))
    grad_normed_two = grad_normed[:local] + grad_other.astype(jnp.float32)
    back_two, gain_grad_two = norm_back(grad_normed_two, middle, inv_two, gain_two)
    grad_middle = back_rows.astype(jnp.float32) + back_two
    middle_low = grad_middle.astype(low)
    grad_proj = contract(attended, middle_low, 1, 0).astype(low)
    back_one, back_two = ordered(core, middle_low[:, : D // 2], middle_low[:, D // 2 :])
    grad_att = (contract(proj_one, back_one, 1, 1) + contract(proj_two, back_two, 1, 1)).astype(
        low
    )

    down_sum = lax.psum_scatter(grad_down, CTX, scatter_dimension=0, tiled=True)
    expand_sum = lax.psum_scatter(grad_expand, CTX, scatter_dimension=0, tiled=True)

    grad_query, key_terms = attend_back(query, all_keys, bias, grad_att, attended, lse)
    key_terms = exchange(key_terms, CTX)
    query_mixed = (
        rotate_back(grad_query.reshape(HEADS, HEAD_DIM, local), cosine, sine)
        .reshape(width, local)
        .astype(low)
    )
    grad_q = contract(normed_one, query_mixed, 0, 1).astype(low)
    kept, sent = ordered(core, grad_q, grad_proj)
    early = (kept.astype(jnp.float32) + swap_cores(sent).astype(jnp.float32)).astype(low)
    early = total(exchange(early.reshape(groups, shard, width), CTX))

    grad_keys = jnp.transpose(jnp.sum(key_terms.astype(jnp.float32), axis=0), (0, 2, 1))
    key_mixed = jnp.concatenate(
        [
            rotate_back(grad_keys[:, :HEAD_DIM], cosine, sine).reshape(kv_width, local),
            grad_keys[:, HEAD_DIM:].reshape(kv_width, local),
        ],
        axis=0,
    ).astype(low)
    grad_kv = contract(normed_one, key_mixed, 0, 1)
    grad_mixed = jnp.concatenate([query_mixed, key_mixed], axis=0)
    mixed_one, mixed_two = ordered(core, grad_mixed[: QKVW // 2], grad_mixed[QKVW // 2 :])
    grad_normed_one = contract(mixed_one, mine[:, : QKVW // 2], 0, 1) + contract(
        mixed_two, theirs[:, : QKVW // 2], 0, 1
    )
    back_first, gain_grad_one = norm_back(grad_normed_one, rows_in, inv_one, gain_one)
    input_grad = (grad_middle + back_first).astype(low).reshape(batch, local, width)
    late = jnp.concatenate(
        [
            grad_kv,
            gain_grad_one[:, None],
            gain_grad_two[:, None],
            jnp.zeros((width, 768 - 2 * kv_width - 2), jnp.float32),
        ],
        axis=1,
    ).astype(low)
    kept, sent = ordered(core, late[:, :384], late[:, 384:])
    late = (kept.astype(jnp.float32) + swap_cores(sent).astype(jnp.float32)).astype(low)
    late = total(exchange(late.reshape(groups, shard, 384), CTX))
    late = total(spread(late, CHIPS, 8))
    late = jnp.concatenate(ordered(core, late, swap_cores(late)), axis=1).astype(jnp.float32)

    expand_sum = total(exchange(expand_sum.reshape(8, shard // 8, FF), CHIPS))
    expand_sum = spread(expand_sum, CHIPS, 8).reshape(shard, FF)
    expand_one, expand_two = ordered(core, expand_sum, swap_cores(expand_sum))
    whole_expand = jnp.concatenate(
        [
            part[:, k * hidden_shard : (k + 1) * hidden_shard]
            for k in range(16)
            for part in (expand_one, expand_two)
        ],
        axis=1,
    ).astype(jnp.float32)
    rest = jnp.concatenate(
        [
            down_sum.reshape(8, hidden_shard // 8, width),
            early.reshape(8, shard // 8, width),
        ],
        axis=1,
    )
    rest = spread(total(exchange(rest, CHIPS)), CHIPS, 8)
    rest_one, rest_two = ordered(core, rest, swap_cores(rest))
    piece = hidden_shard // 8
    whole_down = jnp.concatenate(
        [part[:, :piece].reshape(hidden_shard, width) for part in (rest_one, rest_two)], axis=0
    ).astype(jnp.float32)
    whole_qkv = jnp.concatenate(
        [
            rest_one[:, piece:].reshape(shard, width).astype(jnp.float32),
            late[:, : 2 * kv_width],
        ],
        axis=1,
    )
    whole_proj = rest_two[:, piece:].reshape(shard, width).astype(jnp.float32)
    whole_gains = late[:, 2 * kv_width : 2 * kv_width + 2].T

    new_qkv, qkv_mean, qkv_square = adam_step(
        w_qkv, qkv_first, qkv_second, whole_qkv, 2.0 * D ** (-0.5), 0.1
    )
    new_proj, proj_mean, proj_square = adam_step(
        w_proj, proj_first, proj_second, whole_proj, 2.0 * (D // 8) ** (-0.5), 0.1
    )
    new_expand, expand_mean, expand_square = adam_step(
        w_expand, expand_first, expand_second, whole_expand, 2.0 * D ** (-0.5), 0.1
    )
    new_down, down_mean, down_square = adam_step(
        w_down, down_first, down_second, whole_down, 2.0 * FF ** (-0.5), 0.1
    )
    new_gains, gains_mean, gains_square = adam_step(
        gains, gains_first, gains_second, whole_gains, 1.0, 0.0
    )
    return (
        output.reshape(batch, local, width),
        input_grad,
        new_qkv,
        qkv_mean,
        qkv_square,
        new_proj,
        proj_mean,
        proj_square,
        new_expand,
        expand_mean,
        expand_square,
        new_down,
        down_mean,
        down_square,
        new_gains,
        gains_mean,
        gains_square,
    )


def solution(mesh):
    parts = jax.sharding.Mesh(mesh.devices.reshape(2, 4, 2, 2, 4), AXES)
    dp, ctx = ("zh", "y", "core"), CTX
    rows = P(dp, ctx, None)
    owned = P(ctx, None)
    split = P(None, ctx)
    return jax.shard_map(
        on_device,
        mesh=parts,
        in_specs=(rows, rows, P()) + (owned,) * 12 + (split,) * 3,
        out_specs=(rows, rows) + (owned,) * 12 + (split,) * 3,
        check_vma=False,
    )
```

time: 619 us -> 500 us (0.81)
  starting transfers between devices: 192 us -> 71.7 us
  local copies, waits for them, and re-layouts: 86.3 us -> 38.5 us
  waiting for transfers between devices: 132 us -> 171 us
  blocking collectives: 33.4 us -> 55.3 us
  other arithmetic: 68.2 us -> 47.8 us
  matrix products: 34.6 us -> 48.5 us
    all_to_all x5 -> x10, waiting for transfers between devices: 14.8 us -> 164 us  [exchange(): return lax.all_to_all(stack, axes, 0, 0, tiled=True)]
    ppermute x62 -> x10, waiting for transfers between devices: 117 us -> 6.58 us  [swap_cores(): return lax.ppermute(value, 'core', [(0, 1), (1, 0)])]
    ppermute x62 -> x10, starting transfers between devices: 117 us -> 12.9 us  [swap_cores(): return lax.ppermute(value, 'core', [(0, 1), (1, 0)])]
    all_to_all x0 -> x1, blocking collectives: none -> 55.3 us  [exchange(): return lax.all_to_all(stack, axes, 0, 0, tiled=True)]
    all_gather x1 -> x0, blocking collectives: 33.4 us -> none  [on_device(): full_gains = lax.all_gather(gains.astype(low), 'ctx', axis=1, tiled=True)]
    dynamic_update_slice x22 -> x0, local copies, waits for them, and re-layouts: 22.6 us -> none  [the longest x14 12.7 us: gather_direct(): lax.dynamic_update_index_in_dim(whole, send(piece, target), me ^ k, 0)]
    all_to_all x5 -> x10, starting transfers between devices: 74.5 us -> 58 us  [exchange(): return lax.all_to_all(stack, axes, 0, 0, tiled=True)]
    dot_general x14 -> x17, matrix products: 34.6 us -> 48.5 us  [contract(): lax.dot_general(left, right, (((left_axis,), (right_axis,)), ((), ())), p...]
  transfers between devices with their start and end apart: 68 -> 24, of which waited for: 12 -> 13; matrix products, arithmetic and copies ran while one was open for 27% -> 20% of each run, Pallas kernels for 7% -> 9%
where the time goes in v2:
time: 500 us; the launch traced here: 493 us
  waiting for transfers between devices  171 us (34%)
  starting transfers between devices  71.7 us (14%)
  blocking collectives  55.3 us (11%)
  matrix products  48.5 us (10%)
  other arithmetic  47.8 us (10%)
  Pallas kernels  45.4 us (9%)
  local copies, waits for them, and re-layouts  38.5 us (8%)
  between operations  15.1 us (3%)
    all_to_all x10, waiting for transfers between devices, exchange(): return lax.all_to_all(stack, axes, 0, 0, tiled=True)  164 us
    all_to_all x10, starting transfers between devices, exchange(): return lax.all_to_all(stack, axes, 0, 0, tiled=True)  58 us
    all_to_all x1, blocking collectives, exchange(): return lax.all_to_all(stack, axes, 0, 0, tiled=True)  55.3 us
    dot_general x17, matrix products, contract(): lax.dot_general(left, right, (((left_axis,), (right_axis,)), ((), ())), p...  48.5 us
    pallas_call x1, Pallas kernels, attend_back(): pl.pallas_call(attend_back_kernel, grid=(KV_HEADS,), out_shape=(jax.Shape...  26.7 us
    pallas_call x1, Pallas kernels, attend(): pl.pallas_call(attend_kernel, grid=(KV_HEADS,), out_shape=(jax.ShapeDtype...  18.7 us
    sub x5, other arithmetic, adam_step(): return (master - rate * update, new_first, new_second)  18.4 us
    ppermute x10, starting transfers between devices, swap_cores(): return lax.ppermute(value, 'core', [(0, 1), (1, 0)])  12.9 us
  transfers between devices with their start and end apart: 24, of which 13 were waited for; matrix products, arithmetic and copies ran while one was open for 20% of the time, Pallas kernels for 9%

profile of v2, /device:TPU:1, one launch (start us, length us, event | category | flops | bytes accessed | tf_op | source)
XLA Modules:
  0.0 493.2 jit_solution(6443610154658387999)
XLA Ops:
  12.5 55.3 %all_to_all.55 = bf16[8,120,1280]{2,1,0:T(8,128)(2,1)} all-to-all(bf16[8,120,1280]{2,1,0:T(8,128)(2,1)S(1)} %broadcast_in_dim.41), channel_id=1, replica_groups=mesh['zh'=2,'y'=4,'core'=2,'zl'=2,'x'=4] {'zl','x'}, dimensions={0} | all-to-all | bytes 4915200 | tf_op jit(solution)/shard_map/all_to_all | solution.py:38
  67.9 5.3 %collective-permute-start = (bf16[960,1280]{1,0:T(8,128)(2,1)}, bf16[960,1280]{1,0:T(8,128)(2,1)S(1)}, u32[]{:S(2)}, u32[]{:S(2)}) collective-permute-start(bf16[960,1280]{1,0:T(8,128)(2,1)} %bitcast.2), channel_id=1, source_target_pairs={{0,8},{8,0},{1,9},{9,1},{2,10},{10,2},{3,11},{11,3},{4,12},{12,4},... | collective-permute-start | bytes 7372808 | tf_op jit(solution)/shard_map/ppermute | solution.py:34
  78.0 4.2 all-to-all-done
  92.2 3.6 all-to-all-start.2
  104.5 35.8 %all-to-all-done.2.kv_ref = bf16[8,5,128,256]{3,2,1,0:T(8,128)(2,1)S(1)} async-done(((bf16[8,5,128,256]{3,2,1,0:T(8,128)(2,1)}), bf16[8,5,128,256]{3,2,1,0:T(8,128)(2,1)S(1)}, u32[]{:S(2)}, u32[]{:S(2)}) %all-to-all-start.2) | async-done | bytes 2621472 | tf_op jit(solution)/shard_map/all_to_all | solution.py:38
  143.9 18.7 %attend.1 = (bf16[960,256]{1,0:T(8,128)(2,1)S(1)}, f32[15,1,256]{2,1,0:T(1,128)S(1)}) custom-call(bf16[960,256]{1,0:T(8,128)(2,1)S(1)} %bitcast.92, bf16[8,5,128,256]{3,2,1,0:T(8,128)(2,1)S(1)} %all-to-all-done.2.kv_ref, f32[2048,256]{1,0:T(8,128)S(1)} %copy-done.1), custom_call_target="tpu_custom_call" | custom-call | flops 8053063680 | bytes 8388608 | tf_op jit(solution)/shard_map/attend/pallas_call | solution.py:167
  171.0 7.2 %fusion.48 = f32[512,2560]{1,0:T(8,128)} fusion(bf16[960,2560]{1,0:T(8,128)(2,1)} %all-gather.3.cloned.1.call-done, bf16[256,960]{0,1:T(8,128)(2,1)S(1)} %collective-permute-done.1, bf16[256,960]{0,1:T(8,128)(2,1)S(1)} %multiply_convert_fusion.3), kind=kOutput, calls=%fused_computation.101 | convolution fusion | flops 2518548480 | bytes 11141120 | tf_op jit(solution)/shard_map/dot_general | solution.py:92
  178.2 7.6 %multiply_convert_fusion.1 = (bf16[512,1280]{1,0:T(8,128)(2,1)}, bf16[512,1280]{1,0:T(8,128)(2,1)}, bf16[512,1280]{1,0:T(8,128)(2,1)S(1)}) fusion(f32[512,2560]{1,0:T(8,128)} %fusion.48, bf16[1280,960]{1,0:T(8,128)(2,1)} %all-gather.5.cloned.1.call-done, bf16[256,960]{0,1:T(8,128)(2,1)} %collective-permute-done.3, bf16[256,960]{0,1:T(8,128)(2,1)} %bitcast.9), kind=kOutput, calls=%fused_computation.8 | convolution fusion | flops 1270743040 | bytes 12615680 | tf_op jit(solution)/shard_map/dot_general | solution.py:92
  186.8 4.4 convolution_convert_fusion.1
  191.4 5.6 %fusion.2 = f32[512,960]{0,1:T(8,128)S(1)} fusion(bf16[960,2560]{1,0:T(8,128)(2,1)} %all-gather.3.cloned.1.call-done, bf16[512,1280]{1,0:T(8,128)(2,1)} %get-tuple-element.138, bf16[512,1280]{1,0:T(8,128)(2,1)} %get-tuple-element.137), kind=kOutput, calls=%fused_computation.19 | convolution fusion | flops 2521825280 | bytes 9502720 | tf_op jit(solution)/shard_map/dot_general | solution.py:92
  201.4 4.6 convolution_convert_fusion
  215.0 26.7 %attend_back.1 = (f32[960,256]{1,0:T(8,128)S(1)}, bf16[8,5,256,128]{3,2,1,0:T(8,128)(2,1)}) custom-call(bf16[960,256]{1,0:T(8,128)(2,1)S(1)} %bitcast.93, bf16[8,5,128,256]{3,2,1,0:T(8,128)(2,1)} %copy-done, f32[2048,256]{1,0:T(8,128)S(1)} %copy-done.2, bf16[960,256]{1,0:T(8,128)(2,1)S(1)} %fusion.16.do_ref, bf16[960,256]{1,0:T(8,128)(2,1)S(1)} %get-tuple-element.21.o_ref, ...), custom_call_target="tpu_custom_call" | custom-call | flops 20132659200 | bytes 8388608 | tf_op jit(solution)/shard_map/attend_back/pallas_call | solution.py:189
  241.7 10.3 %all-to-all-start.3 = ((bf16[8,5,256,128]{3,2,1,0:T(8,128)(2,1)}), bf16[8,5,256,128]{3,2,1,0:T(8,128)(2,1)}, u32[]{:S(2)}, u32[]{:S(2)}) async-start(bf16[8,5,256,128]{3,2,1,0:T(8,128)(2,1)} %get-tuple-element.24), calls=%async_computation.3 | async-start | bytes 5242880 | tf_op jit(solution)/shard_map/all_to_all | solution.py:38
  254.6 3.3 collective-permute-done.5
  260.6 40.9 %all-to-all-done.3 = bf16[8,5,256,128]{3,2,1,0:T(8,128)(2,1)} async-done(((bf16[8,5,256,128]{3,2,1,0:T(8,128)(2,1)}), bf16[8,5,256,128]{3,2,1,0:T(8,128)(2,1)}, u32[]{:S(2)}, u32[]{:S(2)}) %all-to-all-start.3) | async-done | bytes 2621472 | tf_op jit(solution)/shard_map/all_to_all | solution.py:38
  301.5 13.6 %all-to-all-start.4 = ((bf16[8,120,960]{2,1,0:T(8,128)(2,1)}), bf16[8,120,960]{2,1,0:T(8,128)(2,1)S(1)}, u32[]{:S(2)}, u32[]{:S(2)}) async-start(bf16[8,120,960]{2,1,0:T(8,128)(2,1)} %bitcast.96), calls=%async_computation.5 | async-start | bytes 3932160 | tf_op jit(solution)/shard_map/all_to_all | solution.py:38
  332.6 20.3 %all-to-all-done.4 = bf16[8,120,960]{2,1,0:T(8,128)(2,1)S(1)} async-done(((bf16[8,120,960]{2,1,0:T(8,128)(2,1)}), bf16[8,120,960]{2,1,0:T(8,128)(2,1)S(1)}, u32[]{:S(2)}, u32[]{:S(2)}) %all-to-all-start.4) | async-done | bytes 1843232 | tf_op jit(solution)/shard_map/all_to_all | solution.py:38
  352.9 5.5 %all-to-all-start.7 = ((bf16[8,120,384]{2,1,0:T(8,128)(2,1)}), bf16[8,120,384]{2,1,0:T(8,128)(2,1)S(1)}, u32[]{:S(2)}, u32[]{:S(2)}) async-start(bf16[8,120,384]{2,1,0:T(8,128)(2,1)} %bitcast.18), calls=%async_computation.8 | async-start | bytes 1474560 | tf_op jit(solution)/shard_map/all_to_all | solution.py:38
  361.0 9.9 %all-to-all-done.7 = bf16[8,120,384]{2,1,0:T(8,128)(2,1)S(1)} async-done(((bf16[8,120,384]{2,1,0:T(8,128)(2,1)}), bf16[8,120,384]{2,1,0:T(8,128)(2,1)S(1)}, u32[]{:S(2)}, u32[]{:S(2)}) %all-to-all-start.7) | async-done | bytes 737312 | tf_op jit(solution)/shard_map/all_to_all | solution.py:38
  370.9 7.2 %all-to-all-start.5 = ((bf16[8,35,960]{2,1,0:T(8,128)(2,1)}), bf16[8,35,960]{2,1,0:T(8,128)(2,1)S(1)}, u32[]{:S(2)}, u32[]{:S(2)}) async-start(bf16[8,35,960]{2,1,0:T(8,128)(2,1)} %pad_maximum_fusion.8), calls=%async_computation.6 | async-start | bytes 1310720 | tf_op jit(solution)/shard_map/all_to_all | solution.py:38
  378.2 13.0 %all-to-all-done.5 = bf16[8,35,960]{2,1,0:T(8,128)(2,1)S(1)} async-done(((bf16[8,35,960]{2,1,0:T(8,128)(2,1)}), bf16[8,35,960]{2,1,0:T(8,128)(2,1)S(1)}, u32[]{:S(2)}, u32[]{:S(2)}) %all-to-all-start.5) | async-done | bytes 537632 | tf_op jit(solution)/shard_map/all_to_all | solution.py:38
  392.3 3.5 all-to-all-start.8
  397.1 12.6 %all-to-all-done.8 = bf16[8,120,384]{2,1,0:T(8,128)(2,1)S(1)} async-done(((bf16[8,120,384]{2,1,0:T(8,128)(2,1)}), bf16[8,120,384]{2,1,0:T(8,128)(2,1)S(1)}, u32[]{:S(2)}, u32[]{:S(2)}) %all-to-all-start.8) | async-done | bytes 737312 | tf_op jit(solution)/shard_map/all_to_all | solution.py:38
  410.7 3.5 all-to-all-start.6
  417.6 9.6 %all-to-all-done.6 = bf16[8,35,960]{2,1,0:T(8,128)(2,1)S(1)} async-done(((bf16[8,35,960]{2,1,0:T(8,128)(2,1)}), bf16[8,35,960]{2,1,0:T(8,128)(2,1)S(1)}, u32[]{:S(2)}, u32[]{:S(2)}) %all-to-all-start.6) | async-done | bytes 537632 | tf_op jit(solution)/shard_map/all_to_all | solution.py:38
  430.7 3.8 all-to-all-start.9
  436.7 11.0 %all-to-all-done.9 = bf16[8,15,2560]{2,1,0:T(8,128)(2,1)S(1)} async-done(((bf16[8,15,2560]{2,1,0:T(8,128)(2,1)}), bf16[8,15,2560]{2,1,0:T(8,128)(2,1)S(1)}, u32[]{:S(2)}, u32[]{:S(2)}) %all-to-all-start.9) | async-done | bytes 614432 | tf_op jit(solution)/shard_map/all_to_all | solution.py:38
  448.7 3.5 all-to-all-start.10
  453.5 4.9 multiply_subtract_fusion.1
  458.4 6.9 %all-to-all-done.10 = bf16[8,15,2560]{2,1,0:T(8,128)(2,1)S(1)} async-done(((bf16[8,15,2560]{2,1,0:T(8,128)(2,1)}), bf16[8,15,2560]{2,1,0:T(8,128)(2,1)S(1)}, u32[]{:S(2)}, u32[]{:S(2)}) %all-to-all-start.10) | async-done | bytes 614432 | tf_op jit(solution)/shard_map/all_to_all | solution.py:38
  475.0 4.1 concatenate.83
  479.1 7.1 %multiply_subtract_fusion = (f32[120,5120]{1,0:T(8,128)}, f32[120,5120]{1,0:T(8,128)}, f32[120,5120]{1,0:T(8,128)}) fusion(f32[120,5120]{1,0:T(8,128)S(1)} %copy-done.7, bf16[120,5120]{1,0:T(8,128)(2,1)} %concatenate.83, f32[120,5120]{1,0:T(8,128)} %param.28, f32[120,5120]{1,0:T(8,128)} %param.29), kind=kLoop, calls=%fused_computation.13 | loop fusion | flops 9830400 | bytes 15974400 | tf_op jit(solution)/shard_map/sub | solution.py:212
  (215 shorter events, 104.3 us)
Async XLA Ops:
  7.2 163.8 %all-gather.3.cloned.1.call-start = ((), (), s32[]{:S(2)}) async-start(), calls=%async_computation.13 | async-start | bytes 5529600 | tf_op jit(solution)/shard_map/all_gather | solution.py:276
  12.5 60.7 %copy-start.27 = (f32[2,120]{1,0:T(2,128)S(1)}, f32[2,120]{1,0:T(2,128)}, u32[]{:S(2)}) copy-start(f32[2,120]{1,0:T(2,128)} %param.33) | copy-start | bytes 2884
  12.5 64.6 %copy-start.30 = (s32[16]{0:T(128)S(1)}, s32[16]{0:T(128)}, u32[]{:S(2)}) copy-start(s32[16]{0:T(128)} %param.20) | copy-start | bytes 196
  12.5 64.8 %copy-start.5 = (bf16[1,256,960]{1,2,0:T(8,128)(2,1)S(1)}, bf16[1,256,960]{1,2,0:T(8,128)(2,1)}, u32[]{:S(2)}) copy-start(bf16[1,256,960]{1,2,0:T(8,128)(2,1)} %param.18) | copy-start | bytes 1474564
  67.9 16.8 %collective-permute-start = (bf16[960,1280]{1,0:T(8,128)(2,1)}, bf16[960,1280]{1,0:T(8,128)(2,1)S(1)}, u32[]{:S(2)}, u32[]{:S(2)}) collective-permute-start(bf16[960,1280]{1,0:T(8,128)(2,1)} %bitcast.2), channel_id=1, source_target_pairs={{0,8},{8,0},{1,9},{9,1},{2,10},{10,2},{3,11},{11,3},{4,12},{12,4},... | collective-permute-start | bytes 7372808 | tf_op jit(solution)/shard_map/ppermute | solution.py:34
  73.8 8.3 %all-to-all-start = ((bf16[8,2,120]{2,1,0:T(2,128)(2,1)}), bf16[8,2,120]{2,1,0:T(2,128)(2,1)S(1)}, u32[]{:S(2)}, u32[]{:S(2)}) async-start(bf16[8,2,120]{2,1,0:T(2,128)(2,1)} %broadcast_in_dim.40), calls=%async_computation | async-start | bytes 8192 | tf_op jit(solution)/shard_map/all_to_all | solution.py:38
  77.8 12.1 %copy-start.19 = (f32[32,256]{0,1:T(8,128)}, f32[32,256]{0,1:T(8,128)S(1)}, u32[]{:S(2)}) copy-start(f32[32,256]{0,1:T(8,128)S(1)} %copy.151) | copy-start | bytes 98308
  78.0 12.0 %copy-start.21 = (f32[32,256]{0,1:T(8,128)}, f32[32,256]{0,1:T(8,128)S(1)}, u32[]{:S(2)}) copy-start(f32[32,256]{0,1:T(8,128)S(1)} %copy.153) | copy-start | bytes 98308
  92.2 48.1 %all-to-all-start.2 = ((bf16[8,5,128,256]{3,2,1,0:T(8,128)(2,1)}), bf16[8,5,128,256]{3,2,1,0:T(8,128)(2,1)S(1)}, u32[]{:S(2)}, u32[]{:S(2)}) async-start(bf16[8,5,128,256]{3,2,1,0:T(8,128)(2,1)} %broadcast_in_dim.44), calls=%async_computation.2 | async-start | bytes 5242880 | tf_op jit(solution)/shard_map/all_to_all | solution.py:38
  95.9 82.3 %all-gather.5.cloned.1.call-start = ((), (), s32[]{:S(2)}) async-start(), calls=%async_computation.14 | async-start | bytes 2949120 | tf_op jit(solution)/shard_map/all_gather | solution.py:263
  97.8 261.1 %reduce-scatter.3.cloned.1.call-start = ((), (), s32[]{:S(2)}) async-start(), calls=%async_computation.15 | async-start | bytes 2949120 | tf_op jit(solution)/shard_map/reduce_scatter | solution.py:340
  140.3 22.3 %copy-start = (bf16[8,5,128,256]{3,2,1,0:T(8,128)(2,1)}, bf16[8,5,128,256]{3,2,1,0:T(8,128)(2,1)S(1)}, u32[]{:S(2)}) copy-start(bf16[8,5,128,256]{3,2,1,0:T(8,128)(2,1)S(1)} %all-to-all-done.2.kv_ref) | copy-start | bytes 7864324
  167.7 3.2 collective-permute-start.1
  169.5 8.7 %collective-permute-start.3 = (bf16[256,960]{0,1:T(8,128)(2,1)}, bf16[256,960]{0,1:T(8,128)(2,1)}, u32[]{:S(2)}, u32[]{:S(2)}) collective-permute-start(bf16[256,960]{0,1:T(8,128)(2,1)} %bitcast.9), channel_id=1, source_target_pairs={{0,8},{8,0},{1,9},{9,1},{2,10},{10,2},{3,11},{11,3},{4,12},{12,4},... | collective-permute-start | bytes 1474568 | tf_op jit(solution)/shard_map/ppermute | solution.py:34
  191.2 237.4 %reduce-scatter.5.cloned.1.call-start = ((), (), s32[]{:S(2)}) async-start(), calls=%async_computation.16 | async-start | bytes 5529600 | tf_op jit(solution)/shard_map/reduce_scatter | solution.py:341
  198.0 8.1 %collective-permute-start.4 = (bf16[256,960]{0,1:T(8,128)(2,1)}, bf16[256,960]{0,1:T(8,128)(2,1)S(1)}, u32[]{:S(2)}, u32[]{:S(2)}) collective-permute-start(bf16[256,960]{0,1:T(8,128)(2,1)} %slice.650), channel_id=1, source_target_pairs={{0,8},{8,0},{1,9},{9,1},{2,10},{10,2},{3,11},{11,3},{4,12},{12,4},... | collective-permute-start | bytes 1474568 | tf_op jit(solution)/shard_map/ppermute | solution.py:34
  201.3 6.7 %collective-permute-start.2 = (bf16[256,960]{0,1:T(8,128)(2,1)}, bf16[256,960]{0,1:T(8,128)(2,1)}, u32[]{:S(2)}, u32[]{:S(2)}) collective-permute-start(bf16[256,960]{0,1:T(8,128)(2,1)} %slice.651), channel_id=1, source_target_pairs={{0,8},{8,0},{1,9},{9,1},{2,10},{10,2},{3,11},{11,3},{4,12},{12,4},... | collective-permute-start | bytes 1474568 | tf_op jit(solution)/shard_map/ppermute | solution.py:34
  241.7 59.8 %all-to-all-start.3 = ((bf16[8,5,256,128]{3,2,1,0:T(8,128)(2,1)}), bf16[8,5,256,128]{3,2,1,0:T(8,128)(2,1)}, u32[]{:S(2)}, u32[]{:S(2)}) async-start(bf16[8,5,256,128]{3,2,1,0:T(8,128)(2,1)} %get-tuple-element.24), calls=%async_computation.3 | async-start | bytes 5242880 | tf_op jit(solution)/shard_map/all_to_all | solution.py:38
  253.6 4.3 collective-permute-start.5
  301.5 51.5 %all-to-all-start.4 = ((bf16[8,120,960]{2,1,0:T(8,128)(2,1)}), bf16[8,120,960]{2,1,0:T(8,128)(2,1)S(1)}, u32[]{:S(2)}, u32[]{:S(2)}) async-start(bf16[8,120,960]{2,1,0:T(8,128)(2,1)} %bitcast.96), calls=%async_computation.5 | async-start | bytes 3932160 | tf_op jit(solution)/shard_map/all_to_all | solution.py:38
  327.7 3.6 collective-permute-start.7
  352.9 18.0 %all-to-all-start.7 = ((bf16[8,120,384]{2,1,0:T(8,128)(2,1)}), bf16[8,120,384]{2,1,0:T(8,128)(2,1)S(1)}, u32[]{:S(2)}, u32[]{:S(2)}) async-start(bf16[8,120,384]{2,1,0:T(8,128)(2,1)} %bitcast.18), calls=%async_computation.8 | async-start | bytes 1474560 | tf_op jit(solution)/shard_map/all_to_all | solution.py:38
  370.9 20.3 %all-to-all-start.5 = ((bf16[8,35,960]{2,1,0:T(8,128)(2,1)}), bf16[8,35,960]{2,1,0:T(8,128)(2,1)S(1)}, u32[]{:S(2)}, u32[]{:S(2)}) async-start(bf16[8,35,960]{2,1,0:T(8,128)(2,1)} %pad_maximum_fusion.8), calls=%async_computation.6 | async-start | bytes 1310720 | tf_op jit(solution)/shard_map/all_to_all | solution.py:38
  392.3 17.5 %all-to-all-start.8 = ((bf16[8,120,384]{2,1,0:T(8,128)(2,1)}), bf16[8,120,384]{2,1,0:T(8,128)(2,1)S(1)}, u32[]{:S(2)}, u32[]{:S(2)}) async-start(bf16[8,120,384]{2,1,0:T(8,128)(2,1)} %broadcast_in_dim.51), calls=%async_computation.9 | async-start | bytes 1474560 | tf_op jit(solution)/shard_map/all_to_all | solution.py:38
  395.8 19.6 %copy-start.8 = (f32[256,960]{0,1:T(8,128)S(1)}, f32[256,960]{0,1:T(8,128)}, u32[]{:S(2)}) copy-start(f32[256,960]{0,1:T(8,128)} %get-tuple-element.132) | copy-start | bytes 2949124
  410.7 16.6 %all-to-all-start.6 = ((bf16[8,35,960]{2,1,0:T(8,128)(2,1)}), bf16[8,35,960]{2,1,0:T(8,128)(2,1)S(1)}, u32[]{:S(2)}, u32[]{:S(2)}) async-start(bf16[8,35,960]{2,1,0:T(8,128)(2,1)} %broadcast_in_dim.47), calls=%async_computation.7 | async-start | bytes 1310720 | tf_op jit(solution)/shard_map/all_to_all | solution.py:38
  414.5 14.0 %collective-permute-start.8 = (bf16[120,384]{0,1:T(8,128)(2,1)S(1)}, bf16[120,384]{0,1:T(8,128)(2,1)S(1)}, u32[]{:S(2)}, u32[]{:S(2)}) collective-permute-start(bf16[120,384]{0,1:T(8,128)(2,1)S(1)} %copy.163), channel_id=1, source_target_pairs={{0,8},{8,0},{1,9},{9,1},{2,10},{10,2},{3,11},{11,3},{4,12},{12,4},... | collective-permute-start | bytes 276488 | tf_op jit(solution)/shard_map/ppermute | solution.py:34
  427.6 8.4 %collective-permute-start.6 = (bf16[8,35,960]{2,0,1:T(8,128)(2,1)S(1)}, bf16[8,35,960]{2,0,1:T(8,128)(2,1)S(1)}, u32[]{:S(2)}, u32[]{:S(2)}) collective-permute-start(bf16[8,35,960]{2,0,1:T(8,128)(2,1)S(1)} %copy.158), channel_id=1, source_target_pairs={{0,8},{8,0},{1,9},{9,1},{2,10},{10,2},{3,11},{11,3},{4,12},{12,4},... | collective-permute-start | bytes 1612808 | tf_op jit(solution)/shard_map/ppermute | solution.py:34
  430.7 17.0 %all-to-all-start.9 = ((bf16[8,15,2560]{2,1,0:T(8,128)(2,1)}), bf16[8,15,2560]{2,1,0:T(8,128)(2,1)S(1)}, u32[]{:S(2)}, u32[]{:S(2)}) async-start(bf16[8,15,2560]{2,1,0:T(8,128)(2,1)} %reshape.265), calls=%async_computation.11 | async-start | bytes 1310720 | tf_op jit(solution)/shard_map/all_to_all | solution.py:38
  448.7 16.6 %all-to-all-start.10 = ((bf16[8,15,2560]{2,1,0:T(8,128)(2,1)}), bf16[8,15,2560]{2,1,0:T(8,128)(2,1)S(1)}, u32[]{:S(2)}, u32[]{:S(2)}) async-start(bf16[8,15,2560]{2,1,0:T(8,128)(2,1)} %broadcast_in_dim.52), calls=%async_computation.12 | async-start | bytes 1310720 | tf_op jit(solution)/shard_map/all_to_all | solution.py:38
  453.5 12.9 %copy-start.17 = (f32[120,960]{1,0:T(8,128)S(1)}, f32[120,960]{1,0:T(8,128)}, u32[]{:S(2)}) copy-start(f32[120,960]{1,0:T(8,128)} %param.24) | copy-start | bytes 1382404
  465.6 6.8 %collective-permute-start.9 = (bf16[120,2560]{1,0:T(8,128)(2,1)S(1)}, bf16[120,2560]{1,0:T(8,128)(2,1)}, u32[]{:S(2)}, u32[]{:S(2)}) collective-permute-start(bf16[120,2560]{1,0:T(8,128)(2,1)S(1)} %reshape.266), channel_id=1, source_target_pairs={{0,8},{8,0},{1,9},{9,1},{2,10},{10,2},{3,11},{11,3},{4,12},{12,4},... | collective-permute-start | bytes 1843208 | tf_op jit(solution)/shard_map/ppermute | solution.py:34
  (28 other events, 92.1 us)
Sparse Core Ops, SparseCore 0:
  12.0 84.6 all-gather.2
  98.9 59.0 all-gather.4
  191.3 46.6 reduce-scatter.2
  240.3 118.7 reduce-scatter.4

commit v3 on v2

v3 whole, which is shorter than its diff:
```python
import functools

import jax
import jax.numpy as jnp
from jax import lax
from jax.experimental import pallas as pl
from jax.experimental.pallas import tpu as pltpu
from jax.sharding import PartitionSpec as P

D = 960
HEADS = 15
KV_HEADS = 5
GROUP = HEADS // KV_HEADS
HEAD_DIM = 64
FF = 2560
STEP = 10
HALF = FF // 2
QKVW = D + 2 * KV_HEADS * HEAD_DIM


eps = 1e-05
rope_base = 100000.0
beta_first = 0.9
beta_second = 0.95
adam_eps = 1e-08
masked_score = -1e30
TALL = 56
PADDED = 896
NEAR = 1408
ATTEND_FLOPS = 20 * 10**9
BACK_FLOPS = 25 * 10**9
FEED_FLOPS = 20 * 10**9
low = jnp.bfloat16


AXES = ("zh", "y", "core", "zl", "x")
CHIPS = ("zh", "y")
CTX = ("zl", "x")


def swap_cores(value):
    return lax.ppermute(value, "core", [(0, 1), (1, 0)])


def to_peer(value, axis, k):
    count = lax.axis_size(axis)
    return lax.ppermute(value, axis, [(i, i ^ k) for i in range(count)])


def double(piece, axis, k, side):
    bit = lax.axis_index(axis) // k % 2 == 0
    came = to_peer(piece, axis, k)
    return jnp.concatenate(
        [jnp.where(bit, piece, came), jnp.where(bit, came, piece)], axis=side
    )


def add_peer(piece, axis, k):
    return (piece.astype(jnp.float32) + to_peer(piece, axis, k).astype(jnp.float32)).astype(low)


def exchange(stack, axes):
    return lax.all_to_all(stack, axes, 0, 0, tiled=True)


def spread(piece, axes, count):
    return exchange(jnp.broadcast_to(piece[None], (count,) + piece.shape), axes)


def total(stack):
    return jnp.sum(stack.astype(jnp.float32), axis=0).astype(low)


def ordered(core, mine, theirs):
    first = core == 0
    return jnp.where(first, mine, theirs), jnp.where(first, theirs, mine)


def rope_tables(positions):
    halfway = HEAD_DIM // 2
    freqs = rope_base ** (-(jnp.arange(halfway, dtype=jnp.float32) * 2.0) / HEAD_DIM)
    angles = freqs[:, None] * positions.astype(jnp.float32)[None, :]
    return (jnp.cos(angles), jnp.sin(angles))


def rms_scale(rows):
    return lax.rsqrt(jnp.mean(rows * rows, axis=-1, keepdims=True) + eps)


def contract(left, right, left_axis, right_axis):
    return lax.dot_general(
        left,
        right,
        (((left_axis,), (right_axis,)), ((), ())),
        preferred_element_type=jnp.float32,
    )


def load_keys(kv_ref):
    columns = jnp.concatenate([kv_ref[j, 0] for j in range(kv_ref.shape[0])], axis=1)
    return columns, columns.T


def fill_bias(order_ref, own_ref, bias_ref):
    slots = order_ref.shape[0]
    span = bias_ref.shape[0] // slots
    ahead = lax.broadcasted_iota(jnp.int32, (span, span), 0) - lax.broadcasted_iota(
        jnp.int32, (span, span), 1
    )
    for s in range(slots):
        for t in range(own_ref.shape[0]):
            gap = (order_ref[s] - own_ref[t]) * span
            bias_ref[s * span : (s + 1) * span, t * span : (t + 1) * span] = jnp.where(
                ahead + gap <= 0, 0.0, masked_score
            )


def attend_kernel(order_ref, own_ref, q_ref, kv_ref, o_ref, lse_ref, bias_ref):
    @pl.when(pl.program_id(0) == 0)
    def _():
        fill_bias(order_ref, own_ref, bias_ref)

    columns, rows = load_keys(kv_ref)
    bias = bias_ref[...]
    blank = jnp.zeros((HEAD_DIM, q_ref.shape[1]), low)
    for h in range(GROUP):
        part = pl.ds(h * HEAD_DIM, HEAD_DIM)
        query = jnp.concatenate([q_ref[part, :], blank], axis=0)
        scores = contract(rows, query, 1, 0) + bias
        top = jnp.max(scores, axis=0, keepdims=True)
        weights = jnp.exp(scores - top)
        total = jnp.sum(weights, axis=0, keepdims=True)
        mixed = contract(columns[HEAD_DIM:], weights.astype(low), 1, 0)
        o_ref[part, :] = (mixed / total).astype(low)
        lse_ref[h] = top + jnp.log(total)


def attend_back_kernel(
    order_ref, own_ref, q_ref, kv_ref, do_ref, o_ref, lse_ref, dq_ref, dkv_ref, bias_ref
):
    @pl.when(pl.program_id(0) == 0)
    def _():
        fill_bias(order_ref, own_ref, bias_ref)

    columns, rows = load_keys(kv_ref)
    bias = bias_ref[...]
    local = q_ref.shape[1]
    blank = jnp.zeros((HEAD_DIM, local), low)
    terms = None
    for h in range(GROUP):
        part = pl.ds(h * HEAD_DIM, HEAD_DIM)
        query = jnp.concatenate([q_ref[part, :], blank], axis=0)
        back = jnp.concatenate([blank, do_ref[part, :]], axis=0)
        delta = jnp.sum(
            do_ref[part, :].astype(jnp.float32) * o_ref[part, :].astype(jnp.float32),
            axis=0,
            keepdims=True,
        )
        weights = jnp.exp(contract(rows, query, 1, 0) + bias - lse_ref[h])
        grad = contract(rows, back, 1, 0)
        scores = (weights * (grad - delta)).astype(low)
        dq_ref[part, :] = contract(columns[:HEAD_DIM], scores, 1, 0) * HEAD_DIM ** (-0.5)
        term = contract(scores, query, 1, 1) + contract(weights.astype(low), back, 1, 1)
        terms = term if terms is None else terms + term
    for j in range(dkv_ref.shape[0]):
        dkv_ref[j, 0] = terms[j * local : (j + 1) * local].astype(low)


def attention_specs(chunks, local):
    wide = GROUP * HEAD_DIM
    heads = pl.BlockSpec((wide, local), lambda g: (g, 0))
    keys = pl.BlockSpec((chunks, 1, 2 * HEAD_DIM, local), lambda g: (0, g, 0, 0))
    sums = pl.BlockSpec((GROUP, 1, local), lambda g: (g, 0, 0))
    return heads, keys, sums


def scalars():
    return pl.BlockSpec(memory_space=pltpu.SMEM)


def attend(order, own, query, keys):
    chunks, _, _, local = keys.shape
    heads, kv, sums = attention_specs(chunks, local)
    return pl.pallas_call(
        attend_kernel,
        grid=(KV_HEADS,),
        out_shape=(
            jax.ShapeDtypeStruct((D, local), low),
            jax.ShapeDtypeStruct((HEADS, 1, local), jnp.float32),
        ),
        in_specs=[scalars(), scalars(), heads, kv],
        out_specs=(heads, sums),
        scratch_shapes=[pltpu.VMEM((chunks * local, local), jnp.float32)],
        compiler_params=pltpu.CompilerParams(vmem_limit_bytes=48 * 1024 * 1024),
        cost_estimate=pl.CostEstimate(
            flops=ATTEND_FLOPS, bytes_accessed=1000, transcendentals=0
        ),
        name="attend",
    )(order, own, query, keys)


def attend_back(order, own, query, keys, back, out, lse):
    chunks, _, _, local = keys.shape
    heads, kv, sums = attention_specs(chunks, local)
    grads = pl.BlockSpec((chunks, 1, local, 2 * HEAD_DIM), lambda g: (0, g, 0, 0))
    return pl.pallas_call(
        attend_back_kernel,
        grid=(KV_HEADS,),
        out_shape=(
            jax.ShapeDtypeStruct((D, local), jnp.float32),
            jax.ShapeDtypeStruct((chunks, KV_HEADS, local, 2 * HEAD_DIM), low),
        ),
        in_specs=[scalars(), scalars(), heads, kv, heads, heads, sums],
        out_specs=(heads, grads),
        scratch_shapes=[pltpu.VMEM((chunks * local, local), jnp.float32)],
        compiler_params=pltpu.CompilerParams(vmem_limit_bytes=48 * 1024 * 1024),
        cost_estimate=pl.CostEstimate(
            flops=BACK_FLOPS, bytes_accessed=1000, transcendentals=0
        ),
        name="attend_back",
    )(order, own, query, keys, back, out, lse)


def whole_call(kernel, name, flops, out_shape, *operands):
    whole = pl.BlockSpec(memory_space=pltpu.VMEM)
    return pl.pallas_call(
        kernel,
        out_shape=out_shape,
        in_specs=[scalars() if value.ndim == 1 else whole for value in operands],
        out_specs=jax.tree.map(lambda _: whole, out_shape),
        compiler_params=pltpu.CompilerParams(vmem_limit_bytes=48 * 1024 * 1024),
        cost_estimate=pl.CostEstimate(flops=flops, bytes_accessed=1000, transcendentals=0),
        name=name,
    )(*operands)


def stage_kernel(
    place_ref, qkv_ref, proj_ref, expand_ref, down_ref, gains_ref, near_ref, wide_ref, tall_ref
):
    first = place_ref[0] == 0
    shard = qkv_ref.shape[0]
    step = FF // 16
    gains = jnp.concatenate(
        [gains_ref[...], jnp.zeros((6, gains_ref.shape[1]), jnp.float32)], axis=0
    )
    gains = jnp.concatenate([gains, jnp.zeros((8, 128 - shard), jnp.float32)], axis=1).T
    near = jnp.concatenate(
        [
            jnp.where(first, qkv_ref[:, : QKVW // 2], qkv_ref[:, QKVW // 2 :]),
            gains[:shard, :2],
            jnp.zeros((shard, PADDED - QKVW // 2 - 2), jnp.float32),
            jnp.where(first, proj_ref[:, : D // 2], proj_ref[:, D // 2 :]),
            jnp.zeros((shard, NEAR - PADDED - D // 2), jnp.float32),
        ],
        axis=1,
    ).astype(low)
    parts = []
    for k in range(4):
        left = expand_ref[:, 2 * k * step : (2 * k + 1) * step]
        right = expand_ref[:, (2 * k + 1) * step : (2 * k + 2) * step]
        parts.append(jnp.where(first, left, right))
    wide = jnp.concatenate(parts, axis=1).astype(low)
    tall = down_ref[...].astype(low)
    for j in range(near_ref.shape[0]):
        near_ref[j] = near
        wide_ref[j] = wide
        tall_ref[j] = tall


def stage(place, qkv, proj, expand, down, gains, groups):
    shard = qkv.shape[0]
    half = down.shape[0] // 2

    def whole(value):
        return pl.BlockSpec(value.shape, lambda i, place: (0, 0))

    outs = [(groups, shard, NEAR), (groups, shard, FF // 4), (groups, half, D)]
    return pl.pallas_call(
        stage_kernel,
        grid_spec=pltpu.PrefetchScalarGridSpec(
            num_scalar_prefetch=1,
            grid=(1,),
            in_specs=[
                whole(qkv),
                whole(proj),
                pl.BlockSpec((shard, HALF), lambda i, place: (0, place[1])),
                pl.BlockSpec((half, D), lambda i, place: (place[0], 0)),
                whole(gains),
            ],
            out_specs=[pl.BlockSpec(out, lambda i, place: (0, 0, 0)) for out in outs],
        ),
        out_shape=[jax.ShapeDtypeStruct(out, low) for out in outs],
        compiler_params=pltpu.CompilerParams(vmem_limit_bytes=40 * 1024 * 1024),
        cost_estimate=pl.CostEstimate(flops=1000, bytes_accessed=8 * 10**6, transcendentals=0),
        name="stage",
    )(place, qkv, proj, expand, down, gains)


def rotated(block, cosine, sine):
    first = block[: HEAD_DIM // 2]
    second = block[HEAD_DIM // 2 :]
    return [first * cosine - second * sine, second * cosine + first * sine]


def project_kernel(
    core_ref,
    rows_ref,
    mine_ref,
    theirs_ref,
    cosine_ref,
    sine_ref,
    normed_ref,
    query_ref,
    keys_ref,
    gains_ref,
):
    first_core = core_ref[0] == 0
    cosine = cosine_ref[...]
    sine = sine_ref[...]
    rows = rows_ref[...].astype(jnp.float32).T
    gains = mine_ref[:, PADDED - 128 : PADDED].astype(jnp.float32).T
    at = QKVW // 2 - (PADDED - 128)
    gains_ref[...] = gains[at : at + 2]
    normed = (rows * rms_scale(rows) * gains[at : at + 1]).astype(low)
    normed_ref[...] = normed
    near = contract(normed, mine_ref[:, :PADDED], 1, 0).T
    away = contract(normed, theirs_ref[:, :PADDED], 1, 0).T
    half = QKVW // 2
    one = jnp.where(first_core, near, away)[:half]
    two = jnp.where(first_core, away, near)[:half]
    mixed = jnp.concatenate([one, two], axis=0)
    scale = HEAD_DIM ** (-0.5)
    for h in range(HEADS):
        span = slice(h * HEAD_DIM, (h + 1) * HEAD_DIM)
        turned = jnp.concatenate(rotated(mixed[span], cosine, sine), axis=0)
        query_ref[span] = (turned.astype(low).astype(jnp.float32) * scale).astype(low)
    for g in range(KV_HEADS):
        at = D + g * HEAD_DIM
        to = at + KV_HEADS * HEAD_DIM
        pair = rotated(mixed[at : at + HEAD_DIM], cosine, sine) + [mixed[to : to + HEAD_DIM]]
        pair = jnp.concatenate(pair, axis=0).astype(low)
        for j in range(keys_ref.shape[0]):
            keys_ref[j, g] = pair


def middle_kernel(core_ref, out_ref, mine_ref, theirs_ref, rows_ref, gains_ref, mid_ref, normed_ref):
    first_core = core_ref[0] == 0
    mixed = out_ref[...].T
    near = contract(mixed, mine_ref[:, PADDED : PADDED + D // 2], 1, 0)
    away = contract(mixed, theirs_ref[:, PADDED : PADDED + D // 2], 1, 0)
    near, away = jnp.where(first_core, near, away), jnp.where(first_core, away, near)
    middle = rows_ref[...].astype(jnp.float32).T + jnp.concatenate([near, away], axis=1)
    mid_ref[...] = middle
    normed_ref[...] = (middle * rms_scale(middle) * gains_ref[1:2]).astype(low)


def turn_kernel(
    core_ref,
    own_ref,
    came_ref,
    mid_ref,
    back_ref,
    gains_ref,
    mine_ref,
    theirs_ref,
    out_ref,
    grad_ref,
    grad_out_ref,
    kept_ref,
    sent_ref,
    gain_grad_ref,
):
    first_core = core_ref[0] == 0
    normed = own_ref[...] + came_ref[...].astype(jnp.float32)
    middle = mid_ref[...]
    inverse = rms_scale(middle)
    scaled = normed * gains_ref[1:2]
    inner = jnp.mean(scaled * middle, axis=-1, keepdims=True)
    grad = back_ref[...].astype(jnp.float32) + inverse * (
        scaled - middle * inverse * inverse * inner
    )
    grad_ref[...] = grad
    gain_grad_ref[...] = jnp.sum(normed * middle * inverse, axis=0, keepdims=True)
    one = grad[:, : D // 2]
    two = grad[:, D // 2 :]
    near = jnp.where(first_core, one, two).astype(low)
    away = jnp.where(first_core, two, one).astype(low)
    grad_out = contract(near, mine_ref[:, PADDED : PADDED + D // 2], 1, 1) + contract(
        away, theirs_ref[:, PADDED : PADDED + D // 2], 1, 1
    )
    grad_out_ref[...] = grad_out.T.astype(low)
    product = contract(out_ref[...], grad.astype(low), 1, 0)
    groups, window, _ = kept_ref.shape
    shard = product.shape[0] // groups
    for j in range(groups):
        top = product[j * shard : j * shard + window]
        bottom = product[(j + 1) * shard - window : (j + 1) * shard]
        kept_ref[j] = jnp.where(first_core, top, bottom).astype(low)
        sent_ref[j] = jnp.where(first_core, bottom, top).astype(low)


def emit_kernel(mid_ref, own_ref, came_ref, out_ref):
    value = mid_ref[...] + own_ref[...] + came_ref[...].astype(jnp.float32)
    out_ref[...] = value.T.astype(low)


def feed_kernel(
    rows_one,
    rows_two,
    back_one,
    back_two,
    expand_ref,
    down_ref,
    fed_ref,
    fed_other_ref,
    normed_ref,
    normed_other_ref,
    down_grad_ref,
    expand_grad_ref,
    rows_ref,
    back_ref,
    columns_ref,
    fed_sum,
    normed_sum,
):
    local = rows_one.shape[0]
    h = pl.program_id(0)

    @pl.when(h == 0)
    def _():
        rows_ref[:local] = rows_one[...]
        rows_ref[local:] = rows_two[...]
        back_ref[:local] = back_one[...]
        back_ref[local:] = back_two[...]
        columns_ref[...] = rows_ref[...].T

    rows = rows_ref[...]
    back = back_ref[...]
    columns = columns_ref[...]
    wide_gate = expand_ref[0]
    wide_up = expand_ref[1]
    down = down_ref[...]
    gate = contract(rows, wide_gate, 1, 0)
    upward = contract(rows, wide_up, 1, 0)
    sigmoid = jax.nn.sigmoid(gate)
    active = gate * sigmoid
    hidden = (active * upward).astype(low)
    grad_hidden = contract(back, down, 1, 1)
    grad_up = (grad_hidden * active).astype(low)
    grad_gate = (grad_hidden * upward * sigmoid * (1.0 + gate * (1.0 - sigmoid))).astype(low)
    fed = contract(hidden, down, 1, 0)
    normed = contract(grad_gate, wide_gate, 1, 1) + contract(grad_up, wide_up, 1, 1)
    down_grad_ref[...] = contract(hidden.T, back, 1, 0).astype(low)
    expand_grad_ref[0] = contract(columns, grad_gate, 1, 0).astype(low)
    expand_grad_ref[1] = contract(columns, grad_up, 1, 0).astype(low)

    @pl.when(h == 0)
    def _():
        fed_sum[...] = fed
        normed_sum[...] = normed

    @pl.when(h == 1)
    def _():
        fed_all = fed_sum[...] + fed
        normed_all = normed_sum[...] + normed
        fed_ref[...] = fed_all[:local]
        fed_other_ref[...] = fed_all[local:].astype(low)
        normed_ref[...] = normed_all[:local]
        normed_other_ref[...] = normed_all[local:].astype(low)


def feed(rows, back, expand, down):
    local, width = rows[0].shape
    _, _, step = expand.shape
    held = pl.BlockSpec((local, width), lambda h: (0, 0))
    pair = pl.BlockSpec((2, width, step), lambda h: (h, 0, 0))
    tall = pl.BlockSpec((step, width), lambda h: (h, 0))
    own = jax.ShapeDtypeStruct((local, width), jnp.float32)
    other = jax.ShapeDtypeStruct((local, width), low)
    return pl.pallas_call(
        feed_kernel,
        grid=(2,),
        out_shape=(
            own,
            other,
            own,
            other,
            jax.ShapeDtypeStruct(down.shape, low),
            jax.ShapeDtypeStruct(expand.shape, low),
        ),
        in_specs=[held] * 4 + [pair, tall],
        out_specs=(held,) * 4 + (tall, pair),
        scratch_shapes=[
            pltpu.VMEM((2 * local, width), low),
            pltpu.VMEM((2 * local, width), low),
            pltpu.VMEM((width, 2 * local), low),
            pltpu.VMEM((2 * local, width), jnp.float32),
            pltpu.VMEM((2 * local, width), jnp.float32),
        ],
        compiler_params=pltpu.CompilerParams(vmem_limit_bytes=56 * 1024 * 1024),
        cost_estimate=pl.CostEstimate(flops=FEED_FLOPS, bytes_accessed=1000, transcendentals=0),
        name="feed",
    )(*rows, *back, expand, down)


def stack_tall(down, kept, came):
    groups, window, width = kept.shape
    proj = (kept.astype(jnp.float32) + came.astype(jnp.float32)).astype(low)
    parts = [down.reshape(groups, 4, -1, width), proj.reshape(groups, 4, window // 4, width)]
    tall = jnp.concatenate([jnp.transpose(part, (1, 0, 2, 3)) for part in parts], axis=2)
    return tall.reshape(4, groups * TALL, width)


def adam_step(master, first, second, grad, rate, decay):
    new_first = beta_first * first + (1.0 - beta_first) * grad
    new_second = beta_second * second + (1.0 - beta_second) * grad * grad
    fix_one = 1.0 - beta_first**STEP
    fix_two = 1.0 - beta_second**STEP
    update = new_first / fix_one / (jnp.sqrt(new_second / fix_two) + adam_eps) + decay * master
    return (master - rate * update, new_first, new_second)


def adam_kernel(assemble, rate, core_ref, mine, theirs, master, first, second, *outs):
    core = core_ref[0]
    one = jnp.where(core == 0, mine[...], theirs[...]).astype(jnp.float32)
    two = jnp.where(core == 0, theirs[...], mine[...]).astype(jnp.float32)
    grad = assemble(one, two)
    new = adam_step(master[...], first[...], second[...], grad, rate, 0.1)
    for out, value in zip(outs, new):
        out[...] = value


def adam(assemble, rate, core, mine, theirs, state, grid, grad_spec, state_spec, name):
    return pl.pallas_call(
        functools.partial(adam_kernel, assemble, rate),
        grid=grid,
        out_shape=(jax.ShapeDtypeStruct(state[0].shape, jnp.float32),) * 3,
        in_specs=[pl.BlockSpec(memory_space=pltpu.SMEM)] + [grad_spec] * 2 + [state_spec] * 3,
        out_specs=(state_spec,) * 3,
        compiler_params=pltpu.CompilerParams(vmem_limit_bytes=32 * 1024 * 1024),
        cost_estimate=pl.CostEstimate(
            flops=1000, bytes_accessed=24 * state[0].size, transcendentals=0
        ),
        name=name,
    )(core.reshape(1), mine, theirs, *state)


def back_rotated(block, cosine, sine):
    first = block[: HEAD_DIM // 2]
    second = block[HEAD_DIM // 2 :]
    return [first * cosine + second * sine, second * cosine - first * sine]


def early_kernel(
    core_ref, dq_ref, cosine_ref, sine_ref, normed_ref, mixed_ref, kept_ref, sent_ref
):
    cosine = cosine_ref[...]
    sine = sine_ref[...]
    first_core = core_ref[0] == 0
    parts = []
    for h in range(HEADS):
        parts += back_rotated(dq_ref[h * HEAD_DIM : (h + 1) * HEAD_DIM], cosine, sine)
    mixed = jnp.concatenate(parts, axis=0)
    mixed_ref[...] = mixed.astype(low)
    weight_halves(first_core, mixed, normed_ref[...].T, None, kept_ref, sent_ref)


def weight_halves(first_core, mixed, columns, gains, kept_ref, sent_ref):
    half = mixed.shape[0] // 2
    blank = jnp.zeros((kept_ref.shape[2] - half, mixed.shape[1]), jnp.float32)
    one = mixed[:half]
    two = mixed[half:]
    near = jnp.concatenate([jnp.where(first_core, one, two), blank], axis=0).T.astype(low)
    away = jnp.concatenate([jnp.where(first_core, two, one), blank], axis=0).T.astype(low)
    groups, rows, lanes = kept_ref.shape
    shard = columns.shape[0] // groups
    for ref, side in ((kept_ref, near), (sent_ref, away)):
        product = contract(columns, side, 1, 0)
        for j in range(groups):
            span = slice(j * shard, (j + 1) * shard)
            tail = jnp.zeros((rows - shard, lanes), jnp.float32)
            if gains is not None:
                tail = jnp.concatenate(
                    [gain[:, span] for gain in gains]
                    + [jnp.zeros((rows - shard - len(gains), shard), jnp.float32)],
                    axis=0,
                )
                tail = jnp.concatenate(
                    [tail, jnp.zeros((rows - shard, lanes - shard), jnp.float32)], axis=1
                )
            ref[j] = jnp.concatenate([product[span], tail], axis=0).astype(low)


def late_kernel(
    core_ref,
    terms_ref,
    mixed_ref,
    cosine_ref,
    sine_ref,
    normed_ref,
    mine_ref,
    theirs_ref,
    rows_ref,
    grad_ref,
    gain_ref,
    gain_grad_ref,
    out_ref,
    kept_ref,
    sent_ref,
):
    cosine = cosine_ref[...]
    sine = sine_ref[...]
    first_core = core_ref[0] == 0
    local = mixed_ref.shape[1]
    parts = []
    values = []
    for g in range(KV_HEADS):
        block = terms_ref[0, g].astype(jnp.float32)
        for j in range(1, terms_ref.shape[0]):
            block = block + terms_ref[j, g].astype(jnp.float32)
        block = block.T
        parts += back_rotated(block[:HEAD_DIM], cosine, sine)
        values.append(block[HEAD_DIM:])
    pair = jnp.concatenate(parts + values, axis=0)
    mixed = jnp.concatenate([mixed_ref[...].astype(jnp.float32), pair], axis=0)
    blank = jnp.zeros((PADDED - QKVW // 2, local), jnp.float32)
    one = mixed[: QKVW // 2]
    two = mixed[QKVW // 2 :]
    near = jnp.concatenate([jnp.where(first_core, one, two), blank], axis=0).T.astype(low)
    away = jnp.concatenate([jnp.where(first_core, two, one), blank], axis=0).T.astype(low)
    grad_normed = contract(near, mine_ref[:, :PADDED], 1, 1) + contract(
        away, theirs_ref[:, :PADDED], 1, 1
    )
    rows = rows_ref[...].astype(jnp.float32).T
    inverse = rms_scale(rows)
    scaled = grad_normed * gain_ref[0:1]
    inner = jnp.mean(scaled * rows, axis=-1, keepdims=True)
    back = inverse * (scaled - rows * inverse * inverse * inner)
    out_ref[...] = (grad_ref[...] + back).T.astype(low)
    gain_one = jnp.sum(grad_normed * rows * inverse, axis=0, keepdims=True)
    gains = (gain_one, gain_grad_ref[...])
    weight_halves(first_core, pair, normed_ref[...].T, gains, kept_ref, sent_ref)


def padded_rows(block, rows):
    return jnp.concatenate(
        [block, jnp.zeros((rows - block.shape[0], block.shape[1]), jnp.float32)], axis=0
    )


def pack_early_kernel(kept_ref, came_ref, expand_ref, out_ref):
    for j in range(out_ref.shape[0]):
        summed = kept_ref[j].astype(jnp.float32) + came_ref[j].astype(jnp.float32)
        expand = padded_rows(expand_ref[j].astype(jnp.float32), summed.shape[0])
        out_ref[j] = jnp.concatenate([summed, expand], axis=1).astype(low)


def pack_late_kernel(kept_ref, came_ref, tall_ref, out_ref):
    for j in range(out_ref.shape[0]):
        summed = kept_ref[j].astype(jnp.float32) + came_ref[j].astype(jnp.float32)
        tall = tall_ref[j].astype(jnp.float32)
        rows = summed.shape[0] // 2
        side = jnp.concatenate(
            [tall[:, 512:], jnp.zeros((tall.shape[0], 1024 - tall.shape[1]), jnp.float32)], axis=1
        )
        tall = jnp.concatenate([padded_rows(tall[:, :512], rows), padded_rows(side, rows)], axis=0)
        out_ref[j] = jnp.concatenate([summed, tall], axis=1).astype(low)


def sum_kernel(early_ref, late_ref, out_ref):
    sums = []
    for ref in (early_ref, late_ref):
        block = ref[0].astype(jnp.float32)
        for j in range(1, ref.shape[0]):
            block = block + ref[j].astype(jnp.float32)
        sums.append(block.astype(low))
    block = jnp.concatenate(sums, axis=1)
    for j in range(out_ref.shape[0]):
        out_ref[j] = block


def finish_kernel(all_ref, wide_ref, rest_ref):
    count = all_ref.shape[0]
    early = slice(0, 512)
    late = slice(512 + FF // 4, 512 + FF // 4 + 384)
    expand = slice(512, 512 + FF // 4)
    tall = slice(512 + FF // 4 + 384, 1024 + FF // 4 + 384)
    sums = []
    for span in (early, late):
        block = all_ref[0, :, span].astype(jnp.float32)
        for j in range(1, count):
            block = block + all_ref[j, :, span].astype(jnp.float32)
        sums.append(block.astype(low))
    wide_ref[...] = jnp.concatenate(sums, axis=1)
    for q in range(count // 2):
        parts = []
        for span in (expand, tall):
            pair = all_ref[q, :, span].astype(jnp.float32)
            pair = pair + all_ref[q + count // 2, :, span].astype(jnp.float32)
            parts.append(pair.astype(low))
        rest_ref[q] = jnp.concatenate(parts, axis=1)


def tall_part(rest, q):
    half = rest.shape[1] // 2
    left = rest[q, :TALL, FF // 4 :]
    right = rest[q, half : half + TALL, FF // 4 : FF // 4 + D - 512]
    return jnp.concatenate([left, right], axis=1)


def weave(one, two):
    step = FF // 16
    parts = []
    for k in range(4):
        span = slice(k * step, (k + 1) * step)
        parts += [one[0, : D // 8, span], two[0, : D // 8, span]]
    return jnp.concatenate(parts, axis=1)


def on_device(
    inputs,
    cotangent,
    span_order,
    w_qkv,
    qkv_first,
    qkv_second,
    w_proj,
    proj_first,
    proj_second,
    w_expand,
    expand_first,
    expand_second,
    w_down,
    down_first,
    down_second,
    gains,
    gains_first,
    gains_second,
):
    core = lax.axis_index("core")
    rank = lax.axis_index(CTX)
    groups = 8
    batch, local, width = inputs.shape
    shard = w_qkv.shape[0]
    hidden_shard = w_down.shape[0] // 2

    y = lax.axis_index("y")
    place = jnp.stack([core, y % 2 * 2 + y // 2]).astype(jnp.int32)
    core_at = place[:1]
    near, expand_low, down_low = stage(place, w_qkv, w_proj, w_expand, w_down, gains, groups)
    mine = exchange(near, CTX).reshape(width, NEAR)
    order_own = lax.dynamic_slice_in_dim(span_order, 2 * rank, 2)
    own_pos = (
        order_own[:, None] * (local // 2) + jnp.arange(local // 2, dtype=jnp.int32)
    ).reshape(local)
    cosine, sine = rope_tables(own_pos)
    mine, cosine, sine, expand_low = lax.optimization_barrier((mine, cosine, sine, expand_low))
    theirs = swap_cores(mine)
    expand_low = exchange(expand_low, CTX).reshape(width, FF // 4)

    tokens = inputs.reshape(local, width).T
    square = (local, width)
    normed_one, query, all_keys, full_gains = whole_call(
        project_kernel,
        "project",
        1000,
        (
            jax.ShapeDtypeStruct(square, low),
            jax.ShapeDtypeStruct((width, local), low),
            jax.ShapeDtypeStruct((groups, KV_HEADS, 2 * HEAD_DIM, local), low),
            jax.ShapeDtypeStruct((2, width), jnp.float32),
        ),
        core_at,
        tokens,
        mine,
        theirs,
        cosine,
        sine,
    )
    all_keys, expand_low = lax.optimization_barrier((all_keys, expand_low))
    expand_low = lax.all_gather(expand_low, "y", axis=0, tiled=False)
    all_keys = exchange(all_keys, CTX)
    all_keys, down_low = lax.optimization_barrier((all_keys, down_low))
    half_down = exchange(down_low, CTX).reshape(HALF, width)
    attended, lse = attend(span_order, order_own, query, all_keys)
    middle, normed_two = whole_call(
        middle_kernel,
        "middle",
        2 * 10**9,
        (jax.ShapeDtypeStruct(square, jnp.float32), jax.ShapeDtypeStruct(square, low)),
        core_at,
        attended,
        mine,
        theirs,
        tokens,
        full_gains,
    )
    normed_two, half_down = lax.optimization_barrier((normed_two, half_down))

    back_rows = cotangent.reshape(local, width)
    fed, fed_other, grad_normed, grad_other, grad_down, grad_expand = feed(
        (normed_two, swap_cores(normed_two)),
        (back_rows, swap_cores(back_rows)),
        expand_low,
        half_down,
    )
    grad_middle, grad_att, proj_kept, proj_sent, gain_grad_two = whole_call(
        turn_kernel,
        "turn",
        3 * 10**9,
        (
            jax.ShapeDtypeStruct(square, jnp.float32),
            jax.ShapeDtypeStruct((width, local), low),
            jax.ShapeDtypeStruct((groups, 64, width), low),
            jax.ShapeDtypeStruct((groups, 64, width), low),
            jax.ShapeDtypeStruct((1, width), jnp.float32),
        ),
        core_at,
        grad_normed,
        swap_cores(grad_other),
        middle,
        back_rows,
        full_gains,
        mine,
        theirs,
        attended,
    )
    output = whole_call(
        emit_kernel,
        "emit",
        1000,
        jax.ShapeDtypeStruct((width, local), low),
        middle,
        fed,
        swap_cores(fed_other),
    )

    expand_sum = lax.psum_scatter(grad_expand, "y", scatter_dimension=0, tiled=False)
    grad_query, key_terms = attend_back(
        span_order, order_own, query, all_keys, grad_att, attended, lse
    )
    key_terms, proj_sent = lax.optimization_barrier((key_terms, proj_sent))
    tall = lax.psum_scatter(
        stack_tall(grad_down, proj_kept, swap_cores(proj_sent)),
        "y",
        scatter_dimension=0,
        tiled=False,
    )
    key_terms = exchange(key_terms, CTX)
    key_terms, output, expand_sum = lax.optimization_barrier((key_terms, output, expand_sum))
    early_half = jax.ShapeDtypeStruct((groups, 128, 512), low)
    query_mixed, kept, sent = whole_call(
        early_kernel,
        "early",
        6 * 10**9,
        (jax.ShapeDtypeStruct((width, local), low), early_half, early_half),
        core_at,
        grad_query,
        cosine,
        sine,
        normed_one,
    )
    early = whole_call(
        pack_early_kernel,
        "pack_early",
        1000,
        jax.ShapeDtypeStruct((groups, 128, 512 + FF // 4), low),
        kept,
        swap_cores(sent),
        expand_sum.reshape(groups, shard, FF // 4),
    )
    early, key_terms = lax.optimization_barrier((early, key_terms))
    early = exchange(early, CTX)
    late_half = jax.ShapeDtypeStruct((groups, 128, 384), low)
    input_grad, kept, sent = whole_call(
        late_kernel,
        "late",
        8 * 10**9,
        (jax.ShapeDtypeStruct((width, local), low), late_half, late_half),
        core_at,
        key_terms,
        query_mixed,
        cosine,
        sine,
        normed_one,
        mine,
        theirs,
        tokens,
        grad_middle,
        full_gains,
        gain_grad_two,
    )
    sent, early = lax.optimization_barrier((sent, early))
    late = whole_call(
        pack_late_kernel,
        "pack_late",
        1000,
        jax.ShapeDtypeStruct((groups, 128, 384 + 512), low),
        kept,
        swap_cores(sent),
        tall.reshape(groups, TALL, width),
    )
    late = exchange(late, CTX)
    parts = whole_call(
        sum_kernel,
        "sum_parts",
        1000,
        jax.ShapeDtypeStruct((8, 128, 512 + FF // 4 + 384 + 512), low),
        early,
        late,
    )
    wide, rest = whole_call(
        finish_kernel,
        "finish",
        1000,
        (
            jax.ShapeDtypeStruct((128, 512 + 384), low),
            jax.ShapeDtypeStruct((4, 128, FF // 4 + 512), low),
        ),
        exchange(parts, CHIPS),
    )
    wide_other = swap_cores(wide)
    rest_other = swap_cores(rest)
    quarter = hidden_shard // 4
    new_expand, expand_mean, expand_square = adam(
        weave,
        2.0 * D ** (-0.5),
        core,
        rest,
        rest_other,
        (w_expand, expand_first, expand_second),
        (4,),
        pl.BlockSpec((1,) + rest.shape[1:], lambda i: (i % 2 * 2 + i // 2, 0, 0)),
        pl.BlockSpec((shard, HALF), lambda i: (0, i)),
        "adam_expand",
    )
    all_rest = pl.BlockSpec(rest.shape, lambda i: (0, 0, 0))
    new_down, down_mean, down_square = adam(
        lambda one, two: jnp.concatenate(
            [tall_part(part, q)[:quarter] for part in (one, two) for q in range(4)], axis=0
        ),
        2.0 * FF ** (-0.5),
        core,
        rest,
        rest_other,
        (w_down, down_first, down_second),
        (1,),
        all_rest,
        pl.BlockSpec((2 * hidden_shard, width), lambda i: (0, 0)),
        "adam_down",
    )
    new_proj, proj_mean, proj_square = adam(
        lambda one, two: jnp.concatenate(
            [tall_part(one, q)[quarter:] for q in range(4)]
            + [tall_part(two, 0)[quarter + 8 :]]
            + [tall_part(two, q)[quarter:] for q in range(1, 4)],
            axis=0,
        ),
        2.0 * (D // 8) ** (-0.5),
        core,
        rest,
        rest_other,
        (w_proj, proj_first, proj_second),
        (1,),
        all_rest,
        pl.BlockSpec((shard, width), lambda i: (0, 0)),
        "adam_proj",
    )
    wide_one, _ = ordered(core, wide, wide_other)
    whole_gains = wide_one[shard : shard + 2, 512 : 512 + shard].astype(jnp.float32)
    new_qkv, qkv_mean, qkv_square = adam(
        lambda one, two: jnp.concatenate(
            [one[:shard, : D // 2], two[:shard, : D // 2]]
            + [part[:shard, 512 : 512 + KV_HEADS * HEAD_DIM] for part in (one, two)],
            axis=1,
        ),
        2.0 * D ** (-0.5),
        core,
        wide,
        wide_other,
        (w_qkv, qkv_first, qkv_second),
        (1,),
        pl.BlockSpec(wide.shape, lambda i: (0, 0)),
        pl.BlockSpec((shard, QKVW), lambda i: (0, 0)),
        "adam_qkv",
    )
    new_gains, gains_mean, gains_square = adam_step(
        gains, gains_first, gains_second, whole_gains, 1.0, 0.0
    )
    return (
        output.T.reshape(batch, local, width),
        input_grad.T.reshape(batch, local, width),
        new_qkv,
        qkv_mean,
        qkv_square,
        new_proj,
        proj_mean,
        proj_square,
        new_expand,
        expand_mean,
        expand_square,
        new_down,
        down_mean,
        down_square,
        new_gains,
        gains_mean,
        gains_square,
    )


def solution(mesh):
    parts = jax.sharding.Mesh(mesh.devices.reshape(2, 4, 2, 2, 4), AXES)
    dp, ctx = ("zh", "y", "core"), CTX
    rows = P(dp, ctx, None)
    owned = P(ctx, None)
    split = P(None, ctx)
    return jax.shard_map(
        on_device,
        mesh=parts,
        in_specs=(rows, rows, P()) + (owned,) * 12 + (split,) * 3,
        out_specs=(rows, rows) + (owned,) * 12 + (split,) * 3,
        check_vma=False,
    )
```

time: 500 us -> 431 us (0.86)
  waiting for transfers between devices: 171 us -> 105 us
  blocking collectives: 55.3 us -> 119 us
  Pallas kernels: 45.4 us -> 108 us
  matrix products: 48.5 us -> 0 us
  other arithmetic: 47.8 us -> 2.8 us
  starting transfers between devices: 71.7 us -> 43.8 us
    all_to_all x10 -> x5, waiting for transfers between devices: 164 us -> 91.3 us  [exchange(): return lax.all_to_all(stack, axes, 0, 0, tiled=True)]
    all_to_all x1 -> x3, blocking collectives: 55.3 us -> 119 us  [exchange(): return lax.all_to_all(stack, axes, 0, 0, tiled=True)]
    pallas_call x0 -> x16, Pallas kernels: none -> 61.1 us  [the longest x10 25.6 us: whole_call(): pl.pallas_call(kernel, out_shape=out_shape, in_specs=[scalars() if value....]
    dot_general x17 -> x0, matrix products: 48.5 us -> none  [contract(): lax.dot_general(left, right, (((left_axis,), (right_axis,)), ((), ())), p...]
    unnamed x74 -> x117, local copies, waits for them, and re-layouts: 6.54 us -> 34.8 us
    all_to_all x10 -> x5, starting transfers between devices: 58 us -> 35.3 us  [exchange(): return lax.all_to_all(stack, axes, 0, 0, tiled=True)]
    sub x5 -> x1, other arithmetic: 18.4 us -> 1.27 us  [adam_step(): return (master - rate * update, new_first, new_second)]
    slice x16 -> x0, local copies, waits for them, and re-layouts: 11.4 us -> none  [the longest x2 2.68 us: on_device(): grad_keys[:, HEAD_DIM:].reshape(kv_width, local)]
  transfers between devices with their start and end apart: 24 -> 18, of which waited for: 13 -> 11; matrix products, arithmetic and copies ran while one was open for 20% -> 1% of each run, Pallas kernels for 9% -> 16%
where the time goes in v3:
time: 431 us; the launch traced here: 429 us
  blocking collectives  119 us (28%)
  Pallas kernels  108 us (25%)
  waiting for transfers between devices  105 us (24%)
  starting transfers between devices  43.8 us (10%)
  local copies, waits for them, and re-layouts  37.1 us (9%)
  between operations  14.2 us (3%)
    all_to_all x3, blocking collectives, exchange(): return lax.all_to_all(stack, axes, 0, 0, tiled=True)  119 us
    all_to_all x5, waiting for transfers between devices, exchange(): return lax.all_to_all(stack, axes, 0, 0, tiled=True)  91.3 us
    all_to_all x5, starting transfers between devices, exchange(): return lax.all_to_all(stack, axes, 0, 0, tiled=True)  35.3 us
    unnamed x117, local copies, waits for them, and re-layouts  34.8 us
    pallas_call x1, Pallas kernels, attend_back(): pl.pallas_call(attend_back_kernel, grid=(KV_HEADS,), out_shape=(jax.Shape...  27 us
    pallas_call x10, Pallas kernels, whole_call(): pl.pallas_call(kernel, out_shape=out_shape, in_specs=[scalars() if value....  25.6 us
    pallas_call x1, Pallas kernels, feed(): pl.pallas_call(feed_kernel, grid=(2,), out_shape=(own, other, own, other,...  21.3 us
    pallas_call x1, Pallas kernels, attend(): pl.pallas_call(attend_kernel, grid=(KV_HEADS,), out_shape=(jax.ShapeDtype...  19.4 us
  transfers between devices with their start and end apart: 18, of which 11 were waited for; matrix products, arithmetic and copies ran while one was open for 1% of the time, Pallas kernels for 16%

profile of v3, /device:TPU:1, one launch (start us, length us, event | category | flops | bytes accessed | tf_op | source)
XLA Modules:
  0.0 429.1 jit_solution(15475787090323241625)
XLA Ops:
  13.1 2.6 stage.1
  18.3 6.3 %all-to-all-start = ((bf16[8,120,1408]{2,1,0:T(8,128)(2,1)}), bf16[8,120,1408]{2,1,0:T(8,128)(2,1)S(1)}, u32[]{:S(2)}, u32[]{:S(2)}) async-start(bf16[8,120,1408]{2,1,0:T(8,128)(2,1)} %copy-done.9), calls=%async_computation | async-start | bytes 5406720 | tf_op jit(solution)/shard_map/all_to_all | solution.py:63
  25.0 33.1 %all-to-all-done = bf16[8,120,1408]{2,1,0:T(8,128)(2,1)S(1)} async-done(((bf16[8,120,1408]{2,1,0:T(8,128)(2,1)}), bf16[8,120,1408]{2,1,0:T(8,128)(2,1)S(1)}, u32[]{:S(2)}, u32[]{:S(2)}) %all-to-all-start) | async-done | bytes 2703392 | tf_op jit(solution)/shard_map/all_to_all | solution.py:63
  59.0 9.2 %all-to-all-start.1 = ((bf16[8,120,640]{2,1,0:T(8,128)(2,1)}), bf16[8,120,640]{2,1,0:T(8,128)(2,1)}, u32[]{:S(2)}, u32[]{:S(2)}) async-start(bf16[8,120,640]{2,1,0:T(8,128)(2,1)} %copy-done.19), calls=%async_computation.1 | async-start | bytes 2457600 | tf_op jit(solution)/shard_map/all_to_all | solution.py:63
  68.3 4.5 %project.1 = (bf16[256,960]{1,0:T(8,128)(2,1)S(1)}, bf16[960,256]{1,0:T(8,128)(2,1)S(1)}, bf16[8,5,128,256]{3,2,1,0:T(8,128)(2,1)S(1)}, f32[2,960]{1,0:T(2,128)S(1)}) custom-call(s32[1]{0:T(128)} %bitcast.core_ref, bf16[960,256]{1,0:T(8,128)(2,1)S(1)} %bitcast.38, bf16[960,1408]{1,0:T(8,128)(2,1)} %bitcast.29, ...), custom_call_target="tpu_custom_call" | custom-call | flops 1000 | bytes 1000 | tf_op jit(solution)/shard_map/project/pallas_call | solution.py:226
  75.8 10.3 %all-to-all-done.1 = bf16[8,120,640]{2,1,0:T(8,128)(2,1)} async-done(((bf16[8,120,640]{2,1,0:T(8,128)(2,1)}), bf16[8,120,640]{2,1,0:T(8,128)(2,1)}, u32[]{:S(2)}, u32[]{:S(2)}) %all-to-all-start.1) | async-done | bytes 1228832 | tf_op jit(solution)/shard_map/all_to_all | solution.py:63
  86.2 35.3 %all_to_all.40.kv_ref = bf16[8,5,128,256]{3,2,1,0:T(8,128)(2,1)S(1)} all-to-all(bf16[8,5,128,256]{3,2,1,0:T(8,128)(2,1)} %copy-done.11), channel_id=1, replica_groups=mesh['zh'=2,'y'=4,'core'=2,'zl'=2,'x'=4] {'zl','x'}, dimensions={0} | all-to-all | bytes 5242880 | tf_op jit(solution)/shard_map/all_to_all | solution.py:63
  121.5 4.4 %all-to-all-start.3 = ((bf16[8,160,960]{2,1,0:T(8,128)(2,1)}), bf16[8,160,960]{2,1,0:T(8,128)(2,1)}, u32[]{:S(2)}, u32[]{:S(2)}) async-start(bf16[8,160,960]{2,1,0:T(8,128)(2,1)} %get-tuple-element.94), calls=%async_computation.3 | async-start | bytes 5242880 | tf_op jit(solution)/shard_map/all_to_all | solution.py:63
  127.2 1.8 collective-permute-start.2
  130.1 19.4 %attend.1 = (bf16[960,256]{1,0:T(8,128)(2,1)S(1)}, f32[15,1,256]{2,1,0:T(1,128)S(1)}) custom-call(s32[16]{0:T(128)S(1)} %copy-done.35, s32[2]{0:T(128)S(1)} %get-tuple-element.147.own_ref, bf16[960,256]{1,0:T(8,128)(2,1)S(1)} %copy-done.42, bf16[8,5,128,256]{3,2,1,0:T(8,128)(2,1)S(1)} %all_to_all.40.kv_ref), custom_call_target="tpu_custom_call" | custom-call | flops 20000000000 | bytes 1000 | tf_op jit(solution)/shard_map/attend/pallas_call | solution.py:184
  149.5 2.8 middle.1
  154.1 4.5 %all-to-all-done.3 = bf16[8,160,960]{2,1,0:T(8,128)(2,1)} async-done(((bf16[8,160,960]{2,1,0:T(8,128)(2,1)}), bf16[8,160,960]{2,1,0:T(8,128)(2,1)}, u32[]{:S(2)}, u32[]{:S(2)}) %all-to-all-start.3) | async-done | bytes 2457632 | tf_op jit(solution)/shard_map/all_to_all | solution.py:63
  161.8 21.3 %feed.1 = (f32[256,960]{1,0:T(8,128)}, bf16[256,960]{1,0:T(8,128)(2,1)}, f32[256,960]{1,0:T(8,128)}, bf16[256,960]{1,0:T(8,128)(2,1)}, bf16[1280,960]{1,0:T(8,128)(2,1)}, /*index=5*/bf16[4,960,640]{2,1,0:T(8,128)(2,1)}) custom-call(bf16[256,960]{1,0:T(8,128)(2,1)} %copy-done.40, bf16[256,960]{1,0:T(8,128)(2,1)} %copy-done.57, bf16[256,960]{1,0:T(8,128)(2,1)} %bitcast.36, ...), custom_call_target="tpu_custom_call" | custom-call | flops 20000000000 | bytes 1000 | tf_op jit(solution)/shard_map/feed/pallas_call | solution.py:480
  186.1 5.2 %turn.1 = (f32[256,960]{1,0:T(8,128)S(1)}, bf16[960,256]{1,0:T(8,128)(2,1)S(1)}, bf16[8,64,960]{2,1,0:T(8,128)(2,1)S(1)}, bf16[8,64,960]{2,1,0:T(8,128)(2,1)S(1)}, f32[1,960]{1,0:T(1,128)S(1)}) custom-call(s32[1]{0:T(128)} %bitcast.core_ref, f32[256,960]{1,0:T(8,128)} %get-tuple-element.98.own_ref, bf16[256,960]{1,0:T(8,128)(2,1)S(1)} %collective-permute-done.3.came_ref, ...), custom_call_target="tpu_custom_call" | custom-call | flops 3000000000 | bytes 1000 | tf_op jit(solution)/shard_map/turn/pallas_call | solution.py:226
  192.3 27.0 %attend_back.1 = (f32[960,256]{1,0:T(8,128)S(1)}, bf16[8,5,256,128]{3,2,1,0:T(8,128)(2,1)}) custom-call(s32[16]{0:T(128)S(1)} %copy-done.35, s32[2]{0:T(128)S(1)} %get-tuple-element.147.own_ref, bf16[960,256]{1,0:T(8,128)(2,1)S(1)} %copy-done.43, bf16[8,5,128,256]{3,2,1,0:T(8,128)(2,1)} %copy-done.10, bf16[960,256]{1,0:T(8,128)(2,1)S(1)} %get-tuple-element.101.do_ref, ...), custom_call_target="tpu_custom_call" | custom-call | flops 24999999488 | bytes 1000 | tf_op jit(solution)/shard_map/attend_back/pallas_call | solution.py:206
  219.7 2.3 collective-permute-done.7
  223.1 2.4 copy.36
  225.5 6.0 %all-to-all-start.4 = ((bf16[8,5,256,128]{3,2,1,0:T(8,128)(2,1)}), bf16[8,5,256,128]{3,2,1,0:T(8,128)(2,1)}, u32[]{:S(2)}, u32[]{:S(2)}) async-start(bf16[8,5,256,128]{3,2,1,0:T(8,128)(2,1)} %get-tuple-element.105), calls=%async_computation.4 | async-start | bytes 5242880 | tf_op jit(solution)/shard_map/all_to_all | solution.py:63
  235.1 3.0 collective-permute-done.4.came_ref
  239.1 25.2 %all-to-all-done.4.terms_ref = bf16[8,5,256,128]{3,2,1,0:T(8,128)(2,1)} async-done(((bf16[8,5,256,128]{3,2,1,0:T(8,128)(2,1)}), bf16[8,5,256,128]{3,2,1,0:T(8,128)(2,1)}, u32[]{:S(2)}, u32[]{:S(2)}) %all-to-all-start.4) | async-done | bytes 2621472 | tf_op jit(solution)/shard_map/all_to_all | solution.py:63
  267.3 9.3 %all-to-all-start.5 = ((bf16[8,128,1152]{2,1,0:T(8,128)(2,1)}), bf16[8,128,1152]{2,1,0:T(8,128)(2,1)S(1)}, u32[]{:S(2)}, u32[]{:S(2)}) async-start(bf16[8,128,1152]{2,1,0:T(8,128)(2,1)} %copy-done.4), calls=%async_computation.6 | async-start | bytes 4718592 | tf_op jit(solution)/shard_map/all_to_all | solution.py:63
  280.9 6.5 %late.1 = (bf16[960,256]{1,0:T(8,128)(2,1)}, bf16[8,128,384]{2,1,0:T(8,128)(2,1)S(1)}, bf16[8,128,384]{2,1,0:T(8,128)(2,1)S(1)}) custom-call(s32[1]{0:T(128)} %bitcast.core_ref, bf16[8,5,256,128]{3,2,1,0:T(8,128)(2,1)} %all-to-all-done.4.terms_ref, bf16[960,256]{1,0:T(8,128)(2,1)S(1)} %copy-done.51, f32[32,256]{1,0:T(8,128)S(1)} %get-tuple-element.83.cosine_ref, ...), custom_call_target="tpu_custom_call" | custom-call | flops 8000000000 | bytes 1000 | tf_op jit(solution)/shard_map/late/pallas_call | solution.py:226
  288.3 18.1 %all-to-all-done.5.early_ref = bf16[8,128,1152]{2,1,0:T(8,128)(2,1)S(1)} async-done(((bf16[8,128,1152]{2,1,0:T(8,128)(2,1)}), bf16[8,128,1152]{2,1,0:T(8,128)(2,1)S(1)}, u32[]{:S(2)}, u32[]{:S(2)}) %all-to-all-start.5) | async-done | bytes 2359328 | tf_op jit(solution)/shard_map/all_to_all | solution.py:63
  307.3 2.3 collective-permute-done.6.came_ref
  312.1 26.9 %all_to_all.41.late_ref = bf16[8,128,896]{2,1,0:T(8,128)(2,1)S(1)} all-to-all(bf16[8,128,896]{2,1,0:T(8,128)(2,1)S(1)} %pack_late.1), channel_id=1, replica_groups=mesh['zh'=2,'y'=4,'core'=2,'zl'=2,'x'=4] {'zl','x'}, dimensions={0} | all-to-all | bytes 3670016 | tf_op jit(solution)/shard_map/all_to_all | solution.py:63
  339.0 2.6 sum_parts.1
  341.6 56.7 %all_to_all.42.all_ref = bf16[8,128,2048]{2,1,0:T(8,128)(2,1)S(1)} all-to-all(bf16[8,128,2048]{2,1,0:T(8,128)(2,1)} %sum_parts.1), channel_id=1, replica_groups=mesh['zh'=2,'y'=4,'core'=2,'zl'=2,'x'=4] {'zh','y'}, dimensions={0} | all-to-all | bytes 8388608 | tf_op jit(solution)/shard_map/all_to_all | solution.py:63
  398.8 2.6 collective-permute-start.9
  401.5 2.7 collective-permute-done.8.theirs
  406.5 3.2 adam_qkv.1
  414.1 2.4 adam_down.1
  416.6 4.6 %adam_expand.1 = (f32[120,5120]{1,0:T(8,128)}, f32[120,5120]{1,0:T(8,128)}, f32[120,5120]{1,0:T(8,128)}) custom-call(s32[1]{0:T(128)} %bitcast.core_ref, bf16[4,128,1152]{2,1,0:T(8,128)(2,1)S(1)} %get-tuple-element.133.mine, bf16[4,128,1152]{2,1,0:T(8,128)(2,1)S(1)} %collective-permute-done.9.theirs, f32[120,5120]{1,0:T(8,128)S(1)} %copy-done.3, ...), custom_call_target="tpu_custom_call" | custom-call | flops 1000 | bytes 14745600 | tf_op jit(solution)/shard_map/adam_expand/pallas_call | solution.py:534
  (154 shorter events, 50.2 us)
Async XLA Ops:
  18.3 6.4 %copy-start.35 = (s32[16]{0:T(128)S(1)}, s32[16]{0:T(128)}, u32[]{:S(2)}) copy-start(s32[16]{0:T(128)} %order_ref.3) | copy-start | bytes 196
  18.3 39.9 %all-to-all-start = ((bf16[8,120,1408]{2,1,0:T(8,128)(2,1)}), bf16[8,120,1408]{2,1,0:T(8,128)(2,1)S(1)}, u32[]{:S(2)}, u32[]{:S(2)}) async-start(bf16[8,120,1408]{2,1,0:T(8,128)(2,1)} %copy-done.9), calls=%async_computation | async-start | bytes 5406720 | tf_op jit(solution)/shard_map/all_to_all | solution.py:63
  24.6 43.6 %copy-start.28 = (bf16[1,256,960]{1,2,0:T(8,128)(2,1)S(1)}, bf16[1,256,960]{1,2,0:T(8,128)(2,1)}, u32[]{:S(2)}) copy-start(bf16[1,256,960]{1,2,0:T(8,128)(2,1)} %param.18) | copy-start | bytes 1474564
  58.2 10.1 %copy-start = (bf16[8,120,1408]{2,1,0:T(8,128)(2,1)}, bf16[8,120,1408]{2,1,0:T(8,128)(2,1)S(1)}, u32[]{:S(2)}) copy-start(bf16[8,120,1408]{2,1,0:T(8,128)(2,1)S(1)} %all-to-all-done) | copy-start | bytes 8110084
  58.2 10.1 %collective-permute-start = (bf16[960,1408]{1,0:T(8,128)(2,1)S(1)}, bf16[960,1408]{1,0:T(8,128)(2,1)}, u32[]{:S(2)}, u32[]{:S(2)}) collective-permute-start(bf16[960,1408]{1,0:T(8,128)(2,1)S(1)} %bitcast.28), channel_id=1, source_target_pairs={{0,8},{8,0},{1,9},{9,1},{2,10},{10,2},{3,11},{11,3},{4,12},{12,4},... | collective-permute-start | bytes 8110088 | tf_op jit(solution)/shard_map/ppermute | solution.py:42
  59.0 27.1 %all-to-all-start.1 = ((bf16[8,120,640]{2,1,0:T(8,128)(2,1)}), bf16[8,120,640]{2,1,0:T(8,128)(2,1)}, u32[]{:S(2)}, u32[]{:S(2)}) async-start(bf16[8,120,640]{2,1,0:T(8,128)(2,1)} %copy-done.19), calls=%async_computation.1 | async-start | bytes 2457600 | tf_op jit(solution)/shard_map/all_to_all | solution.py:63
  68.2 92.8 %all-gather.3.cloned.1.call-start = ((), (), s32[]{:S(2)}) async-start(), calls=%async_computation.12 | async-start | bytes 6144000 | tf_op jit(solution)/shard_map/all_gather | solution.py:781
  121.5 7.5 %copy-start.10 = (bf16[8,5,128,256]{3,2,1,0:T(8,128)(2,1)}, bf16[8,5,128,256]{3,2,1,0:T(8,128)(2,1)S(1)}, u32[]{:S(2)}) copy-start(bf16[8,5,128,256]{3,2,1,0:T(8,128)(2,1)S(1)} %all_to_all.40.kv_ref) | copy-start | bytes 7864324
  121.5 37.1 %all-to-all-start.3 = ((bf16[8,160,960]{2,1,0:T(8,128)(2,1)}), bf16[8,160,960]{2,1,0:T(8,128)(2,1)}, u32[]{:S(2)}, u32[]{:S(2)}) async-start(bf16[8,160,960]{2,1,0:T(8,128)(2,1)} %get-tuple-element.94), calls=%async_computation.3 | async-start | bytes 5242880 | tf_op jit(solution)/shard_map/all_to_all | solution.py:63
  125.9 138.4 %reduce-scatter.3.cloned.1.call-start = ((), (), s32[]{:S(2)}) async-start(), calls=%async_computation.10 | async-start | bytes 6144000 | tf_op jit(solution)/shard_map/reduce_scatter | solution.py:838
  127.2 22.3 %copy-start.26 = (bf16[1,256,960]{2,1,0:T(8,128)(2,1)}, bf16[1,256,960]{2,1,0:T(8,128)(2,1)S(1)}, u32[]{:S(2)}) copy-start(bf16[1,256,960]{2,1,0:T(8,128)(2,1)S(1)} %copy.35) | copy-start | bytes 1474564
  127.2 32.2 %collective-permute-start.2 = (bf16[256,960]{1,0:T(8,128)(2,1)S(1)}, bf16[256,960]{1,0:T(8,128)(2,1)}, u32[]{:S(2)}, u32[]{:S(2)}) collective-permute-start(bf16[256,960]{1,0:T(8,128)(2,1)S(1)} %bitcast.35), channel_id=1, source_target_pairs={{0,8},{8,0},{1,9},{9,1},{2,10},{10,2},{3,11},{11,3},{4,12},{12,4},... | collective-permute-start | bytes 1474568 | tf_op jit(solution)/shard_map/ppermute | solution.py:42
  130.1 19.4 %copy-start.1 = (bf16[8,120,1408]{2,1,0:T(8,128)(2,1)S(1)}, bf16[8,120,1408]{2,1,0:T(8,128)(2,1)}, u32[]{:S(2)}) copy-start(bf16[8,120,1408]{2,1,0:T(8,128)(2,1)} %copy-done) | copy-start | bytes 8110084
  130.1 19.4 %copy-start.29 = (bf16[1,256,960]{1,2,0:T(8,128)(2,1)S(1)}, bf16[1,256,960]{1,2,0:T(8,128)(2,1)}, u32[]{:S(2)}) copy-start(bf16[1,256,960]{1,2,0:T(8,128)(2,1)} %param.18) | copy-start | bytes 1474564
  154.1 6.9 %copy-start.40 = (bf16[256,960]{1,0:T(8,128)(2,1)}, bf16[256,960]{1,0:T(8,128)(2,1)S(1)}, u32[]{:S(2)}) copy-start(bf16[256,960]{1,0:T(8,128)(2,1)S(1)} %get-tuple-element.95.rows_one) | copy-start | bytes 1474564
  158.6 2.4 collective-permute-start.1
  183.2 124.1 %reduce-scatter.5.cloned.1.call-start = ((), (), s32[]{:S(2)}) async-start(), calls=%async_computation.11 | async-start | bytes 4587520 | tf_op jit(solution)/shard_map/reduce_scatter | solution.py:843
  184.2 1.9 collective-permute-start.3
  186.1 6.2 %copy-start.43 = (bf16[960,256]{1,0:T(8,128)(2,1)S(1)}, bf16[960,256]{1,0:T(8,128)(2,1)}, u32[]{:S(2)}) copy-start(bf16[960,256]{1,0:T(8,128)(2,1)} %copy-done.41) | copy-start | bytes 1474564
  219.3 2.7 collective-permute-start.7
  225.5 38.8 %all-to-all-start.4 = ((bf16[8,5,256,128]{3,2,1,0:T(8,128)(2,1)}), bf16[8,5,256,128]{3,2,1,0:T(8,128)(2,1)}, u32[]{:S(2)}, u32[]{:S(2)}) async-start(bf16[8,5,256,128]{3,2,1,0:T(8,128)(2,1)} %get-tuple-element.105), calls=%async_computation.4 | async-start | bytes 5242880 | tf_op jit(solution)/shard_map/all_to_all | solution.py:63
  234.4 29.9 %collective-permute-start.5 = (bf16[8,128,512]{2,1,0:T(8,128)(2,1)S(1)}, bf16[8,128,512]{2,1,0:T(8,128)(2,1)S(1)}, u32[]{:S(2)}, u32[]{:S(2)}) collective-permute-start(bf16[8,128,512]{2,1,0:T(8,128)(2,1)S(1)} %get-tuple-element.113), channel_id=1, source_target_pairs={{0,8},{8,0},{1,9},{9,1},{2,10},{10,2},{3,11},{11,3},{4,12},{12,4},... | collective-permute-start | bytes 3145736 | tf_op jit(solution)/shard_map/ppermute | solution.py:42
  235.1 3.0 collective-permute-start.4
  267.3 39.2 %all-to-all-start.5 = ((bf16[8,128,1152]{2,1,0:T(8,128)(2,1)}), bf16[8,128,1152]{2,1,0:T(8,128)(2,1)S(1)}, u32[]{:S(2)}, u32[]{:S(2)}) async-start(bf16[8,128,1152]{2,1,0:T(8,128)(2,1)} %copy-done.4), calls=%async_computation.6 | async-start | bytes 4718592 | tf_op jit(solution)/shard_map/all_to_all | solution.py:63
  306.4 3.1 collective-permute-start.6
  398.8 10.9 %copy-start.34 = (f32[2,120]{1,0:T(2,128)S(1)}, f32[2,120]{1,0:T(2,128)}, u32[]{:S(2)}) copy-start(f32[2,120]{1,0:T(2,128)} %gains_ref.1) | copy-start | bytes 2884
  398.8 10.9 %copy-start.53 = (f32[2,120]{1,0:T(2,128)S(1)}, f32[2,120]{1,0:T(2,128)}, u32[]{:S(2)}) copy-start(f32[2,120]{1,0:T(2,128)} %param.34) | copy-start | bytes 2884
  398.8 10.9 %copy-start.54 = (f32[2,120]{1,0:T(2,128)S(1)}, f32[2,120]{1,0:T(2,128)}, u32[]{:S(2)}) copy-start(f32[2,120]{1,0:T(2,128)} %param.35) | copy-start | bytes 2884
  398.8 12.1 %collective-permute-start.9 = (bf16[4,128,1152]{2,1,0:T(8,128)(2,1)S(1)}, bf16[4,128,1152]{2,1,0:T(8,128)(2,1)S(1)}, u32[]{:S(2)}, u32[]{:S(2)}) collective-permute-start(bf16[4,128,1152]{2,1,0:T(8,128)(2,1)S(1)} %get-tuple-element.133.mine), channel_id=1, source_target_pairs={{0,8},{8,0},{1,9},{9,1},{2,10},{10,2},{3,11},{11,3},{4,12},{12,4},... | collective-permute-start | bytes 3538952 | tf_op jit(solution)/shard_map/ppermute | solution.py:42
  401.4 2.8 collective-permute-start.8
  401.5 9.5 %copy-start.6 = (f32[320,960]{1,0:T(8,128)S(1)}, f32[320,960]{1,0:T(8,128)}, u32[]{:S(2)}) copy-start(f32[320,960]{1,0:T(8,128)} %master.7) | copy-start | bytes 3686404
  406.5 10.1 %copy-start.13 = (f32[120,5120]{1,0:T(8,128)S(1)}, f32[120,5120]{1,0:T(8,128)}, u32[]{:S(2)}) copy-start(f32[120,5120]{1,0:T(8,128)} %second.6) | copy-start | bytes 7372804
  (44 other events, 96.5 us)
Sparse Core Ops, SparseCore 0:
  86.3 54.2 all-gather.2
  183.3 55.3 reduce-scatter.2
  241.2 42.2 reduce-scatter.4
